TPU v7x, 32 devices: a whole 2x2x4 slice. The times are simulated.
32 devices in a mesh: dp: 4 (over z), seq: 8 (over y, x, core).
Axes of the slice: x: 2, y: 2, z: 4, core: 2. Of those that a mesh axis runs over, the one named last changes fastest.
Arguments:
- inputs: float32 [8, 2048, 1536], P('dp', 'seq'), may hold values from -6 to 6
- segments: int32 [8, 2048], P('dp', 'seq'), may hold values from -1 to 7, as said below
- norm1_gain: float32 [1536], replicated, may hold values from 0.25 to 1.75
- norm1_bias: float32 [1536], replicated, may hold values from -3 to 3
- w_query: bfloat16 [1536, 1536], P(('dp', 'seq')), may hold values from -0.15625 to 0.15625
- w_key: bfloat16 [1536, 1536], P(('dp', 'seq')), may hold values from -0.15625 to 0.15625
- w_value: bfloat16 [1536, 1536], P(('dp', 'seq')), may hold values from -0.15625 to 0.15625
- w_out: bfloat16 [1536, 1536], P(('dp', 'seq')), may hold values from -0.625 to 0.625
- norm2_gain: float32 [1536], replicated, may hold values from 0.25 to 1.75
- norm2_bias: float32 [1536], replicated, may hold values from -3 to 3
- w_up: bfloat16 [1536, 6144], P(('dp', 'seq')), may hold values from -0.15625 to 0.15625
- w_down: bfloat16 [6144, 1536], P(('dp', 'seq')), may hold values from -0.078125 to 0.078125
- cotangent: float32 [8, 2048, 1536], P('dp', 'seq'), may hold values from -6 to 6
Outputs:
- output: float32 [8, 2048, 1536], P('dp', 'seq')
- d_inputs: float32 [8, 2048, 1536], P('dp', 'seq')
- d_norm1_gain: float32 [1536], P(('dp', 'seq'))
- d_norm1_bias: float32 [1536], P(('dp', 'seq'))
- d_w_query: float32 [1536, 1536], P(('dp', 'seq'))
- d_w_key: float32 [1536, 1536], P(('dp', 'seq'))
- d_w_value: float32 [1536, 1536], P(('dp', 'seq'))
- d_w_out: float32 [1536, 1536], P(('dp', 'seq'))
- d_norm2_gain: float32 [1536], P(('dp', 'seq'))
- d_norm2_bias: float32 [1536], P(('dp', 'seq'))
- d_w_up: float32 [1536, 6144], P(('dp', 'seq'))
- d_w_down: float32 [6144, 1536], P(('dp', 'seq'))
Inputs may be any that keep to these rules, and one draw needn't show every extreme that they name: `segments`: along each sequence the ids start at 0 and rise by one at the first token of each later document; the last 1 to 128 tokens are padding with id -1.
All inputs are finite; a program needn't handle non-finite values.
Results may differ from a plain program's by a relative error of at most 0.019.
Values may be sent and summed in bfloat16 or wider, within the bound.
A program may use at most 320 MiB of HBM per device.

v0:
```python
import math

import jax
import jax.numpy as jnp
from jax import lax
from jax.sharding import PartitionSpec as P

HEAD_DIM = 128


EPSILON = 1e-05
MASKED = -1e30


def layer_norm(values, gain, offset):
    centre = values - jnp.mean(values, axis=-1, keepdims=True)
    spread = jnp.mean(centre * centre, axis=-1, keepdims=True)
    return centre * lax.rsqrt(spread + EPSILON) * gain + offset


def gelu(values):
    return 0.5 * values * (1.0 + lax.erf(values * (1.0 / math.sqrt(2.0))))


def angles(positions):
    half = HEAD_DIM // 2
    rates = jnp.exp(jnp.arange(half, dtype=jnp.float32) * (-math.log(10000.0) / half))
    turned = positions.astype(jnp.float32)[:, None] * rates[None, :]
    return (jnp.cos(turned)[:, None, :], jnp.sin(turned)[:, None, :])


def rotary(values, cosine, sine):
    half = values.shape[-1] // 2
    first = values[..., :half]
    second = values[..., half:]
    return jnp.concatenate(
        [first * cosine - second * sine, second * cosine + first * sine], axis=-1
    )


def lower(values):
    return values.astype(jnp.bfloat16)


def project(acts, weight):
    return jnp.einsum("gcd,de->gce", acts, weight, preferred_element_type=jnp.float32)


def project_back(grads, weight):
    return jnp.einsum("gce,de->gcd", grads, weight, preferred_element_type=jnp.float32)


def outer_sum(left, right):
    return jnp.einsum("gci,gcj->ij", left, right, preferred_element_type=jnp.float32)


def shards(
    inputs,
    segments,
    norm1_gain,
    norm1_bias,
    w_query,
    w_key,
    w_value,
    w_out,
    norm2_gain,
    norm2_bias,
    w_up,
    w_down,
    cotangent,
):
    groups, columns, width = inputs.shape
    heads_count = width // HEAD_DIM
    scale = 1.0 / math.sqrt(HEAD_DIM)
    full_query, full_key, full_value, full_out, full_up, full_down = (
        lax.all_gather(w_query, ("dp", "seq"), axis=0, tiled=True),
        lax.all_gather(w_key, ("dp", "seq"), axis=0, tiled=True),
        lax.all_gather(w_value, ("dp", "seq"), axis=0, tiled=True),
        lax.all_gather(w_out, ("dp", "seq"), axis=0, tiled=True),
        lax.all_gather(w_up, ("dp", "seq"), axis=0, tiled=True),
        lax.all_gather(w_down, ("dp", "seq"), axis=0, tiled=True),
    )
    key_ids = lax.all_gather(segments, "seq", axis=1, tiled=True)
    length = key_ids.shape[1]
    rank = lax.axis_index("seq")
    places = rank * columns + jnp.arange(columns, dtype=jnp.int32)
    key_places = jnp.arange(length, dtype=jnp.int32)
    cosine, sine = angles(places)

    def turn(values):
        shaped = values.reshape(groups, columns, heads_count, HEAD_DIM)
        return rotary(shaped, cosine, sine).reshape(groups, columns, width)

    def permitted(segment_row, key_row):
        same = segment_row[:, None] == key_row[None, :]
        causal = key_places[None, :] <= places[:, None]
        live = (key_row[None, :] >= 0) | (key_places[None, :] == places[:, None])
        return same & causal & live

    def scores_of(query_row, key_block, segment_row, key_row):
        heads_query = query_row.reshape(columns, heads_count, HEAD_DIM)
        heads_key = key_block.reshape(length, heads_count, HEAD_DIM)
        raw = (
            jnp.einsum("chd,lhd->hcl", heads_query, heads_key, preferred_element_type=jnp.float32)
            * scale
        )
        return jnp.where(permitted(segment_row, key_row)[None], raw, MASKED)

    normed_one = layer_norm(inputs, norm1_gain, norm1_bias)
    act_one = lower(normed_one)
    query_zero = project(act_one, full_query)
    key_zero = project(act_one, full_key)
    value_low = lower(project(act_one, full_value))
    query_low = lower(turn(query_zero))
    key_low = lower(turn(key_zero))
    keys_all, values_all = (
        lax.all_gather(key_low, "seq", axis=1, tiled=True),
        lax.all_gather(value_low, "seq", axis=1, tiled=True),
    )

    def attend(items):
        query_row, key_block, value_block, segment_row, key_row = items
        scores = scores_of(query_row, key_block, segment_row, key_row)
        top = jnp.max(scores, axis=-1, keepdims=True)
        expo = jnp.exp(scores - top)
        total = jnp.sum(expo, axis=-1, keepdims=True)
        probs = lower(expo / total)
        heads_value = value_block.reshape(length, heads_count, HEAD_DIM)
        mixed = jnp.einsum("hcl,lhd->chd", probs, heads_value, preferred_element_type=jnp.float32)
        return (mixed.reshape(columns, width), top[..., 0] + jnp.log(total[..., 0]))

    mixed_all, log_totals = lax.map(attend, (query_low, keys_all, values_all, segments, key_ids))
    mixed_low = lower(mixed_all)
    first_sum = inputs + project(mixed_low, full_out)
    act_two = lower(layer_norm(first_sum, norm2_gain, norm2_bias))
    upper = project(act_two, full_up)
    hidden_low = lower(gelu(upper))
    output = first_sum + project(hidden_low, full_down)
    half_width = width // 2
    half_hidden = full_up.shape[1] // 2
    grad_out_low = lower(cotangent)
    down_left = outer_sum(hidden_low, grad_out_low[..., :half_width])
    down_right = outer_sum(hidden_low, grad_out_low[..., half_width:])
    grad_hidden = project_back(grad_out_low, full_down)
    gelu_values, gelu_back = jax.vjp(gelu, upper)
    grad_upper = lower(gelu_back(grad_hidden)[0])
    up_left = outer_sum(act_two, grad_upper[..., :half_hidden])
    up_right = outer_sum(act_two, grad_upper[..., half_hidden:])
    grad_act_two = project_back(grad_upper, full_up)
    normed_two, norm_two_back = jax.vjp(layer_norm, first_sum, norm2_gain, norm2_bias)
    grad_first_norm, gain_two_grad, offset_two_grad = norm_two_back(grad_act_two)
    grad_first = cotangent + grad_first_norm
    grad_attn_low = lower(grad_first)
    out_grad = outer_sum(mixed_low, grad_attn_low)
    grad_mixed = lower(project_back(grad_attn_low, full_out))
    heads_mixed = mixed_all.reshape(groups, columns, heads_count, HEAD_DIM)
    heads_gm = grad_mixed.astype(jnp.float32).reshape(groups, columns, heads_count, HEAD_DIM)
    deltas = jnp.transpose(jnp.sum(heads_mixed * heads_gm, axis=-1), (0, 2, 1))
    key_source, value_source = (key_low, value_low)

    def attend_back(carry, items):
        query_row, grad_row, log_row, delta_row, segment_row, key_row, key_part, value_part = items
        queries_all, grads_all = (
            lax.all_gather(query_row, "seq", axis=0, tiled=True),
            lax.all_gather(grad_row, "seq", axis=0, tiled=True),
        )
        logs_all, deltas_all = (
            lax.all_gather(log_row, "seq", axis=1, tiled=True),
            lax.all_gather(delta_row, "seq", axis=1, tiled=True),
        )
        own_mask = (segment_row[None, :] == key_row[:, None]) & (
            places[None, :] <= key_places[:, None]
        )
        own_mask = own_mask & (
            (segment_row[None, :] >= 0) | (places[None, :] == key_places[:, None])
        )
        heads_query = queries_all.reshape(length, heads_count, HEAD_DIM)
        heads_grad = grads_all.reshape(length, heads_count, HEAD_DIM)
        heads_key = key_part.reshape(columns, heads_count, HEAD_DIM)
        heads_value = value_part.reshape(columns, heads_count, HEAD_DIM)
        raw = (
            jnp.einsum("lhd,chd->hlc", heads_query, heads_key, preferred_element_type=jnp.float32)
            * scale
        )
        scores = jnp.where(own_mask[None], raw, MASKED)
        probs = jnp.exp(scores - logs_all[..., None])
        grad_probs = jnp.einsum(
            "lhd,chd->hlc", heads_grad, heads_value, preferred_element_type=jnp.float32
        )
        grad_scores = lower(probs * (grad_probs - deltas_all[..., None]))
        grad_values = jnp.einsum(
            "hlc,lhd->chd", lower(probs), heads_grad, preferred_element_type=jnp.float32
        )
        grad_keys = (
            jnp.einsum("hlc,lhd->chd", grad_scores, heads_query, preferred_element_type=jnp.float32)
            * scale
        )
        partial_query = (
            jnp.einsum("hlc,chd->lhd", grad_scores, heads_key, preferred_element_type=jnp.float32)
            * scale
        )
        grad_query = lax.psum_scatter(
            partial_query.reshape(length, width).astype(jnp.bfloat16),
            "seq",
            scatter_dimension=0,
            tiled=True,
        ).astype(jnp.float32)
        return (
            carry,
            (grad_query, grad_keys.reshape(columns, width), grad_values.reshape(columns, width)),
        )

    start_carry = jnp.zeros((), jnp.float32)
    end_carry, grads_seq = lax.scan(
        attend_back,
        start_carry,
        (query_low, grad_mixed, log_totals, deltas, segments, key_ids, key_source, value_source),
    )
    grad_query_all, grad_key_all, grad_value_all = grads_seq
    turned_query, turn_back = jax.vjp(turn, query_zero)
    grad_query_low = lower(turn_back(grad_query_all)[0])
    grad_key_low = lower(turn_back(grad_key_all)[0])
    grad_value_low = lower(grad_value_all)
    query_grad = outer_sum(act_one, grad_query_low)
    key_grad = outer_sum(act_one, grad_key_low)
    value_grad = outer_sum(act_one, grad_value_low)
    grad_act_one = project_back(grad_query_low, full_query) + project_back(grad_key_low, full_key)
    grad_act_one = grad_act_one + project_back(grad_value_low, full_value)
    normed_again, norm_one_back = jax.vjp(layer_norm, inputs, norm1_gain, norm1_bias)
    grad_input_norm, gain_one_grad, offset_one_grad = norm_one_back(grad_act_one)
    grad_input = grad_first + grad_input_norm
    summed = (
        lax.psum_scatter(query_grad, ("dp", "seq"), scatter_dimension=0, tiled=True),
        lax.psum_scatter(key_grad, ("dp", "seq"), scatter_dimension=0, tiled=True),
        lax.psum_scatter(value_grad, ("dp", "seq"), scatter_dimension=0, tiled=True),
        lax.psum_scatter(out_grad, ("dp", "seq"), scatter_dimension=0, tiled=True),
        lax.psum_scatter(up_left, ("dp", "seq"), scatter_dimension=0, tiled=True),
        lax.psum_scatter(up_right, ("dp", "seq"), scatter_dimension=0, tiled=True),
        lax.psum_scatter(down_left, ("dp", "seq"), scatter_dimension=0, tiled=True),
        lax.psum_scatter(down_right, ("dp", "seq"), scatter_dimension=0, tiled=True),
        lax.psum_scatter(gain_one_grad, ("dp", "seq"), scatter_dimension=0, tiled=True),
        lax.psum_scatter(offset_one_grad, ("dp", "seq"), scatter_dimension=0, tiled=True),
        lax.psum_scatter(gain_two_grad, ("dp", "seq"), scatter_dimension=0, tiled=True),
        lax.psum_scatter(offset_two_grad, ("dp", "seq"), scatter_dimension=0, tiled=True),
    )
    query_grad, key_grad, value_grad, out_grad = (summed[0], summed[1], summed[2], summed[3])
    up_left, up_right, down_left, down_right = (summed[4], summed[5], summed[6], summed[7])
    gain_one_grad, offset_one_grad, gain_two_grad, offset_two_grad = (
        summed[8],
        summed[9],
        summed[10],
        summed[11],
    )
    up_grad = jnp.concatenate([up_left, up_right], axis=1)
    down_grad = jnp.concatenate([down_left, down_right], axis=1)
    return (
        output,
        grad_input,
        gain_one_grad,
        offset_one_grad,
        query_grad,
        key_grad,
        value_grad,
        out_grad,
        gain_two_grad,
        offset_two_grad,
        up_grad,
        down_grad,
    )


def solution(mesh):
    placed = (
        P("dp", "seq", None),
        P("dp", "seq"),
        P(),
        P(),
        P(("dp", "seq"), None),
        P(("dp", "seq"), None),
        P(("dp", "seq"), None),
        P(("dp", "seq"), None),
        P(),
        P(),
        P(("dp", "seq"), None),
        P(("dp", "seq"), None),
        P("dp", "seq", None),
    )
    return jax.shard_map(
        shards,
        mesh=mesh,
        in_specs=placed,
        out_specs=(
            P("dp", "seq", None),
            P("dp", "seq", None),
            P(("dp", "seq")),
            P(("dp", "seq")),
            P(("dp", "seq"), None),
            P(("dp", "seq"), None),
            P(("dp", "seq"), None),
            P(("dp", "seq"), None),
            P(("dp", "seq")),
            P(("dp", "seq")),
            P(("dp", "seq"), None),
            P(("dp", "seq"), None),
        ),
        check_vma=False,
    )
```

profile of v0, /device:TPU:0, one launch (start us, length us, event | category | flops | bytes accessed | tf_op | source)
XLA Modules:
  0.0 2556.1 jit_solution(2098317319195395891)
XLA Ops:
  15.1 62.2 %all-gather.27.cloned.1.call-done = bf16[1536,1536]{1,0:T(8,128)(2,1)} async-done(((bf16[48,1536]{1,0:T(8,128)(2,1)}), bf16[1536,1536]{1,0:T(8,128)(2,1)}) %all-gather.27.cloned.1.call-update) | async-done | bytes 4718608 | tf_op jit(solution)/shard_map/all_gather | solution.py:78
  84.3 58.4 %all-gather.33.cloned.1.call-done = bf16[1536,1536]{1,0:T(8,128)(2,1)} async-done(((bf16[48,1536]{1,0:T(8,128)(2,1)}), bf16[1536,1536]{1,0:T(8,128)(2,1)}) %all-gather.33.cloned.1.call-update) | async-done | bytes 4718608 | tf_op jit(solution)/shard_map/all_gather | solution.py:77
  147.7 60.4 %all-gather.31.cloned.1.call-done = bf16[1536,1536]{1,0:T(8,128)(2,1)} async-done(((bf16[48,1536]{1,0:T(8,128)(2,1)}), bf16[1536,1536]{1,0:T(8,128)(2,1)}) %all-gather.31.cloned.1.call-update) | async-done | bytes 4718608 | tf_op jit(solution)/shard_map/all_gather | solution.py:76
  230.3 50.6 %all-gather.29.cloned.1.call-done = bf16[2,2048,1536]{2,1,0:T(8,128)(2,1)} async-done(((bf16[2,256,1536]{2,1,0:T(8,128)(2,1)}), bf16[2,2048,1536]{2,1,0:T(8,128)(2,1)}) %all-gather.29.cloned.1.call-update) | async-done | bytes 12582928 | tf_op jit(solution)/shard_map/all_gather | solution.py:118
  280.9 76.3 %all-gather.35.cloned.1.call-done = bf16[2,2048,1536]{1,2,0:T(8,128)(2,1)} async-done(((bf16[2,256,1536]{1,2,0:T(8,128)(2,1)}), bf16[2,2048,1536]{1,2,0:T(8,128)(2,1)}) %all-gather.35.cloned.1.call-update) | async-done | bytes 12582928 | tf_op jit(solution)/shard_map/all_gather | solution.py:117
  359.0 119.5 %while.30 = (s32[]{:T(128)}, f32[2,256,1536]{1,2,0:T(8,128)}, f32[2,12,256]{2,1,0:T(8,128)S(1)}, bf16[2,2048,1536]{2,1,0:T(8,128)(2,1)}, s32[2,256]{1,0:T(2,128)...) while((s32[]{:T(128)}, f32[2,256,1536]{1,2,0:T(8,128)}, ...), condition=%wide.region_5.6_spmd.clone.clone, body=%wide.region_2.5_spmd.clone.clone.sunk | while | flops 3299867904 | bytes 135148688 | solution.py:132
  491.7 58.3 %all-gather.39.cloned.1.call-done = bf16[1536,6144]{1,0:T(8,128)(2,1)} async-done(((bf16[48,6144]{1,0:T(8,128)(2,1)}), bf16[1536,6144]{1,0:T(8,128)(2,1)}) %all-gather.39.cloned.1.call-update) | async-done | bytes 18874384 | tf_op jit(solution)/shard_map/all_gather | solution.py:80
  568.3 107.5 %all-gather.41.cloned.1.call-done = bf16[6144,1536]{1,0:T(8,128)(2,1)} async-done(((bf16[192,1536]{1,0:T(8,128)(2,1)}), bf16[6144,1536]{1,0:T(8,128)(2,1)}) %all-gather.41.cloned.1.call-update) | async-done | bytes 18874384 | tf_op jit(solution)/shard_map/all_gather | solution.py:81
  745.2 387.5 %while.31 = (s32[]{:T(128)}, f32[2,256,1536]{1,2,0:T(8,128)}, f32[2,256,1536]{1,2,0:T(8,128)}, bf16[2,256,1536]{1,2,0:T(8,128)(2,1)}, bf16[2,256,1536]{1,2,0:T(8...) while((s32[]{:T(128)}, f32[2,256,1536]{1,2,0:T(8,128)}, ...), condition=%wide.region_13.14_spmd.clone.clone, body=%wide.region_11.13_spmd.clone.clone.sunk | while | flops 8126202368 | bytes 275847040 | solution.py:214
  771.2 23.0 all-gather.43.cloned.1.call-done
  809.6 33.6 %all-gather.45.cloned.1.call-done = bf16[1,2048,1536]{1,2,0:T(8,128)(2,1)} async-done(((bf16[1,256,1536]{1,2,0:T(8,128)(2,1)}), bf16[1,2048,1536]{1,2,0:T(8,128)(2,1)}) %all-gather.45.cloned.1.call-update) | async-done | bytes 6291472 | tf_op jit(solution)/shard_map/while/body/eval_jaxpr/all_gather | solution.py:165
  897.4 37.7 %reduce-scatter.26.cloned.1.call-done = bf16[256,1536]{0,1:T(8,128)(2,1)} async-done(((bf16[2048,1536]{0,1:T(8,128)(2,1)}), bf16[256,1536]{0,1:T(8,128)(2,1)}) %reduce-scatter.26.cloned.1.call-update) | async-done | bytes 786448 | tf_op jit(solution)/shard_map/while/body/eval_jaxpr/reduce_scatter | solution.py:202
  963.7 24.6 all-gather.43.cloned.1.call-done
  1003.7 33.8 %all-gather.45.cloned.1.call-done = bf16[1,2048,1536]{1,2,0:T(8,128)(2,1)} async-done(((bf16[1,256,1536]{1,2,0:T(8,128)(2,1)}), bf16[1,2048,1536]{1,2,0:T(8,128)(2,1)}) %all-gather.45.cloned.1.call-update) | async-done | bytes 6291472 | tf_op jit(solution)/shard_map/while/body/eval_jaxpr/all_gather | solution.py:165
  1091.7 37.7 %reduce-scatter.26.cloned.1.call-done = bf16[256,1536]{0,1:T(8,128)(2,1)} async-done(((bf16[2048,1536]{0,1:T(8,128)(2,1)}), bf16[256,1536]{0,1:T(8,128)(2,1)}) %reduce-scatter.26.cloned.1.call-update) | async-done | bytes 786448 | tf_op jit(solution)/shard_map/while/body/eval_jaxpr/reduce_scatter | solution.py:202
  1222.7 42.1 %all-reduce.8 = (f32[1536]{0:T(1024)S(1)}, f32[1536]{0:T(1024)S(1)}, f32[1536]{0:T(1024)S(1)}, f32[1536]{0:T(1024)S(1)}) all-reduce(f32[1536]{0:T(1024)S(1)} %get-tuple-element.311, f32[1536]{0:T(1024)S(1)} %get-tuple-element.316, f32[1536]{0:T(1024)S(1)} %copy-done.45, ...), channel_id=7, replica_groups=mesh['dp'=4,'seq'=8] {'dp','seq'}, use_global_device_ids=true, to_apply=%region_17.18.clone | all-reduce | flops 6144 | bytes 49152
  1289.9 57.3 %reduce-scatter.24.cloned.1.call-done = f32[192,768]{1,0:T(8,128)} async-done(((f32[6144,768]{1,0:T(8,128)}), f32[192,768]{1,0:T(8,128)}) %reduce-scatter.24.cloned.1.call-update) | async-done | bytes 589840 | tf_op jit(solution)/shard_map/reduce_scatter | solution.py:240
  1347.2 211.9 %reduce-scatter.22.cloned.1.call-done = f32[192,768]{1,0:T(8,128)} async-done(((f32[6144,768]{1,0:T(8,128)}), f32[192,768]{1,0:T(8,128)}) %reduce-scatter.22.cloned.1.call-update) | async-done | bytes 589840 | tf_op jit(solution)/shard_map/reduce_scatter | solution.py:239
  1561.4 209.5 %reduce-scatter.20.cloned.1.call-done = f32[48,3072]{1,0:T(8,128)} async-done(((f32[1536,3072]{1,0:T(8,128)}), f32[48,3072]{1,0:T(8,128)}) %reduce-scatter.20.cloned.1.call-update) | async-done | bytes 589840 | tf_op jit(solution)/shard_map/reduce_scatter | solution.py:238
  1770.9 211.8 %reduce-scatter.18.cloned.1.call-done = f32[48,3072]{1,0:T(8,128)} async-done(((f32[1536,3072]{1,0:T(8,128)}), f32[48,3072]{1,0:T(8,128)}) %reduce-scatter.18.cloned.1.call-update) | async-done | bytes 589840 | tf_op jit(solution)/shard_map/reduce_scatter | solution.py:237
  1985.1 138.7 %reduce-scatter.10.cloned.1.call-done = f32[48,1536]{1,0:T(8,128)} async-done(((f32[1536,1536]{1,0:T(8,128)}), f32[48,1536]{1,0:T(8,128)}) %reduce-scatter.10.cloned.1.call-update) | async-done | bytes 294928 | tf_op jit(solution)/shard_map/reduce_scatter | solution.py:233
  2123.8 141.8 %reduce-scatter.12.cloned.1.call-done = f32[48,1536]{1,0:T(8,128)} async-done(((f32[1536,1536]{1,0:T(8,128)}), f32[48,1536]{1,0:T(8,128)}) %reduce-scatter.12.cloned.1.call-update) | async-done | bytes 294928 | tf_op jit(solution)/shard_map/reduce_scatter | solution.py:234
  2265.7 141.3 %reduce-scatter.14.cloned.1.call-done = f32[48,1536]{1,0:T(8,128)} async-done(((f32[1536,1536]{1,0:T(8,128)}), f32[48,1536]{1,0:T(8,128)}) %reduce-scatter.14.cloned.1.call-update) | async-done | bytes 294928 | tf_op jit(solution)/shard_map/reduce_scatter | solution.py:235
  2406.9 142.2 %reduce-scatter.16.cloned.1.call-done = f32[48,1536]{1,0:T(8,128)} async-done(((f32[1536,1536]{1,0:T(8,128)}), f32[48,1536]{1,0:T(8,128)}) %reduce-scatter.16.cloned.1.call-update) | async-done | bytes 294928 | tf_op jit(solution)/shard_map/reduce_scatter | solution.py:236
  (289 shorter events, 579.3 us)
Async XLA Ops:
  7.2 70.1 %all-gather.27.cloned.1.call-start = ((), (), s32[]{:S(2)}) async-start(), calls=%async_computation.9 | async-start | bytes 4866048 | tf_op jit(solution)/shard_map/all_gather | solution.py:78
  7.9 134.8 %all-gather.33.cloned.1.call-start = ((), (), s32[]{:S(2)}) async-start(), calls=%async_computation.12 | async-start | bytes 4866048 | tf_op jit(solution)/shard_map/all_gather | solution.py:77
  8.7 199.4 %all-gather.31.cloned.1.call-start = ((), (), s32[]{:S(2)}) async-start(), calls=%async_computation.11 | async-start | bytes 4866048 | tf_op jit(solution)/shard_map/all_gather | solution.py:76
  9.4 271.4 %all-gather.29.cloned.1.call-start = ((), (), s32[]{:S(2)}) async-start(), calls=%async_computation.10 | async-start | bytes 14155776 | tf_op jit(solution)/shard_map/all_gather | solution.py:118
  83.9 273.3 %all-gather.35.cloned.1.call-start = ((), (), s32[]{:S(2)}) async-start(), calls=%async_computation.13 | async-start | bytes 14155776 | tf_op jit(solution)/shard_map/all_gather | solution.py:117
  84.3 128.8 %copy-start.27 = (f32[256,64]{0,1:T(8,128)}, f32[256,64]{0,1:T(8,128)S(1)}, u32[]{:S(2)}) copy-start(f32[256,64]{0,1:T(8,128)S(1)} %get-tuple-element.386) | copy-start | bytes 196612
  84.3 128.8 %copy-start.29 = (f32[256,64]{0,1:T(8,128)}, f32[256,64]{0,1:T(8,128)S(1)}, u32[]{:S(2)}) copy-start(f32[256,64]{0,1:T(8,128)S(1)} %get-tuple-element.387) | copy-start | bytes 196612
  216.6 266.8 %all-gather.37.cloned.1.call-start = ((), (), s32[]{:S(2)}) async-start(), calls=%async_computation.14 | async-start | bytes 4866048 | tf_op jit(solution)/shard_map/all_gather | solution.py:79
  217.2 332.8 %all-gather.39.cloned.1.call-start = ((), (), s32[]{:S(2)}) async-start(), calls=%async_computation.15 | async-start | bytes 19464192 | tf_op jit(solution)/shard_map/all_gather | solution.py:80
  217.9 457.8 %all-gather.41.cloned.1.call-start = ((), (), s32[]{:S(2)}) async-start(), calls=%async_computation.16 | async-start | bytes 19464192 | tf_op jit(solution)/shard_map/all_gather | solution.py:81
  745.4 48.9 %all-gather.43.cloned.1.call-start = ((), (), s32[]{:S(2)}) async-start(), calls=%async_computation.25 | async-start | bytes 7077888 | tf_op jit(solution)/shard_map/while/body/eval_jaxpr/all_gather | solution.py:164
  747.5 95.7 %all-gather.45.cloned.1.call-start = ((), (), s32[]{:S(2)}) async-start(), calls=%async_computation.26 | async-start | bytes 7077888 | tf_op jit(solution)/shard_map/while/body/eval_jaxpr/all_gather | solution.py:165
  749.9 185.2 %reduce-scatter.26.cloned.1.call-start = ((), (), s32[]{:S(2)}) async-start(), calls=%async_computation.27 | async-start | bytes 7077888 | tf_op jit(solution)/shard_map/while/body/eval_jaxpr/reduce_scatter | solution.py:202
  938.0 50.3 %all-gather.43.cloned.1.call-start = ((), (), s32[]{:S(2)}) async-start(), calls=%async_computation.25 | async-start | bytes 7077888 | tf_op jit(solution)/shard_map/while/body/eval_jaxpr/all_gather | solution.py:164
  940.1 97.4 %all-gather.45.cloned.1.call-start = ((), (), s32[]{:S(2)}) async-start(), calls=%async_computation.26 | async-start | bytes 7077888 | tf_op jit(solution)/shard_map/while/body/eval_jaxpr/all_gather | solution.py:165
  942.5 186.8 %reduce-scatter.26.cloned.1.call-start = ((), (), s32[]{:S(2)}) async-start(), calls=%async_computation.27 | async-start | bytes 7077888 | tf_op jit(solution)/shard_map/while/body/eval_jaxpr/reduce_scatter | solution.py:202
  1132.7 214.5 %reduce-scatter.24.cloned.1.call-start = ((), (), s32[]{:S(2)}) async-start(), calls=%async_computation.24 | async-start | bytes 19464192 | tf_op jit(solution)/shard_map/reduce_scatter | solution.py:240
  1133.3 425.8 %reduce-scatter.22.cloned.1.call-start = ((), (), s32[]{:S(2)}) async-start(), calls=%async_computation.23 | async-start | bytes 19464192 | tf_op jit(solution)/shard_map/reduce_scatter | solution.py:239
  1146.0 624.9 %reduce-scatter.20.cloned.1.call-start = ((), (), s32[]{:S(2)}) async-start(), calls=%async_computation.22 | async-start | bytes 19464192 | tf_op jit(solution)/shard_map/reduce_scatter | solution.py:238
  1160.0 822.8 %reduce-scatter.18.cloned.1.call-start = ((), (), s32[]{:S(2)}) async-start(), calls=%async_computation.21 | async-start | bytes 19464192 | tf_op jit(solution)/shard_map/reduce_scatter | solution.py:237
  1172.5 951.4 %reduce-scatter.10.cloned.1.call-start = ((), (), s32[]{:S(2)}) async-start(), calls=%async_computation.17 | async-start | bytes 9732096 | tf_op jit(solution)/shard_map/reduce_scatter | solution.py:233
  1184.7 1080.9 %reduce-scatter.12.cloned.1.call-start = ((), (), s32[]{:S(2)}) async-start(), calls=%async_computation.18 | async-start | bytes 9732096 | tf_op jit(solution)/shard_map/reduce_scatter | solution.py:234
  1190.1 1216.8 %reduce-scatter.14.cloned.1.call-start = ((), (), s32[]{:S(2)}) async-start(), calls=%async_computation.19 | async-start | bytes 9732096 | tf_op jit(solution)/shard_map/reduce_scatter | solution.py:235
  1196.9 1352.2 %reduce-scatter.16.cloned.1.call-start = ((), (), s32[]{:S(2)}) async-start(), calls=%async_computation.20 | async-start | bytes 9732096 | tf_op jit(solution)/shard_map/reduce_scatter | solution.py:236
  (53 other events, 437.4 us)
Sparse Core Ops, SparseCore 0:
  10.9 66.3 all-gather.26
  80.2 62.4 all-gather.32
  145.6 62.4 all-gather.30
  209.8 70.9 all-gather.28
  282.6 74.5 all-gather.34
  359.9 63.6 all-gather.36
  426.5 123.4 all-gather.38
  552.9 122.8 all-gather.40
  748.7 45.5 all-gather.42
  796.5 46.6 all-gather.44
  873.3 61.7 reduce-scatter.25
  941.0 47.3 all-gather.42
  990.8 46.6 all-gather.44
  1067.6 61.7 reduce-scatter.25
  1139.6 207.4 reduce-scatter.23
  1353.4 205.5 reduce-scatter.21
  1565.3 205.5 reduce-scatter.19
  1777.2 205.5 reduce-scatter.17
  1989.2 134.5 reduce-scatter.9
  2131.2 134.4 reduce-scatter.11
  2272.1 134.7 reduce-scatter.13
  2414.4 134.6 reduce-scatter.15
where the time goes:
time: 2560 us
  waiting for transfers between devices  1920 us (75%)
  matrix products  376 us (15%)
  local copies, waits for them, and re-layouts  93.2 us (4%)
  blocking collectives  86.2 us (3%)
  other arithmetic  60 us (2%)
    reduce_scatter x1, waiting for transfers between devices, shards(): lax.psum_scatter(down_left, ('dp', 'seq'), scatter_dimension=0, tiled=True)  212 us
    reduce_scatter x1, waiting for transfers between devices, shards(): lax.psum_scatter(up_left, ('dp', 'seq'), scatter_dimension=0, tiled=True)  212 us
    reduce_scatter x1, waiting for transfers between devices, shards(): lax.psum_scatter(up_right, ('dp', 'seq'), scatter_dimension=0, tiled=True)  209 us
    reduce_scatter x1, waiting for transfers between devices, shards(): lax.psum_scatter(out_grad, ('dp', 'seq'), scatter_dimension=0, tiled=True)  142 us
    reduce_scatter x1, waiting for transfers between devices, shards(): lax.psum_scatter(key_grad, ('dp', 'seq'), scatter_dimension=0, tiled=True)  142 us
    reduce_scatter x1, waiting for transfers between devices, shards(): lax.psum_scatter(value_grad, ('dp', 'seq'), scatter_dimension=0, tiled=True)  141 us
    reduce_scatter x1, waiting for transfers between devices, shards(): lax.psum_scatter(query_grad, ('dp', 'seq'), scatter_dimension=0, tiled=True)  139 us
    all_gather x1, waiting for transfers between devices, shards(): lax.all_gather(w_down, ('dp', 'seq'), axis=0, tiled=True)  107 us
  transfers between devices with their start and end apart: 22, of which 21 were waited for; matrix products, arithmetic and copies ran while one was open for 15% of the time, Pallas kernels for 0%

commit v1 on v0

v1 whole, which is shorter than its diff:
```python
import functools
import math

import jax
import jax.numpy as jnp
from jax import lax
from jax.experimental import pallas as pl
from jax.experimental.pallas import tpu as pltpu
from jax.sharding import PartitionSpec as P

HEAD_DIM = 128


EPSILON = 1e-05
MASKED = -1e30
LOG2E = math.log2(math.e)
NT = (((1,), (1,)), ((), ()))
NN = (((1,), (0,)), ((), ()))


def dot(left, right, dims=NN):
    return lax.dot_general(left, right, dims, preferred_element_type=jnp.float32)


def allowed_pairs(key_col, query_row, diagonal):
    same = key_col == query_row
    if not diagonal:
        return same
    shape = (key_col.shape[0], query_row.shape[1])
    key_at = lax.broadcasted_iota(jnp.int32, shape, 0)
    query_at = lax.broadcasted_iota(jnp.int32, shape, 1)
    return (same & (key_at <= query_at)) | (key_at == query_at)


def attend_kernel(block, parts, q_ref, k_ref, v_ref, col_ref, row_ref, o_ref, ot_ref, lse_ref, vt_ref):
    step = pl.program_id(1)

    @pl.when(step == 0)
    def _():
        whole = v_ref[...].reshape(-1, HEAD_DIM)
        vt_ref[...] = whole.T

    query = q_ref[pl.ds(step * parts, parts)].reshape(block, HEAD_DIM)
    query_row = row_ref[0, pl.ds(step, 1), :]
    unit = LOG2E / math.sqrt(HEAD_DIM)

    def visit(j, carry, diagonal):
        top, total, mixed = carry
        key = k_ref[pl.ds(j * parts, parts)].reshape(block, HEAD_DIM)
        at = pl.multiple_of(j * block, block)
        key_col = col_ref[0, pl.ds(at, block), :]
        scores = dot(key, query, NT) * unit
        scores = jnp.where(allowed_pairs(key_col, query_row, diagonal), scores, MASKED)
        above = jnp.maximum(top, jnp.max(scores, axis=0, keepdims=True))
        expo = jnp.exp2(scores - above)
        fade = jnp.exp2(top - above)
        total = total * fade + jnp.sum(expo, axis=0, keepdims=True)
        mixed = mixed * fade + dot(vt_ref[:, pl.ds(at, block)], expo.astype(jnp.bfloat16))
        return above, total, mixed

    start = (
        jnp.full((1, block), MASKED, jnp.float32),
        jnp.zeros((1, block), jnp.float32),
        jnp.zeros((HEAD_DIM, block), jnp.float32),
    )
    carry = lax.fori_loop(0, step, lambda j, c: visit(j, c, False), start)
    top, total, mixed = visit(step, carry, True)
    mixed = mixed / total
    ot_ref[0, 0] = mixed
    lse_ref[0, pl.ds(step, 1), :] = top + jnp.log2(total)
    o_ref[...] = mixed.T.astype(jnp.bfloat16).reshape(o_ref.shape)


def attend_back_kernel(
    block, parts, q_ref, k_ref, v_ref, g_ref, ot_ref, lse_ref, col_ref, row_ref, cos_ref, sin_ref,
    out_ref, kt_ref, dk_ref, dv_ref,
):
    step = pl.program_id(1)
    last = pl.num_programs(1) - 1
    scale = 1.0 / math.sqrt(HEAD_DIM)

    @pl.when(step == 0)
    def _():
        kt_ref[...] = k_ref[...].reshape(-1, HEAD_DIM).T
        dk_ref[...] = jnp.zeros_like(dk_ref)
        dv_ref[...] = jnp.zeros_like(dv_ref)

    query = q_ref[pl.ds(step * parts, parts)].reshape(block, HEAD_DIM)
    grad = g_ref[pl.ds(step * parts, parts)].reshape(block, HEAD_DIM)
    query_row = row_ref[0, pl.ds(step, 1), :]
    lse = lse_ref[0, pl.ds(step, 1), :]
    delta = jnp.sum(ot_ref[0, 0] * grad.astype(jnp.float32).T, axis=0, keepdims=True)
    unit = LOG2E * scale

    def visit(j, dqt, diagonal):
        at = pl.multiple_of(j * block, block)
        key = k_ref[pl.ds(j * parts, parts)].reshape(block, HEAD_DIM)
        value = v_ref[pl.ds(j * parts, parts)].reshape(block, HEAD_DIM)
        key_col = col_ref[0, pl.ds(at, block), :]
        scores = dot(key, query, NT) * unit - lse
        probs = jnp.where(allowed_pairs(key_col, query_row, diagonal), jnp.exp2(scores), 0.0)
        grad_probs = dot(value, grad, NT)
        grad_scores = (probs * (grad_probs - delta)).astype(jnp.bfloat16)
        dv_ref[pl.ds(at, block), :] += dot(probs.astype(jnp.bfloat16), grad)
        dk_ref[pl.ds(at, block), :] += dot(grad_scores, query)
        return dqt + dot(kt_ref[:, pl.ds(at, block)], grad_scores)

    dqt = lax.fori_loop(
        0, step, lambda j, c: visit(j, c, False), jnp.zeros((HEAD_DIM, block), jnp.float32)
    )
    dqt = visit(step, dqt, True)

    def turn_back(values, cosine, sine):
        return values * cosine - pltpu.roll(values, HEAD_DIM // 2, 1) * sine

    at = pl.multiple_of(step * block, block)
    dq = turn_back(dqt.T * scale, cos_ref[pl.ds(at, block), :], sin_ref[pl.ds(at, block), :])
    out_ref[pl.ds(step * parts, parts), 0, 0] = dq.astype(jnp.bfloat16).reshape(parts, -1, HEAD_DIM)

    @pl.when(step == last)
    def _():
        dk = turn_back(dk_ref[...] * scale, cos_ref[...], sin_ref[...])
        shape = (out_ref.shape[0],) + out_ref.shape[3:]
        out_ref[:, 0, 1] = dk.astype(jnp.bfloat16).reshape(shape)
        out_ref[:, 0, 2] = dv_ref[...].astype(jnp.bfloat16).reshape(shape)


def pair_spec(count, which, columns):
    return pl.BlockSpec((count, None, None, columns, HEAD_DIM), lambda p, i: (0, p, which, 0, 0))


def attend(packed, seg_col, seg_row):
    count, per, _, columns, _ = packed.shape
    length = count * columns
    block = seg_row.shape[2]
    steps, parts = length // block, block // columns
    return pl.pallas_call(
        functools.partial(attend_kernel, block, parts),
        grid=(per, steps),
        in_specs=[
            pair_spec(count, 0, columns),
            pair_spec(count, 1, columns),
            pair_spec(count, 2, columns),
            pl.BlockSpec((1, length, 1), lambda p, i: (p, 0, 0)),
            pl.BlockSpec((1, steps, block), lambda p, i: (p, 0, 0)),
        ],
        out_specs=[
            pl.BlockSpec((parts, None, columns, HEAD_DIM), lambda p, i: (i, p, 0, 0)),
            pl.BlockSpec((1, 1, HEAD_DIM, block), lambda p, i: (p, i, 0, 0)),
            pl.BlockSpec((1, steps, block), lambda p, i: (p, 0, 0)),
        ],
        out_shape=[
            jax.ShapeDtypeStruct((count, per, columns, HEAD_DIM), jnp.bfloat16),
            jax.ShapeDtypeStruct((per, steps, HEAD_DIM, block), jnp.float32),
            jax.ShapeDtypeStruct((per, steps, block), jnp.float32),
        ],
        scratch_shapes=[pltpu.VMEM((HEAD_DIM, length), jnp.bfloat16)],
        compiler_params=pltpu.CompilerParams(vmem_limit_bytes=56 << 20),
    )(packed, packed, packed, seg_col, seg_row)


def attend_back(packed, grads, mixed_t, lse, seg_col, seg_row, cosine, sine):
    count, per, _, columns, _ = packed.shape
    length = count * columns
    block = seg_row.shape[2]
    steps, parts = length // block, block // columns
    return pl.pallas_call(
        functools.partial(attend_back_kernel, block, parts),
        grid=(per, steps),
        in_specs=[
            pair_spec(count, 0, columns),
            pair_spec(count, 1, columns),
            pair_spec(count, 2, columns),
            pl.BlockSpec((count, None, columns, HEAD_DIM), lambda p, i: (0, p, 0, 0)),
            pl.BlockSpec((1, 1, HEAD_DIM, block), lambda p, i: (p, i, 0, 0)),
            pl.BlockSpec((1, steps, block), lambda p, i: (p, 0, 0)),
            pl.BlockSpec((1, length, 1), lambda p, i: (p, 0, 0)),
            pl.BlockSpec((1, steps, block), lambda p, i: (p, 0, 0)),
            pl.BlockSpec((length, HEAD_DIM), lambda p, i: (0, 0)),
            pl.BlockSpec((length, HEAD_DIM), lambda p, i: (0, 0)),
        ],
        out_specs=pl.BlockSpec((count, 1, 3, columns, HEAD_DIM), lambda p, i: (0, p, 0, 0, 0)),
        out_shape=jax.ShapeDtypeStruct((count, per, 3, columns, HEAD_DIM), jnp.bfloat16),
        scratch_shapes=[
            pltpu.VMEM((HEAD_DIM, length), jnp.bfloat16),
            pltpu.VMEM((length, HEAD_DIM), jnp.float32),
            pltpu.VMEM((length, HEAD_DIM), jnp.float32),
        ],
        compiler_params=pltpu.CompilerParams(vmem_limit_bytes=56 << 20),
    )(packed, packed, packed, grads, mixed_t, lse, seg_col, seg_row, cosine, sine)


MESH = pl.DeviceIdType.MESH


class Plan:
    def __init__(self, mesh):
        self.n_dp, self.n_seq = mesh.shape["dp"], mesh.shape["seq"]
        bits = [1 << i for i in range(self.n_seq.bit_length() - 1)]
        self.bits = bits[::-1]
        if len(bits) == 3:
            self.orders = ((2, 4, 1), (4, 2, 1))
        else:
            turn = len(bits) // 2
            self.orders = (tuple(bits), tuple(bits[turn:] + bits[:turn]))
        self.hops = len(bits)
        self.masks = range(1, self.n_dp)

    def lead(self):
        return (self.n_dp,) + (2,) * self.hops


def place():
    return lax.axis_index("dp"), lax.axis_index("seq")


def partner_dp(plan, mask):
    dp, seq = place()
    return (lax.bitwise_xor(dp, mask), seq)


def partner_seq(bit):
    dp, seq = place()
    return (dp, lax.bitwise_xor(seq, bit))


def own_bit(bit):
    return lax.bitwise_and(lax.div(place()[1], bit), 1)


def greet(plan):
    barrier = pltpu.get_barrier_semaphore()
    others = [partner_dp(plan, m) for m in plan.masks] + [partner_seq(b) for b in plan.bits]
    for other in others:
        pl.semaphore_signal(barrier, inc=1, device_id=other, device_id_type=MESH)
    pl.semaphore_wait(barrier, len(others))


def gather_copies(plan, src, dst, half, cols, stage, slot, send, recv):
    dp, _ = place()
    me = tuple(own_bit(b) for b in plan.bits)
    copies = []
    if stage == 0:
        base = 0
        for n, mask in enumerate(plan.masks):
            at = half * (len(plan.masks) + plan.hops) + n
            copies.append(pltpu.make_async_remote_copy(
                src.at[:, cols], dst.at[(dp,) + me + (slice(None), cols)],
                send.at[slot, at], recv.at[slot, at],
                device_id=partner_dp(plan, mask), device_id_type=MESH))
    else:
        order = plan.orders[half]
        done = order[: stage - 1]
        where = tuple(slice(None) if b in done else m for b, m in zip(plan.bits, me))
        part = dst.at[(slice(None),) + where + (slice(None), cols)]
        at = half * (len(plan.masks) + plan.hops) + len(plan.masks) + stage - 1
        copies.append(pltpu.make_async_remote_copy(
            part, part, send.at[slot, at], recv.at[slot, at],
            device_id=partner_seq(order[stage - 1]), device_id_type=MESH))
    return copies


def gather_kernel(plan, pieces, count, lag, *refs):
    ins, outs = refs[:count], refs[count : 2 * count]
    held = refs[2 * count : 3 * count]
    send, recv, local = refs[3 * count :]
    loads = [pltpu.make_async_copy(src, own, local.at[i]) for i, (src, own) in enumerate(zip(ins, held))]
    for load in loads:
        load.start()
    greet(plan)
    dp, _ = place()
    me = tuple(own_bit(b) for b in plan.bits)
    keeps = [
        pltpu.make_async_copy(own, dst.at[(dp,) + me], local.at[i])
        for i, (own, dst) in enumerate(zip(held, outs))
    ]
    for load, keep in zip(loads, keeps):
        load.wait()
        keep.start()
    stages = plan.hops + 1

    def copies(u, stage):
        which, start, size = pieces[u]
        half = size // 2
        return [
            c
            for h in range(2)
            for c in gather_copies(
                plan, held[which], outs[which], h, pl.ds(start + h * half, half), stage, u % (2 * lag), send, recv
            )
        ]

    total = len(pieces)
    for tick in range(total + lag * stages):
        for stage in reversed(range(stages + 1)):
            u = tick - lag * stage
            if not 0 <= u < total:
                continue
            if stage > 0:
                for c in copies(u, stage - 1):
                    c.wait_recv()
                if u == 0 and stage == 1:
                    for keep in keeps:
                        keep.wait()
            if stage < stages:
                if u >= 2 * lag:
                    for c in copies(u - 2 * lag, stage):
                        c.wait_send()
                for c in copies(u, stage):
                    c.start()
    for u in range(max(total - 2 * lag, 0), total):
        for stage in range(stages):
            for c in copies(u, stage):
                c.wait_send()


def gather(plan, arrays, chunk_bytes, lag, collective_id):
    pieces = []
    for i, a in enumerate(arrays):
        rows, cols = a.shape
        n = max(1, round(rows * cols * 2 * plan.n_dp * plan.n_seq / chunk_bytes))
        while cols % (256 * n):
            n -= 1
        pieces += [(i, j * (cols // n), cols // n) for j in range(n)]
    count = len(arrays)
    each = 2 * (len(plan.masks) + plan.hops)
    outs = pl.pallas_call(
        functools.partial(gather_kernel, plan, pieces, count, lag),
        out_shape=[jax.ShapeDtypeStruct(plan.lead() + a.shape, a.dtype) for a in arrays],
        in_specs=[pl.BlockSpec(memory_space=pl.ANY)] * count,
        out_specs=[pl.BlockSpec(memory_space=pl.ANY)] * count,
        scratch_shapes=[pltpu.VMEM(a.shape, a.dtype) for a in arrays] + [
            pltpu.SemaphoreType.DMA((2 * lag, each)),
            pltpu.SemaphoreType.DMA((2 * lag, each)),
            pltpu.SemaphoreType.DMA((count,)),
        ],
        compiler_params=pltpu.CompilerParams(collective_id=collective_id, has_side_effects=True),
    )(*arrays)
    return [o.reshape(-1, o.shape[-1]) for o in outs]


def reduce_kernel(plan, jobs, count, lag, *refs):
    k = len(jobs)
    lefts, rights, out_ref = refs[:k], refs[k : 2 * k], refs[2 * k]
    hops, slots = plan.hops, 2 * lag
    scratch = refs[2 * k + 1 :]
    sums = [scratch[h * (hops + 1) : (h + 1) * (hops + 1)] for h in range(2)]
    scratch = scratch[2 * (hops + 1) :]
    got = [scratch[h * (hops + 1) : (h + 1) * (hops + 1)] for h in range(2)]
    send, recv = scratch[2 * (hops + 1) :]
    tick = pl.program_id(0)
    half = out_ref.shape[-1] // 2
    rows = out_ref.shape[-2]
    orders = [order[::-1] for order in plan.orders]
    dp, _ = place()

    @pl.when(tick == 0)
    def _():
        greet(plan)

    def at_bit(h, stage, value):
        left = [b for b in plan.bits if b not in orders[h][:stage]]
        return (slice(None),) + tuple(value if b == orders[h][stage] else slice(None) for b in left)

    def copies(h, stage, slot):
        if stage < hops:
            bit = orders[h][stage]
            at = h * (hops + len(plan.masks)) + stage
            return [pltpu.make_async_remote_copy(
                sums[h][stage].at[(slot,) + at_bit(h, stage, 1 - own_bit(bit))], got[h][stage].at[slot],
                send.at[slot, at], recv.at[slot, at], device_id=partner_seq(bit), device_id_type=MESH)]
        out = []
        for n, mask in enumerate(plan.masks):
            at = h * (hops + len(plan.masks)) + hops + n
            out.append(pltpu.make_async_remote_copy(
                sums[h][hops].at[slot, lax.bitwise_xor(dp, mask)], got[h][hops].at[slot, n],
                send.at[slot, at], recv.at[slot, at], device_id=partner_dp(plan, mask), device_id_type=MESH))
        return out

    def wide(values):
        return values.astype(jnp.float32)

    for stage in reversed(range(1, hops + 2)):
        u = tick - lag * stage

        @pl.when((u >= 0) & (u < count))
        def _(stage=stage, u=u):
            slot = lax.rem(u, slots)
            for h in range(2):
                for copy in copies(h, stage - 1, slot):
                    copy.wait()
                if stage <= hops:
                    mine = (slot,) + at_bit(h, stage - 1, own_bit(orders[h][stage - 1]))
                    total = wide(sums[h][stage - 1][mine]) + wide(got[h][stage - 1][slot])
                    sums[h][stage][slot] = total.astype(jnp.bfloat16)
                    for copy in copies(h, stage, slot):
                        copy.start()
                else:
                    total = wide(sums[h][hops][slot, dp])
                    for n in range(len(plan.masks)):
                        total = total + wide(got[h][hops][slot, n])
                    out_ref[0, :, h * half : (h + 1) * half] = total

    for (start, stop, cols), left, right in zip(jobs, lefts, rights):

        @pl.when((tick >= start) & (tick < stop))
        def _(start=start, cols=cols, left=left, right=right):
            slot = lax.rem(tick, slots)
            which = lax.div(tick - start, cols)
            step = rows * plan.n_seq
            for z in range(plan.n_dp):
                part = lax.dot_general(left[which, z * step : (z + 1) * step, :], right[...],
                    (((1,), (0,)), ((), ())), preferred_element_type=jnp.float32).astype(jnp.bfloat16)
                for h in range(2):
                    piece = part[:, h * half : (h + 1) * half]
                    sums[h][0][slot, z] = piece.reshape(plan.lead()[1:] + (rows, half))
            for h in range(2):
                for copy in copies(h, 0, slot):
                    copy.start()


def reduce_products(plan, pairs, width, lag, collective_id):
    jobs, start = [], 0
    left_specs, right_specs = [], []
    for left, right in pairs:
        cols = right.shape[1] // width
        stop = start + left.shape[0] * cols
        jobs.append((start, stop, cols))
        left_specs.append(pl.BlockSpec(left.shape, lambda t: (0, 0, 0)))
        right_specs.append(pl.BlockSpec(
            (right.shape[0], width),
            functools.partial(lambda t, start, stop, cols: (0, lax.rem(jnp.clip(t, start, stop - 1) - start, cols)),
                start=start, stop=stop, cols=cols)))
        start = stop
    count = start
    rows = pairs[0][0].shape[1] // (plan.n_dp * plan.n_seq)
    half = width // 2
    slots, hops = 2 * lag, plan.hops
    tail = lag * (hops + 1)
    sums = [pltpu.VMEM((slots, plan.n_dp) + (2,) * (hops - s) + (rows, half), jnp.bfloat16) for s in range(hops + 1)]
    got = [pltpu.VMEM((slots, plan.n_dp) + (2,) * (hops - 1 - s) + (rows, half), jnp.bfloat16) for s in range(hops)]
    got.append(pltpu.VMEM((slots, len(plan.masks), rows, half), jnp.bfloat16))
    each = 2 * (hops + len(plan.masks))
    return pl.pallas_call(
        functools.partial(reduce_kernel, plan, jobs, count, lag),
        grid=(count + tail,),
        in_specs=left_specs + right_specs,
        out_specs=pl.BlockSpec((1, rows, width), lambda t: (jnp.maximum(t - tail, 0), 0, 0)),
        out_shape=jax.ShapeDtypeStruct((count, rows, width), jnp.float32),
        scratch_shapes=sums + sums + got + got + [
            pltpu.SemaphoreType.DMA((slots, each)),
            pltpu.SemaphoreType.DMA((slots, each)),
        ],
        compiler_params=pltpu.CompilerParams(
            collective_id=collective_id, has_side_effects=True, vmem_limit_bytes=60 << 20),
    )(*[p[0] for p in pairs], *[p[1] for p in pairs])


def layer_norm(values, gain, offset):
    centre = values - jnp.mean(values, axis=-1, keepdims=True)
    spread = jnp.mean(centre * centre, axis=-1, keepdims=True)
    return centre * lax.rsqrt(spread + EPSILON) * gain + offset


def gelu(values):
    return 0.5 * values * (1.0 + lax.erf(values * (1.0 / math.sqrt(2.0))))


def lower(values):
    return values.astype(jnp.bfloat16)


def project(acts, weight):
    return jnp.einsum("gcd,de->gce", acts, weight, preferred_element_type=jnp.float32)


def project_back(grads, weight):
    return jnp.einsum("gce,de->gcd", grads, weight, preferred_element_type=jnp.float32)


def outer_sum(left, right):
    return jnp.einsum("gci,gcj->ij", left, right, preferred_element_type=jnp.float32)


def shards(
    inputs,
    segments,
    norm1_gain,
    norm1_bias,
    w_query,
    w_key,
    w_value,
    w_out,
    norm2_gain,
    norm2_bias,
    w_up,
    w_down,
    cotangent,
    *,
    plan,
):
    count = plan.n_seq
    axes = ("dp", "seq")
    groups, columns, width = inputs.shape
    heads = width // HEAD_DIM
    length = columns * count
    block = min(512, length)
    per = -(-groups * heads // count)
    weights = (w_query, w_key, w_value, w_out, w_up, w_down)
    own_kernels = w_query.shape[0] % 16 == 0
    if own_kernels:
        full = gather(plan, weights, 1.6e6, 2, 1)
    else:
        full = [lax.all_gather(w, axes, axis=0, tiled=True) for w in weights]
    full_query, full_key, full_value, full_out, full_up, full_down = full
    rank = lax.axis_index("seq")

    ids = lax.all_gather(segments, "seq", axis=1, tiled=True)
    pair_at = jnp.minimum(rank * per + jnp.arange(per, dtype=jnp.int32), groups * heads - 1)
    pair_ids = ids[pair_at // heads]
    seg_row = pair_ids.reshape(per, length // block, block)
    seg_col = jnp.where(pair_ids < 0, -2, pair_ids)[..., None]

    half = HEAD_DIM // 2
    rates = jnp.exp(jnp.arange(half, dtype=jnp.float32) * (-math.log(10000.0) / half))
    turned = jnp.arange(length, dtype=jnp.float32)[:, None] * rates[None, :]
    cosine, sine = jnp.cos(turned), jnp.sin(turned)
    cosine_all = jnp.concatenate([cosine, cosine], axis=1)
    sine_all = jnp.concatenate([-sine, sine], axis=1)
    cosine_own = lax.dynamic_slice_in_dim(cosine_all, rank * columns, columns)[None, :, None, :]
    sine_own = lax.dynamic_slice_in_dim(sine_all, rank * columns, columns)[None, :, None, :]

    def turn(values):
        shaped = values.reshape(groups, columns, heads, HEAD_DIM)
        return shaped * cosine_own + jnp.roll(shaped, half, axis=-1) * sine_own

    def to_pairs(values):
        shaped = values.reshape(groups, columns, heads, HEAD_DIM)
        shaped = jnp.transpose(shaped, (0, 2, 1, 3)).reshape(groups * heads, columns, HEAD_DIM)
        shaped = jnp.pad(shaped, ((0, count * per - groups * heads), (0, 0), (0, 0)))
        return shaped.reshape(count, per, columns, HEAD_DIM)

    def from_pairs(values):
        shaped = values.reshape(count * per, columns, HEAD_DIM)[: groups * heads]
        shaped = shaped.reshape(groups, heads, columns, HEAD_DIM)
        return jnp.transpose(shaped, (0, 2, 1, 3)).reshape(groups, columns, width)

    def swap(values):
        return lax.all_to_all(values, "seq", 0, 0)

    act_one = lower(layer_norm(inputs, norm1_gain, norm1_bias))
    query_low = lower(turn(project(act_one, full_query)))
    key_low = lower(turn(project(act_one, full_key)))
    value_low = lower(project(act_one, full_value))
    packed = swap(jnp.stack([to_pairs(query_low), to_pairs(key_low), to_pairs(value_low)], axis=2))
    mixed_pairs, mixed_t, lse = attend(packed, seg_col, seg_row)
    mixed_low = from_pairs(swap(mixed_pairs))

    first_sum = inputs + project(mixed_low, full_out)
    act_two = lower(layer_norm(first_sum, norm2_gain, norm2_bias))
    upper = project(act_two, full_up)
    hidden_low = lower(gelu(upper))
    output = first_sum + project(hidden_low, full_down)
    grad_out_low = lower(cotangent)
    grad_hidden = project_back(grad_out_low, full_down)
    gelu_values, gelu_back = jax.vjp(gelu, upper)
    grad_upper = lower(gelu_back(grad_hidden)[0])
    grad_act_two = project_back(grad_upper, full_up)
    normed_two, norm_two_back = jax.vjp(layer_norm, first_sum, norm2_gain, norm2_bias)
    grad_first_norm, gain_two_grad, offset_two_grad = norm_two_back(grad_act_two)
    grad_first = cotangent + grad_first_norm
    grad_attn_low = lower(grad_first)
    grad_mixed = lower(project_back(grad_attn_low, full_out))

    tokens = groups * columns
    width_piece = 512

    def flat(values):
        return values.reshape(tokens, -1)

    def left_of(values):
        turned = flat(values).T
        every = plan.n_dp * plan.n_seq
        turned = turned.reshape(every, -1, width // every, tokens)
        return jnp.transpose(turned, (1, 0, 2, 3)).reshape(-1, width, tokens)

    def reduce_all(pairs, collective_id):
        out = reduce_products(plan, pairs, width_piece, 2, collective_id)
        results, at = [], 0
        for left, right in pairs:
            blocks, cols = left.shape[0], right.shape[1] // width_piece
            part = out[at : at + blocks * cols].reshape(blocks, cols, -1, width_piece)
            results.append(jnp.transpose(part, (0, 2, 1, 3)).reshape(-1, right.shape[1]))
            at += blocks * cols
        return results

    if own_kernels:
        sums_one = reduce_all(
            [
                (left_of(hidden_low), flat(grad_out_low)),
                (left_of(act_two), flat(grad_upper)),
                (left_of(mixed_low), flat(grad_attn_low)),
            ],
            2,
        )

    def reduce_last(norm_sums):
        left = left_of(act_one)
        stacked = jnp.pad(jnp.stack(norm_sums, axis=1), ((0, 0), (0, tokens - len(norm_sums))))
        return reduce_all(
            [
                (left, flat(grad_query_low)),
                (left, flat(grad_key_low)),
                (left, flat(grad_value_low)),
                (lower(stacked)[None], jnp.eye(tokens, width_piece, dtype=jnp.bfloat16)),
            ],
            3,
        )

    grads = attend_back(
        packed, swap(to_pairs(grad_mixed)), mixed_t, lse, seg_col, seg_row, cosine_all, sine_all
    )
    grads = swap(grads)
    grad_query_low, grad_key_low, grad_value_low = (from_pairs(grads[:, :, i]) for i in range(3))

    grad_act_one = project_back(grad_query_low, full_query) + project_back(grad_key_low, full_key)
    grad_act_one = grad_act_one + project_back(grad_value_low, full_value)
    normed_again, norm_one_back = jax.vjp(layer_norm, inputs, norm1_gain, norm1_bias)
    grad_input_norm, gain_one_grad, offset_one_grad = norm_one_back(grad_act_one)
    grad_input = grad_first + grad_input_norm

    norm_sums = [gain_one_grad, offset_one_grad, gain_two_grad, offset_two_grad]
    if own_kernels:
        first, second = sums_one, reduce_last(norm_sums)
        down_grad, up_grad, out_grad = first
        query_grad, key_grad, value_grad, norm_rows = second
        norm_rows = [norm_rows[:, i] for i in range(4)]
    else:
        def spread(values):
            return lax.psum_scatter(values, axes, scatter_dimension=0, tiled=True).astype(jnp.float32)

        down_grad = spread(lower(outer_sum(hidden_low, grad_out_low)))
        up_grad = spread(lower(outer_sum(act_two, grad_upper)))
        out_grad = spread(lower(outer_sum(mixed_low, grad_attn_low)))
        query_grad = spread(lower(outer_sum(act_one, grad_query_low)))
        key_grad = spread(lower(outer_sum(act_one, grad_key_low)))
        value_grad = spread(lower(outer_sum(act_one, grad_value_low)))
        norm_rows = [spread(v) for v in norm_sums]

    return (
        output,
        grad_input,
        norm_rows[0],
        norm_rows[1],
        query_grad,
        key_grad,
        value_grad,
        out_grad,
        norm_rows[2],
        norm_rows[3],
        up_grad,
        down_grad,
    )


def solution(mesh):
    placed = (
        P("dp", "seq", None),
        P("dp", "seq"),
        P(),
        P(),
        P(("dp", "seq"), None),
        P(("dp", "seq"), None),
        P(("dp", "seq"), None),
        P(("dp", "seq"), None),
        P(),
        P(),
        P(("dp", "seq"), None),
        P(("dp", "seq"), None),
        P("dp", "seq", None),
    )
    return jax.shard_map(
        functools.partial(shards, plan=Plan(mesh)),
        mesh=mesh,
        in_specs=placed,
        out_specs=(
            P("dp", "seq", None),
            P("dp", "seq", None),
            P(("dp", "seq")),
            P(("dp", "seq")),
            P(("dp", "seq"), None),
            P(("dp", "seq"), None),
            P(("dp", "seq"), None),
            P(("dp", "seq"), None),
            P(("dp", "seq")),
            P(("dp", "seq")),
            P(("dp", "seq"), None),
            P(("dp", "seq"), None),
        ),
        check_vma=False,
    )
```

time: 2560 us -> 985 us (0.38)
  waiting for transfers between devices: 1920 us -> 34.7 us
  Pallas kernels: 0 us -> 599 us
  matrix products: 376 us -> 116 us
  blocking collectives: 86.2 us -> 57.7 us
    reduce_scatter x10 -> x0, waiting for transfers between devices: 1330 us -> none  [the longest x1 212 us: shards(): lax.psum_scatter(down_left, ('dp', 'seq'), scatter_dimension=0, tiled=True)]
    pallas_call x0 -> x5, Pallas kernels: none -> 599 us  [the longest x2 290 us: reduce_products(): pl.pallas_call(functools.partial(reduce_kernel, plan, jobs, count, lag),...]
    all_gather x12 -> x0, waiting for transfers between devices: 589 us -> none  [the longest x1 107 us: shards(): lax.all_gather(w_down, ('dp', 'seq'), axis=0, tiled=True)]
    dot_general x22 -> x0, matrix products: 259 us -> none  [the longest x8 71.7 us: outer_sum(): jnp.einsum('gci,gcj->ij', left, right, preferred_element_type=jnp.float32)]
    dynamic_slice x28 -> x2, local copies, waits for them, and re-layouts: 50.3 us -> 0.19 us  [the longest x1 0.09 us: shards(): lax.dynamic_slice_in_dim(sine_all, rank * columns, columns)]
    unnamed x1 -> x0, blocking collectives: 42.1 us -> none
    all_to_all x0 -> x4, waiting for transfers between devices: none -> 34.7 us  [swap(): return lax.all_to_all(values, 'seq', 0, 0)]
    reshape x0 -> x7, local copies, waits for them, and re-layouts: none -> 28.4 us  [the longest x3 13.7 us: flat(): return values.reshape(tokens, -1)]
  transfers between devices with their start and end apart: 22 -> 4, of which waited for: 21 -> 2; matrix products, arithmetic and copies ran while one was open for 15% -> 7% of each run, Pallas kernels for 0% -> 21%
where the time goes in v1:
time: 985 us; the launch traced here: 974 us
  Pallas kernels  599 us (61%)
  matrix products  116 us (12%)
  local copies, waits for them, and re-layouts  103 us (10%)
  blocking collectives  57.7 us (6%)
  other arithmetic  43.5 us (4%)
  waiting for transfers between devices  34.7 us (4%)
  starting transfers between devices  18.1 us (2%)
    pallas_call x2, Pallas kernels, reduce_products(): pl.pallas_call(functools.partial(reduce_kernel, plan, jobs, count, lag),...  290 us
    pallas_call x1, Pallas kernels, gather(): pl.pallas_call(functools.partial(gather_kernel, plan, pieces, count, lag)...  247 us
    dot_general x6, matrix products, project(): jnp.einsum('gcd,de->gce', acts, weight, preferred_element_type=jnp.float32)  59.6 us
    all_gather x1, blocking collectives, shards(): ids = lax.all_gather(segments, 'seq', axis=1, tiled=True)  57.7 us
    dot_general x6, matrix products, project_back(): jnp.einsum('gce,de->gcd', grads, weight, preferred_element_type=jnp.float32)  56.1 us
    pallas_call x1, Pallas kernels, attend_back(): pl.pallas_call(functools.partial(attend_back_kernel, block, parts), grid=...  37.7 us
    all_to_all x4, waiting for transfers between devices, swap(): return lax.all_to_all(values, 'seq', 0, 0)  34.7 us
    pallas_call x1, Pallas kernels, attend(): pl.pallas_call(functools.partial(attend_kernel, block, parts), grid=(per,...  24.6 us
  transfers between devices with their start and end apart: 4, of which 2 were waited for; matrix products, arithmetic and copies ran while one was open for 7% of the time, Pallas kernels for 21%

profile of v1, /device:TPU:0, one launch (start us, length us, event | category | flops | bytes accessed | tf_op | source)
XLA Modules:
  0.0 973.9 jit_solution(15235076610286518416)
XLA Ops:
  12.8 247.3 %shard_map.220 = (bf16[4,2,2,2,48,1536]{5,4,3,2,1,0:T(8,128)(2,1)}, bf16[4,2,2,2,48,1536]{5,4,3,2,1,0:T(8,128)(2,1)}, bf16[4,2,2,2,48,1536]{5,4,3,2,1,0:T(8,128)...) custom-call(bf16[48,1536]{1,0:T(8,128)(2,1)} %refs_0_.1, ...), custom_call_target="tpu_custom_call" | custom-call | tf_op jit(solution)/shard_map/pallas_call | solution.py:327
  260.1 6.6 convolution_convert_fusion.1
  271.9 6.7 copy.86
  278.5 7.1 fusion.12
  285.6 6.7 copy.82
  292.3 5.1 fusion.14
  306.0 5.0 pad_maximum_fusion
  315.8 57.7 %all_gather.3 = s32[2,2048]{1,0:T(2,128)S(1)} all-gather(s32[2,256]{1,0:T(2,128)S(1)} %copy-done.33), channel_id=1, replica_groups=mesh['dp'=4,'seq'=8] {'seq'}, dimensions={1}, use_global_device_ids=true | all-gather | bytes 18432 | tf_op jit(solution)/shard_map/all_gather | solution.py:518
  380.7 24.6 %shard_map.221 = (bf16[8,3,256,128]{3,2,1,0:T(8,128)(2,1)}, f32[3,4,128,512]{3,2,1,0:T(8,128)}, f32[3,4,512]{2,1,0:T(4,128)}) custom-call(bf16[8,3,3,256,128]{4,3,2,1,0:T(8,128)(2,1)} %all-to-all-done.q_ref.k_ref.v_ref, bf16[8,3,3,256,128]{4,3,2,1,0:T(8,128)(2,1)} %all-to-all-done.q_ref.k_ref.v_ref, ...), custom_call_target="tpu_custom_call" | custom-call | tf_op jit(solution)/shard_map/pallas_call | solution.py:137
  412.9 17.8 %all-to-all-done.1 = bf16[8,3,256,128]{3,2,1,0:T(8,128)(2,1)} async-done(((bf16[8,3,256,128]{3,2,1,0:T(8,128)(2,1)}), bf16[8,3,256,128]{3,2,1,0:T(8,128)(2,1)}, u32[]{:S(2)}, u32[]{:S(2)}) %all-to-all-start.1) | async-done | bytes 1572896 | tf_op jit(solution)/shard_map/all_to_all | solution.py:549
  433.3 5.2 fusion.32
  440.3 18.7 %multiply_convert_fusion = (bf16[2,256,6144]{2,1,0:T(8,128)(2,1)}, f32[2,256,6144]{2,1,0:T(8,128)}) fusion(bf16[2,256,1536]{2,1,0:T(8,128)(2,1)S(1)} %add_convert_fusion, bf16[1536,6144,1]{1,0,2:T(8,128)(2,1)} %bitcast.262), kind=kOutput, calls=%fused_computation.9 | convolution fusion | flops 9679405056 | bytes 39321600 | tf_op jit(solution)/shard_map/gcd,de->gce/dot_general | solution.py:474
  459.0 19.4 %fusion.4 = bf16[2,256,6144]{2,1,0:T(8,128)(2,1)} fusion(f32[2,256,6144]{2,1,0:T(8,128)} %get-tuple-element.62, bf16[6144,1536,1]{1,0,2:T(8,128)(2,1)} %bitcast.260, bf16[2,256,1536]{2,1,0:T(8,128)(2,1)S(1)} %copy-done.13), kind=kOutput, calls=%fused_computation.7 | convolution fusion | flops 9704570880 | bytes 39321600 | tf_op jit(solution)/shard_map/gce,de->gcd/dot_general | solution.py:478
  478.4 17.8 %multiply_reduce_fusion = (bf16[1536]{0:T(1024)(128)(2,1)S(1)}, f32[2,256]{1,0:T(2,128)S(1)}, bf16[1536]{0:T(1024)(128)(2,1)S(1)}, f32[2,256,1536]{2,1,0:T(8,128)}) fusion(f32[2,256,1536]{2,1,0:T(8,128)S(1)} %copy-done.3, f32[2,256]{1,0:T(2,128)S(1)} %fusion.25, f32[2,256]{1,0:T(2,128)S(1)} %broadcast_multiply_fusion, f32[1536]{0:T(1024)S(1)} %copy-done.22, ...), kind=kOutput, calls=%fused_computation.25 | convolution fusion | flops 9669963776 | bytes 31475712 | tf_op jit(solution)/shard_map/gce,de->gcd/dot_general | solution.py:478
  502.0 6.1 convolution_convert_fusion
  521.8 17.0 %all-to-all-done.2.g_ref = bf16[8,3,256,128]{3,2,1,0:T(8,128)(2,1)} async-done(((bf16[8,3,256,128]{3,2,1,0:T(8,128)(2,1)}), bf16[8,3,256,128]{3,2,1,0:T(8,128)(2,1)}, u32[]{:S(2)}, u32[]{:S(2)}) %all-to-all-start.2) | async-done | bytes 1572896 | tf_op jit(solution)/shard_map/all_to_all | solution.py:549
  538.7 37.7 %shard_map.222 = bf16[8,3,3,256,128]{4,3,2,1,0:T(8,128)(2,1)} custom-call(bf16[8,3,3,256,128]{4,3,2,1,0:T(8,128)(2,1)} %all-to-all-done.q_ref.k_ref.v_ref, bf16[8,3,3,256,128]{4,3,2,1,0:T(8,128)(2,1)} %all-to-all-done.q_ref.k_ref.v_ref, bf16[8,3,3,256,128]{4,3,2,1,0:T(8,128)(2,1)} %all-to-all-done.q_ref.k_ref.v_ref, ...), custom_call_target="tpu_custom_call" | custom-call | tf_op jit(solution)/shard_map/pallas_call | solution.py:167
  595.0 8.5 copy.113
  603.5 6.0 copy.114
  609.5 206.4 %shard_map.224 = f32[27,48,512]{2,1,0:T(8,128)} custom-call(bf16[4,1536,512]{2,1,0:T(8,128)(2,1)} %bitcast.206, bf16[1,1536,512]{2,1,0:T(8,128)(2,1)} %bitcast.235, bf16[1,1536,512]{2,1,0:T(8,128)(2,1)} %bitcast.234, bf16[512,1536]{1,0:T(8,128)(2,1)} %bitcast.236, bf16[512,6144]{1,0:T(8,128)(2,1)} %bitcast.232, bf16[512,1536]{1,0:T(8,128)(2,1)} %bitcast.237), custom_call_target="tpu_custom_call" | custom-call | tf_op jit(solution)/shard_map/pallas_call | solution.py:444
  823.1 16.8 %convolution_add_fusion = f32[2,256,1536]{2,1,0:T(8,128)} fusion(f32[2,256,1536]{2,1,0:T(8,128)S(1)} %copy-done.3, bf16[2,256,6144]{2,1,0:T(8,128)(2,1)} %get-tuple-element.61, bf16[6144,1536,1]{1,0,2:T(8,128)(2,1)} %bitcast.261), kind=kOutput, calls=%fused_computation.15 | convolution fusion | flops 9664462848 | bytes 31457280 | tf_op jit(solution)/shard_map/gcd,de->gce/dot_general | solution.py:474
  850.8 4.9 fusion.33
  878.5 83.4 %shard_map.223 = f32[10,48,512]{2,1,0:T(8,128)} custom-call(bf16[1,1536,512]{2,1,0:T(8,128)(2,1)} %bitcast.202, bf16[1,1536,512]{2,1,0:T(8,128)(2,1)} %bitcast.203, bf16[1,1536,512]{2,1,0:T(8,128)(2,1)} %bitcast.204, bf16[1,1536,512]{2,1,0:T(8,128)(2,1)} %pad_bitcast_fusion.refs_3_, bf16[512,1536]{1,0:T(8,128)(2,1)} %bitcast.219, ...), custom_call_target="tpu_custom_call" | custom-call | tf_op jit(solution)/shard_map/pallas_call | solution.py:444
  964.1 5.5 add_add_fusion.2
  (157 shorter events, 134.1 us)
Async XLA Ops:
  3.5 6.9 copy-start.20
  3.9 6.2 copy-start.29
  4.0 6.4 copy-start.23
  4.0 6.4 copy-start.18
  292.3 5.1 copy-start.11
  311.0 69.7 %all-to-all-start = ((bf16[8,3,3,256,128]{4,3,2,1,0:T(8,128)(2,1)}), bf16[8,3,3,256,128]{4,3,2,1,0:T(8,128)(2,1)}, u32[]{:S(2)}, u32[]{:S(2)}) async-start(bf16[8,3,3,256,128]{4,3,2,1,0:T(8,128)(2,1)} %pad_maximum_fusion), calls=%async_computation | async-start | bytes 9437184 | tf_op jit(solution)/shard_map/all_to_all | solution.py:549
  405.3 25.3 %all-to-all-start.1 = ((bf16[8,3,256,128]{3,2,1,0:T(8,128)(2,1)}), bf16[8,3,256,128]{3,2,1,0:T(8,128)(2,1)}, u32[]{:S(2)}, u32[]{:S(2)}) async-start(bf16[8,3,256,128]{3,2,1,0:T(8,128)(2,1)} %get-tuple-element.24), calls=%async_computation.1 | async-start | bytes 3145728 | tf_op jit(solution)/shard_map/all_to_all | solution.py:549
  440.3 18.7 %copy-start.12 = (bf16[2,256,1536]{2,1,0:T(8,128)(2,1)}, bf16[2,256,1536]{2,1,0:T(8,128)(2,1)S(1)}, u32[]{:S(2)}) copy-start(bf16[2,256,1536]{2,1,0:T(8,128)(2,1)S(1)} %add_convert_fusion) | copy-start | bytes 4718596
  440.3 18.7 %copy-start.13 = (bf16[2,256,1536]{2,1,0:T(8,128)(2,1)S(1)}, bf16[2,256,1536]{2,1,0:T(8,128)(2,1)}, u32[]{:S(2)}) copy-start(bf16[2,256,1536]{2,1,0:T(8,128)(2,1)} %convert_element_type.42) | copy-start | bytes 4718596
  459.0 19.4 %copy-start.3 = (f32[2,256,1536]{2,1,0:T(8,128)S(1)}, f32[2,256,1536]{2,1,0:T(8,128)}, u32[]{:S(2)}) copy-start(f32[2,256,1536]{2,1,0:T(8,128)} %copy-done.2) | copy-start | bytes 9437188
  513.4 25.3 %all-to-all-start.2 = ((bf16[8,3,256,128]{3,2,1,0:T(8,128)(2,1)}), bf16[8,3,256,128]{3,2,1,0:T(8,128)(2,1)}, u32[]{:S(2)}, u32[]{:S(2)}) async-start(bf16[8,3,256,128]{3,2,1,0:T(8,128)(2,1)} %bitcast.224), calls=%async_computation.2 | async-start | bytes 3145728 | tf_op jit(solution)/shard_map/all_to_all | solution.py:549
  576.4 263.6 %all-to-all-start.3 = ((bf16[8,3,3,256,128]{4,3,2,1,0:T(8,128)(2,1)}), bf16[8,3,3,256,128]{4,3,2,1,0:T(8,128)(2,1)}, u32[]{:S(2)}, u32[]{:S(2)}) async-start(bf16[8,3,3,256,128]{4,3,2,1,0:T(8,128)(2,1)} %shard_map.222), calls=%async_computation.3 | async-start | bytes 9437184 | tf_op jit(solution)/shard_map/all_to_all | solution.py:549
  844.0 5.3 copy-start.8
  844.0 5.3 copy-start.6
  850.8 4.9 copy-start.16
  850.8 9.7 %slice-start = ((s8[4718592]{0:T(1024)(128)(4,1)}), s8[4194304]{0:T(1024)(128)(4,1)S(1)}, s32[]{:S(2)}) async-start(s8[4718592]{0:T(1024)(128)(4,1)} %bitcast.265), calls=%async_computation.4 | async-start | bytes 8388608
  855.8 4.8 copy-start.1
  855.8 4.8 copy-start.15
  855.8 4.8 copy-start.19
  855.8 4.8 copy-start.21
  855.8 4.8 slice-start.1
  878.5 85.6 %copy-start.32 = (f32[2,256]{1,0:T(2,128)S(1)}, f32[2,256]{1,0:T(2,128)}, u32[]{:S(2)}) copy-start(f32[2,256]{1,0:T(2,128)} %get-tuple-element.31) | copy-start | bytes 6148
  878.5 85.6 %copy-start.26 = (f32[2,256]{1,0:T(2,128)S(1)}, f32[2,256]{1,0:T(2,128)}, u32[]{:S(2)}) copy-start(f32[2,256]{1,0:T(2,128)} %copy-done.25) | copy-start | bytes 6148
  878.5 85.6 %copy-start.28 = (f32[2,256]{1,0:T(2,128)S(1)}, f32[2,256]{1,0:T(2,128)}, u32[]{:S(2)}) copy-start(f32[2,256]{1,0:T(2,128)} %copy-done.27) | copy-start | bytes 6148
  (16 other events, 36.9 us)

commit v2 on v1

--- a/solution.py
+++ b/solution.py
@@ -71,12 +71,10 @@
     o_ref[...] = mixed.T.astype(jnp.bfloat16).reshape(o_ref.shape)
 
 
-def attend_back_kernel(
-    block, parts, q_ref, k_ref, v_ref, g_ref, ot_ref, lse_ref, col_ref, row_ref, cos_ref, sin_ref,
+def attend_back_step(
+    block, parts, step, last, q_ref, k_ref, v_ref, g_ref, ot_ref, lse_ref, col_ref, row_ref, cos_ref, sin_ref,
     out_ref, kt_ref, dk_ref, dv_ref,
 ):
-    step = pl.program_id(1)
-    last = pl.num_programs(1) - 1
     scale = 1.0 / math.sqrt(HEAD_DIM)
 
     @pl.when(step == 0)
@@ -115,14 +113,13 @@
 
     at = pl.multiple_of(step * block, block)
     dq = turn_back(dqt.T * scale, cos_ref[pl.ds(at, block), :], sin_ref[pl.ds(at, block), :])
-    out_ref[pl.ds(step * parts, parts), 0, 0] = dq.astype(jnp.bfloat16).reshape(parts, -1, HEAD_DIM)
+    out_ref[0, pl.ds(at, block), :] = dq.astype(jnp.bfloat16)
 
     @pl.when(step == last)
     def _():
         dk = turn_back(dk_ref[...] * scale, cos_ref[...], sin_ref[...])
-        shape = (out_ref.shape[0],) + out_ref.shape[3:]
-        out_ref[:, 0, 1] = dk.astype(jnp.bfloat16).reshape(shape)
-        out_ref[:, 0, 2] = dv_ref[...].astype(jnp.bfloat16).reshape(shape)
+        out_ref[1] = dk.astype(jnp.bfloat16)
+        out_ref[2] = dv_ref[...].astype(jnp.bfloat16)
 
 
 def pair_spec(count, which, columns):
@@ -159,35 +156,66 @@
     )(packed, packed, packed, seg_col, seg_row)
 
 
-def attend_back(packed, grads, mixed_t, lse, seg_col, seg_row, cosine, sine):
-    count, per, _, columns, _ = packed.shape
-    length = count * columns
-    block = seg_row.shape[2]
-    steps, parts = length // block, block // columns
-    return pl.pallas_call(
-        functools.partial(attend_back_kernel, block, parts),
-        grid=(per, steps),
-        in_specs=[
-            pair_spec(count, 0, columns),
-            pair_spec(count, 1, columns),
-            pair_spec(count, 2, columns),
-            pl.BlockSpec((count, None, columns, HEAD_DIM), lambda p, i: (0, p, 0, 0)),
-            pl.BlockSpec((1, 1, HEAD_DIM, block), lambda p, i: (p, i, 0, 0)),
-            pl.BlockSpec((1, steps, block), lambda p, i: (p, 0, 0)),
-            pl.BlockSpec((1, length, 1), lambda p, i: (p, 0, 0)),
-            pl.BlockSpec((1, steps, block), lambda p, i: (p, 0, 0)),
-            pl.BlockSpec((length, HEAD_DIM), lambda p, i: (0, 0)),
-            pl.BlockSpec((length, HEAD_DIM), lambda p, i: (0, 0)),
-        ],
-        out_specs=pl.BlockSpec((count, 1, 3, columns, HEAD_DIM), lambda p, i: (0, p, 0, 0, 0)),
-        out_shape=jax.ShapeDtypeStruct((count, per, 3, columns, HEAD_DIM), jnp.bfloat16),
-        scratch_shapes=[
+class AttendBack:
+    def __init__(self, first, packed, grads, mixed_t, lse, seg_col, seg_row, cosine, sine):
+        count, per, _, columns, _ = packed.shape
+        length = count * columns
+        self.block = seg_row.shape[2]
+        self.steps, self.parts = length // self.block, self.block // columns
+        self.first, self.ticks = first, per * self.steps
+        self.operands = (packed, packed, packed, grads, mixed_t, lse, seg_col, seg_row, cosine, sine)
+
+        def pair(t):
+            return lax.div(jnp.clip(t - first, 0, self.ticks - 1), self.steps)
+
+        def step(t):
+            return lax.rem(jnp.clip(t - first, 0, self.ticks - 1), self.steps)
+
+        def whole(which):
+            return pl.BlockSpec((count, None, None, columns, HEAD_DIM), lambda t: (0, pair(t), which, 0, 0))
+
+        rows = pl.BlockSpec((1, self.steps, self.block), lambda t: (pair(t), 0, 0))
+        table = pl.BlockSpec((length, HEAD_DIM), lambda t: (0, 0))
+        self.in_specs = [
+            whole(0),
+            whole(1),
+            whole(2),
+            pl.BlockSpec((count, None, columns, HEAD_DIM), lambda t: (0, pair(t), 0, 0)),
+            pl.BlockSpec((1, 1, HEAD_DIM, self.block), lambda t: (pair(t), step(t), 0, 0)),
+            rows,
+            pl.BlockSpec((1, length, 1), lambda t: (pair(t), 0, 0)),
+            rows,
+            table,
+            table,
+        ]
+        self.out_specs = [pl.BlockSpec((3, length, HEAD_DIM), lambda t: (0, 0, pair(t)))]
+        self.out_shapes = [jax.ShapeDtypeStruct((3, length, per * HEAD_DIM), jnp.bfloat16)]
+        self.scratch = [
             pltpu.VMEM((HEAD_DIM, length), jnp.bfloat16),
             pltpu.VMEM((length, HEAD_DIM), jnp.float32),
             pltpu.VMEM((length, HEAD_DIM), jnp.float32),
-        ],
+        ]
+
+    def run(self, tick, refs):
+        @pl.when((tick >= self.first) & (tick < self.first + self.ticks))
+        def _():
+            step = lax.rem(tick - self.first, self.steps)
+            attend_back_step(self.block, self.parts, step, self.steps - 1, *refs)
+
+
+def attend_back_alone(work):
+    def kernel(*refs):
+        work.run(pl.program_id(0), refs)
+
+    return pl.pallas_call(
+        kernel,
+        grid=(work.first + work.ticks,),
+        in_specs=work.in_specs,
+        out_specs=work.out_specs,
+        out_shape=work.out_shapes,
+        scratch_shapes=work.scratch,
         compiler_params=pltpu.CompilerParams(vmem_limit_bytes=56 << 20),
-    )(packed, packed, packed, grads, mixed_t, lse, seg_col, seg_row, cosine, sine)
+    )(*work.operands)[0]
 
 
 MESH = pl.DeviceIdType.MESH
@@ -236,114 +264,15 @@
     pl.semaphore_wait(barrier, len(others))
 
 
-def gather_copies(plan, src, dst, half, cols, stage, slot, send, recv):
-    dp, _ = place()
-    me = tuple(own_bit(b) for b in plan.bits)
-    copies = []
-    if stage == 0:
-        base = 0
-        for n, mask in enumerate(plan.masks):
-            at = half * (len(plan.masks) + plan.hops) + n
-            copies.append(pltpu.make_async_remote_copy(
-                src.at[:, cols], dst.at[(dp,) + me + (slice(None), cols)],
-                send.at[slot, at], recv.at[slot, at],
-                device_id=partner_dp(plan, mask), device_id_type=MESH))
-    else:
-        order = plan.orders[half]
-        done = order[: stage - 1]
-        where = tuple(slice(None) if b in done else m for b, m in zip(plan.bits, me))
-        part = dst.at[(slice(None),) + where + (slice(None), cols)]
-        at = half * (len(plan.masks) + plan.hops) + len(plan.masks) + stage - 1
-        copies.append(pltpu.make_async_remote_copy(
-            part, part, send.at[slot, at], recv.at[slot, at],
-            device_id=partner_seq(order[stage - 1]), device_id_type=MESH))
-    return copies
-
-
-def gather_kernel(plan, pieces, count, lag, *refs):
-    ins, outs = refs[:count], refs[count : 2 * count]
-    held = refs[2 * count : 3 * count]
-    send, recv, local = refs[3 * count :]
-    loads = [pltpu.make_async_copy(src, own, local.at[i]) for i, (src, own) in enumerate(zip(ins, held))]
-    for load in loads:
-        load.start()
-    greet(plan)
-    dp, _ = place()
-    me = tuple(own_bit(b) for b in plan.bits)
-    keeps = [
-        pltpu.make_async_copy(own, dst.at[(dp,) + me], local.at[i])
-        for i, (own, dst) in enumerate(zip(held, outs))
-    ]
-    for load, keep in zip(loads, keeps):
-        load.wait()
-        keep.start()
-    stages = plan.hops + 1
-
-    def copies(u, stage):
-        which, start, size = pieces[u]
-        half = size // 2
-        return [
-            c
-            for h in range(2)
-            for c in gather_copies(
-                plan, held[which], outs[which], h, pl.ds(start + h * half, half), stage, u % (2 * lag), send, recv
-            )
-        ]
-
-    total = len(pieces)
-    for tick in range(total + lag * stages):
-        for stage in reversed(range(stages + 1)):
-            u = tick - lag * stage
-            if not 0 <= u < total:
-                continue
-            if stage > 0:
-                for c in copies(u, stage - 1):
-                    c.wait_recv()
-                if u == 0 and stage == 1:
-                    for keep in keeps:
-                        keep.wait()
-            if stage < stages:
-                if u >= 2 * lag:
-                    for c in copies(u - 2 * lag, stage):
-                        c.wait_send()
-                for c in copies(u, stage):
-                    c.start()
-    for u in range(max(total - 2 * lag, 0), total):
-        for stage in range(stages):
-            for c in copies(u, stage):
-                c.wait_send()
-
-
-def gather(plan, arrays, chunk_bytes, lag, collective_id):
-    pieces = []
-    for i, a in enumerate(arrays):
-        rows, cols = a.shape
-        n = max(1, round(rows * cols * 2 * plan.n_dp * plan.n_seq / chunk_bytes))
-        while cols % (256 * n):
-            n -= 1
-        pieces += [(i, j * (cols // n), cols // n) for j in range(n)]
-    count = len(arrays)
-    each = 2 * (len(plan.masks) + plan.hops)
-    outs = pl.pallas_call(
-        functools.partial(gather_kernel, plan, pieces, count, lag),
-        out_shape=[jax.ShapeDtypeStruct(plan.lead() + a.shape, a.dtype) for a in arrays],
-        in_specs=[pl.BlockSpec(memory_space=pl.ANY)] * count,
-        out_specs=[pl.BlockSpec(memory_space=pl.ANY)] * count,
-        scratch_shapes=[pltpu.VMEM(a.shape, a.dtype) for a in arrays] + [
-            pltpu.SemaphoreType.DMA((2 * lag, each)),
-            pltpu.SemaphoreType.DMA((2 * lag, each)),
-            pltpu.SemaphoreType.DMA((count,)),
-        ],
-        compiler_params=pltpu.CompilerParams(collective_id=collective_id, has_side_effects=True),
-    )(*arrays)
-    return [o.reshape(-1, o.shape[-1]) for o in outs]
-
-
-def reduce_kernel(plan, jobs, count, lag, *refs):
+def reduce_kernel(plan, jobs, count, lag, beside, *refs):
     k = len(jobs)
-    lefts, rights, out_ref = refs[:k], refs[k : 2 * k], refs[2 * k]
+    lefts, rights, refs = refs[:k], refs[k : 2 * k], refs[2 * k :]
+    more = [0, 0, 0] if beside is None else [len(beside.in_specs), len(beside.out_specs), len(beside.scratch)]
+    extra, refs = refs[: more[0]], refs[more[0] :]
+    out_ref, extra = refs[0], extra + refs[1 : 1 + more[1]]
+    scratch = refs[1 + more[1] :]
+    extra, scratch = extra + scratch[: more[2]], scratch[more[2] :]
     hops, slots = plan.hops, 2 * lag
-    scratch = refs[2 * k + 1 :]
     sums = [scratch[h * (hops + 1) : (h + 1) * (hops + 1)] for h in range(2)]
     scratch = scratch[2 * (hops + 1) :]
     got = [scratch[h * (hops + 1) : (h + 1) * (hops + 1)] for h in range(2)]
@@ -418,8 +347,11 @@
                 for copy in copies(h, 0, slot):
                     copy.start()
 
-
-def reduce_products(plan, pairs, width, lag, collective_id):
+    if beside is not None:
+        beside.run(tick, extra)
+
+
+def reduce_products(plan, pairs, width, lag, collective_id, beside=None):
     jobs, start = [], 0
     left_specs, right_specs = [], []
     for left, right in pairs:
@@ -441,19 +373,429 @@
     got = [pltpu.VMEM((slots, plan.n_dp) + (2,) * (hops - 1 - s) + (rows, half), jnp.bfloat16) for s in range(hops)]
     got.append(pltpu.VMEM((slots, len(plan.masks), rows, half), jnp.bfloat16))
     each = 2 * (hops + len(plan.masks))
+    out_specs = [pl.BlockSpec((1, rows, width), lambda t: (jnp.maximum(t - tail, 0), 0, 0))]
+    out_shapes = [jax.ShapeDtypeStruct((count, rows, width), jnp.float32)]
+    more_in, more_scratch, more_operands = [], [], []
+    if beside is not None:
+        more_in, more_scratch, more_operands = beside.in_specs, beside.scratch, beside.operands
+        out_specs, out_shapes = out_specs + beside.out_specs, out_shapes + beside.out_shapes
     return pl.pallas_call(
-        functools.partial(reduce_kernel, plan, jobs, count, lag),
+        functools.partial(reduce_kernel, plan, jobs, count, lag, beside),
         grid=(count + tail,),
-        in_specs=left_specs + right_specs,
-        out_specs=pl.BlockSpec((1, rows, width), lambda t: (jnp.maximum(t - tail, 0), 0, 0)),
-        out_shape=jax.ShapeDtypeStruct((count, rows, width), jnp.float32),
-        scratch_shapes=sums + sums + got + got + [
+        in_specs=left_specs + right_specs + more_in,
+        out_specs=out_specs,
+        out_shape=out_shapes,
+        scratch_shapes=more_scratch + sums + sums + got + got + [
             pltpu.SemaphoreType.DMA((slots, each)),
             pltpu.SemaphoreType.DMA((slots, each)),
         ],
         compiler_params=pltpu.CompilerParams(
             collective_id=collective_id, has_side_effects=True, vmem_limit_bytes=60 << 20),
-    )(*[p[0] for p in pairs], *[p[1] for p in pairs])
+    )(*[p[0] for p in pairs], *[p[1] for p in pairs], *more_operands)
+
+
+class Copies:
+    def __init__(self, send, recv):
+        self.send, self.recv, self.count, self.sent = send, recv, 0, []
+
+    def remote(self, src, dst, device):
+        at = self.count
+        self.count += 1
+        return pltpu.make_async_remote_copy(
+            src, dst, self.send.at[at], self.recv.at[at], device_id=device, device_id_type=MESH)
+
+    def run(self, pieces, lag):
+        last = max(start + lag * len(stages) for start, stages in pieces)
+        for tick in range(last + 1):
+            for stage in reversed(range(max(len(stages) for _, stages in pieces) + 1)):
+                for start, stages in pieces:
+                    if start + lag * stage != tick or stage > len(stages):
+                        continue
+                    if stage > 0:
+                        for copy in stages[stage - 1][1]:
+                            copy.wait_recv()
+                    if stage < len(stages):
+                        ahead, copies = stages[stage]
+                        if ahead is not None:
+                            ahead()
+                        for copy in copies:
+                            copy.start()
+        for _, stages in pieces:
+            for _, copies in stages:
+                for copy in copies:
+                    copy.wait_send()
+
+
+def start_kernel(
+    plan, splits, lag, h_ref, q_ref, k_ref, v_ref, *refs,
+):
+    n = len(splits)
+    ins, refs = refs[:n], refs[n:]
+    hs_ref, w_ref, outs = refs[0], refs[1], refs[2 : 2 + n]
+    hv, wv, halves = refs[2 + n : 5 + n]
+    held = refs[5 + n : 5 + 2 * n]
+    send, recv, local = refs[5 + 2 * n :]
+    dp, seq = place()
+    y, x, c = own_bit(4), own_bit(2), own_bit(1)
+    loads = [pltpu.make_async_copy(h_ref.at[y], hv, local.at[0])]
+    loads += [pltpu.make_async_copy(r, wv.at[i], local.at[1 + i]) for i, r in enumerate((q_ref, k_ref, v_ref))]
+    loads += [pltpu.make_async_copy(r, o, local.at[4 + i]) for i, (r, o) in enumerate(zip(ins, held))]
+    for load in loads:
+        load.start()
+    greet(plan)
+    for load in loads:
+        load.wait()
+    own = pltpu.make_async_copy(hv, hs_ref.at[y, x, c], local.at[0])
+    own.start()
+    me = (y, x, c)
+    keeps = [pltpu.make_async_copy(o, d.at[(dp,) + me], local.at[4 + i]) for i, (o, d) in enumerate(zip(held, outs))]
+    for keep in keeps:
+        keep.start()
+    run = Copies(send, recv)
+    pieces = []
+
+    tokens = hv.shape[0]
+    parts = 4
+    for i in range(parts):
+        rows = pl.ds(i * (tokens // parts), tokens // parts)
+        first = run.remote(h_ref.at[1 - y, rows], hs_ref.at[y, x, c, rows], partner_seq(4))
+        second = [run.remote(hs_ref.at[:, x, c, rows], hs_ref.at[:, x, c, rows], partner_seq(2))]
+        third = [run.remote(hs_ref.at[:, :, c, rows], hs_ref.at[:, :, c, rows], partner_seq(1))]
+        pieces.append((i, [(None, [first]), (own.wait if i == 0 else None, second), (None, third)]))
+
+    half, quarter = halves.shape[-1], w_ref.shape[-1]
+    for i in range(3):
+        mine = pltpu.make_async_copy(
+            halves.at[i, :, :, pl.ds(c * quarter, quarter)], w_ref.at[i, dp, y, :, c], local.at[1 + i])
+
+        def cut(i=i, mine=mine):
+            halves[i, x] = wv[i, :, pl.ds(pl.multiple_of(x * half, 128), half)]
+            mine.start()
+
+        to_x = [run.remote(wv.at[i, :, pl.ds((1 - x) * half, half)], halves.at[i, x], partner_seq(2))]
+        to_core = [run.remote(
+            halves.at[i, :, :, pl.ds((1 - c) * quarter, quarter)], w_ref.at[i, dp, y, :, c], partner_seq(1))]
+        to_z = [run.remote(w_ref.at[i, dp, y], w_ref.at[i, dp, y], partner_dp(plan, m)) for m in plan.masks]
+        to_y = [run.remote(w_ref.at[i, :, y], w_ref.at[i, :, y], partner_seq(4))]
+        pieces.append((i, [(None, to_x), (cut, to_core), (mine.wait, to_z), (None, to_y)]))
+
+    tick = parts
+    for src, dst, keep, (count, size) in zip(held, outs, keeps, splits):
+        for j in range(count):
+            stages = []
+            for stage in range(plan.hops + 1):
+                copies = []
+                for h in range(2):
+                    cols = pl.ds(j * size + h * (size // 2), size // 2)
+                    if stage == 0:
+                        for m in plan.masks:
+                            copies.append(run.remote(
+                                src.at[:, cols], dst.at[(dp,) + me + (slice(None), cols)], partner_dp(plan, m)))
+                    else:
+                        order = plan.orders[h]
+                        where = tuple(slice(None) if b in order[: stage - 1] else m for b, m in zip(plan.bits, me))
+                        part = dst.at[(slice(None),) + where + (slice(None), cols)]
+                        copies.append(run.remote(part, part, partner_seq(order[stage - 1])))
+                stages.append((keep.wait if stage == 1 and j == 0 else None, copies))
+            pieces.append((tick, stages))
+            tick += 1
+    run.run(pieces, lag)
+
+
+def start(plan, acts, weights, whole, piece, lag, collective_id):
+    groups, columns, width = acts.shape
+    rows = weights[0].shape[0]
+    quarter = width // 4
+    splits, copies = [], 4 * 3 + 3 * (3 + len(plan.masks))
+    for a in whole:
+        count = max(1, a.shape[1] // piece)
+        while a.shape[1] % (256 * count):
+            count -= 1
+        splits.append((count, a.shape[1] // count))
+        copies += count * 2 * (len(plan.masks) + plan.hops)
+    hbm = pl.BlockSpec(memory_space=pl.ANY)
+    outs = pl.pallas_call(
+        functools.partial(start_kernel, plan, splits, lag),
+        out_shape=[
+            jax.ShapeDtypeStruct((2, 2, 2, columns, width), acts.dtype),
+            jax.ShapeDtypeStruct((3,) + plan.lead() + (rows, quarter), acts.dtype),
+        ] + [jax.ShapeDtypeStruct(plan.lead() + a.shape, a.dtype) for a in whole],
+        in_specs=[hbm] * (4 + len(whole)),
+        out_specs=[hbm] * (2 + len(whole)),
+        scratch_shapes=[
+            pltpu.VMEM((columns, width), acts.dtype),
+            pltpu.VMEM((3, rows, width), acts.dtype),
+            pltpu.VMEM((3, 2, rows, width // 2), acts.dtype),
+        ] + [pltpu.VMEM(a.shape, a.dtype) for a in whole] + [
+            pltpu.SemaphoreType.DMA((copies,)),
+            pltpu.SemaphoreType.DMA((copies,)),
+            pltpu.SemaphoreType.DMA((4 + len(whole),)),
+        ],
+        compiler_params=pltpu.CompilerParams(
+            collective_id=collective_id, has_side_effects=True, vmem_limit_bytes=32 << 20),
+    )(acts, *weights, *whole)
+    tokens, projections = outs[0], outs[1]
+    return (
+        tokens.reshape(8, columns, width),
+        projections.reshape(3, width, quarter),
+        [o.reshape(-1, o.shape[-1]) for o in outs[2:]],
+    )
+
+
+def project_kernel(x_ref, w_ref, cos_ref, sin_ref, out_ref, turned_ref):
+    parts, columns, width = x_ref.shape
+    acts = x_ref[...].reshape(parts * columns, width)
+    heads = out_ref.shape[1]
+    for kind in range(3):
+        made = dot(acts, w_ref[kind])
+        for p in range(heads):
+            head = made[:, p * HEAD_DIM : (p + 1) * HEAD_DIM]
+            if kind < 2:
+                head = head * cos_ref[...] + pltpu.roll(head, HEAD_DIM // 2, 1) * sin_ref[...]
+            out_ref[:, p, kind] = head.astype(jnp.bfloat16).reshape(parts, columns, HEAD_DIM)
+    turned_ref[...] = acts.T
+
+
+def project_heads(acts, weights, cosine, sine):
+    owners, columns, width = acts.shape
+    parts = 512 // columns
+    block = parts * columns
+    heads = weights.shape[2] // HEAD_DIM
+    table = pl.BlockSpec((block, HEAD_DIM), lambda i: (i, 0))
+    return pl.pallas_call(
+        project_kernel,
+        grid=(owners // parts,),
+        in_specs=[
+            pl.BlockSpec((parts, columns, width), lambda i: (i, 0, 0)),
+            pl.BlockSpec(weights.shape, lambda i: (0, 0, 0)),
+            table,
+            table,
+        ],
+        out_specs=[
+            pl.BlockSpec((parts, heads, 3, columns, HEAD_DIM), lambda i: (i, 0, 0, 0, 0)),
+            pl.BlockSpec((width, block), lambda i: (0, i)),
+        ],
+        out_shape=[
+            jax.ShapeDtypeStruct((owners, heads, 3, columns, HEAD_DIM), jnp.bfloat16),
+            jax.ShapeDtypeStruct((width, owners * columns), jnp.bfloat16),
+        ],
+        compiler_params=pltpu.CompilerParams(vmem_limit_bytes=56 << 20),
+    )(acts, weights, cosine, sine)
+
+
+def finish_kernel(
+    plan, parts, g_any, t_any, w_any, x_any, gx_any, gain_ref, more_ref,
+    dx_ref, dw_ref, dn_ref,
+    g_ref, t_ref, w_ref, x_ref, gx_ref,
+    made, made_y, sum_y, made_z, sum_z, sides, made_x,
+    acts, acts_c, sum_c, acts_x, sum_x, acts_y,
+    totals, norms, norms_c, norms_sc, norms_x, norms_sx, norms_y, norms_sy, norms_z,
+    send, recv, local,
+):
+    dp, _ = place()
+    y, x, c = own_bit(4), own_bit(2), own_bit(1)
+    loads = [
+        pltpu.make_async_copy(src, dst, local.at[i])
+        for i, (src, dst) in enumerate(
+            ((g_any, g_ref), (w_any, w_ref), (t_any, t_ref), (x_any, x_ref), (gx_any, gx_ref)))
+    ]
+    for load in loads:
+        load.start()
+    greet(plan)
+    for load in loads[:2]:
+        load.wait()
+    run = Copies(send, recv)
+    columns, width = x_ref.shape[1:]
+    quarter = w_ref.shape[2]
+    half = 2 * quarter
+    rows = dw_ref.shape[1]
+    size = columns // parts
+    low = jnp.bfloat16
+
+    def wide(values):
+        return values.astype(jnp.float32)
+
+    def product(i):
+        def go():
+            if i == 0:
+                loads[2].wait()
+            step = 8 * rows
+            for z in range(plan.n_dp):
+                part = dot(t_ref[z * step : (z + 1) * step, :], g_ref[i])
+                made[i, z] = part.astype(low).reshape(2, 2, 2, rows, quarter)
+        return go
+
+    def product_y(i):
+        def go():
+            sum_y[i] = (wide(made[i, :, y]) + wide(made_y[i])).astype(low)
+        return go
+
+    def product_z(i):
+        def go():
+            total = wide(sum_y[i, dp])
+            for n in range(len(plan.masks)):
+                total = total + wide(made_z[i, n])
+            sum_z[i] = total.astype(low)
+        return go
+
+    def product_c(i):
+        def go():
+            sides[i, :, :, pl.ds(pl.multiple_of(c * quarter, 128), quarter)] = sum_z[i, :, c]
+        return go
+
+    def product_x(i):
+        def go():
+            dw_ref[i, :, pl.ds(pl.multiple_of(x * half, 128), half)] = wide(sides[i, x])
+            dw_ref[i, :, pl.ds(pl.multiple_of((1 - x) * half, 128), half)] = wide(made_x[i])
+        return go
+
+    def back(i):
+        def go():
+            pieces = [g_ref[k].reshape(8, columns, quarter)[:, i * size : (i + 1) * size].reshape(8 * size, quarter)
+                      for k in range(3)]
+            step = 512
+            for n in range(width // step):
+                total = sum(dot(pieces[k], w_ref[k, n * step : (n + 1) * step, :], NT) for k in range(3))
+                acts[i, :, :, :, :, n * step : (n + 1) * step] = total.astype(low).reshape(2, 2, 2, size, step)
+        return go
+
+    def back_c(i):
+        def go():
+            sum_c[i] = (wide(acts[i, :, :, c]) + wide(acts_c[i])).astype(low)
+        return go
+
+    def back_x(i):
+        def go():
+            sum_x[i] = (wide(sum_c[i, :, x]) + wide(acts_x[i])).astype(low)
+        return go
+
+    def norm_back(i):
+        def go():
+            if i == 0:
+                for load in loads[3:]:
+                    load.wait()
+                totals[...] = jnp.zeros_like(totals)
+            gain = gain_ref[...]
+            for s in range(2):
+                mine = wide(sum_x[i, s])
+                grad = jnp.where(y == s, mine, wide(acts_y[i]))
+                at = pl.ds(i * size, size)
+                values = x_ref[s, at]
+                centre = values - jnp.mean(values, axis=-1, keepdims=True)
+                spread = lax.rsqrt(jnp.mean(centre * centre, axis=-1, keepdims=True) + EPSILON)
+                normed = centre * spread
+                grown = grad * gain
+                mean_one = jnp.mean(grown, axis=-1, keepdims=True)
+                mean_two = jnp.mean(grown * normed, axis=-1, keepdims=True)
+                dx_ref[s, at] = gx_ref[s, at] + (grown - mean_one - normed * mean_two) * spread
+                totals[0:1] += jnp.sum(grad * normed, axis=0, keepdims=True)
+                totals[1:2] += jnp.sum(grad, axis=0, keepdims=True)
+        return go
+
+    pieces = []
+    for i in range(parts):
+        pieces.append((i if i < 2 else 2 * i - 1, [
+            (back(i), [run.remote(acts.at[i, :, :, 1 - c], acts_c.at[i], partner_seq(1))]),
+            (back_c(i), [run.remote(sum_c.at[i, :, 1 - x], acts_x.at[i], partner_seq(2))]),
+            (back_x(i), [run.remote(sum_x.at[i, 1 - y], acts_y.at[i], partner_seq(4))]),
+            (norm_back(i), []),
+        ]))
+    for i in range(3):
+        pieces.append((2 * i + 2, [
+            (product(i), [run.remote(made.at[i, :, 1 - y], made_y.at[i], partner_seq(4))]),
+            (product_y(i), [
+                run.remote(sum_y.at[i, lax.bitwise_xor(dp, m)], made_z.at[i, n], partner_dp(plan, m))
+                for n, m in enumerate(plan.masks)]),
+            (product_z(i), [run.remote(
+                sum_z.at[i, :, 1 - c], sides.at[i, :, :, pl.ds(c * quarter, quarter)], partner_seq(1))]),
+            (product_c(i), [run.remote(sides.at[i, 1 - x], made_x.at[i], partner_seq(2))]),
+            (product_x(i), []),
+        ]))
+
+    def norms_start():
+        totals[2:4] = more_ref[...]
+        turned = totals[...].T.astype(low)
+        norms[...] = turned.reshape(norms.shape)
+
+    def norms_add(total, kept, got):
+        def go():
+            total[...] = (wide(kept()) + wide(got[...])).astype(low)
+        return go
+
+    def norms_end():
+        total = wide(norms_sy[dp])
+        for n in range(len(plan.masks)):
+            total = total + wide(norms_z[n])
+        dn_ref[...] = total
+
+    end = max(start + 2 * (len(stages) - 1) for start, stages in pieces if len(stages) == 4) + 1
+    pieces.append((end, [
+        (norms_start, [run.remote(norms.at[:, :, :, 1 - c], norms_c, partner_seq(1))]),
+        (norms_add(norms_sc, lambda: norms[:, :, :, c], norms_c), [run.remote(norms_sc.at[:, :, 1 - x], norms_x, partner_seq(2))]),
+        (norms_add(norms_sx, lambda: norms_sc[:, :, x], norms_x), [run.remote(norms_sx.at[:, 1 - y], norms_y, partner_seq(4))]),
+        (norms_add(norms_sy, lambda: norms_sx[:, y], norms_y), [
+            run.remote(norms_sy.at[lax.bitwise_xor(dp, m)], norms_z.at[n], partner_dp(plan, m))
+            for n, m in enumerate(plan.masks)]),
+        (norms_end, []),
+    ]))
+    run.run(pieces, 2)
+
+
+def finish(plan, grads, turned, weights, inputs, grad_first, gain, more, collective_id):
+    _, columns, width = inputs.shape
+    quarter = weights.shape[2]
+    n_dp, masks = plan.n_dp, len(plan.masks)
+    rows = width // (8 * n_dp)
+    parts = 4
+    size = columns // parts
+    low = jnp.bfloat16
+    hbm = pl.BlockSpec(memory_space=pl.ANY)
+    vmem = pl.BlockSpec(memory_space=pltpu.VMEM)
+    copies = 3 * (3 + masks) + 3 * parts + 3 + masks
+    return pl.pallas_call(
+        functools.partial(finish_kernel, plan, parts),
+        out_shape=[
+            jax.ShapeDtypeStruct(inputs.shape, jnp.float32),
+            jax.ShapeDtypeStruct((3, rows, width), jnp.float32),
+            jax.ShapeDtypeStruct((rows, 128), jnp.float32),
+        ],
+        in_specs=[hbm] * 5 + [vmem] * 2,
+        out_specs=[vmem] * 3,
+        scratch_shapes=[
+            pltpu.VMEM(grads.shape, low),
+            pltpu.VMEM(turned.shape, low),
+            pltpu.VMEM(weights.shape, low),
+            pltpu.VMEM(inputs.shape, jnp.float32),
+            pltpu.VMEM(inputs.shape, jnp.float32),
+            pltpu.VMEM((3, n_dp, 2, 2, 2, rows, quarter), low),
+            pltpu.VMEM((3, n_dp, 2, 2, rows, quarter), low),
+            pltpu.VMEM((3, n_dp, 2, 2, rows, quarter), low),
+            pltpu.VMEM((3, masks, 2, 2, rows, quarter), low),
+            pltpu.VMEM((3, 2, 2, rows, quarter), low),
+            pltpu.VMEM((3, 2, rows, 2 * quarter), low),
+            pltpu.VMEM((3, rows, 2 * quarter), low),
+            pltpu.VMEM((parts, 2, 2, 2, size, width), low),
+            pltpu.VMEM((parts, 2, 2, size, width), low),
+            pltpu.VMEM((parts, 2, 2, size, width), low),
+            pltpu.VMEM((parts, 2, size, width), low),
+            pltpu.VMEM((parts, 2, size, width), low),
+            pltpu.VMEM((parts, size, width), low),
+            pltpu.VMEM((128, width), jnp.float32),
+            pltpu.VMEM((n_dp, 2, 2, 2, rows, 128), low),
+            pltpu.VMEM((n_dp, 2, 2, rows, 128), low),
+            pltpu.VMEM((n_dp, 2, 2, rows, 128), low),
+            pltpu.VMEM((n_dp, 2, rows, 128), low),
+            pltpu.VMEM((n_dp, 2, rows, 128), low),
+            pltpu.VMEM((n_dp, rows, 128), low),
+            pltpu.VMEM((n_dp, rows, 128), low),
+            pltpu.VMEM((masks, rows, 128), low),
+            pltpu.SemaphoreType.DMA((copies,)),
+            pltpu.SemaphoreType.DMA((copies,)),
+            pltpu.SemaphoreType.DMA((5,)),
+        ],
+        compiler_params=pltpu.CompilerParams(
+            collective_id=collective_id, has_side_effects=True, vmem_limit_bytes=62 << 20),
+    )(grads, turned, weights, inputs, grad_first, gain, more)
 
 
 def layer_norm(values, gain, offset):
@@ -506,13 +848,14 @@
     length = columns * count
     block = min(512, length)
     per = -(-groups * heads // count)
-    weights = (w_query, w_key, w_value, w_out, w_up, w_down)
-    own_kernels = w_query.shape[0] % 16 == 0
-    if own_kernels:
-        full = gather(plan, weights, 1.6e6, 2, 1)
-    else:
-        full = [lax.all_gather(w, axes, axis=0, tiled=True) for w in weights]
-    full_query, full_key, full_value, full_out, full_up, full_down = full
+    fast = (
+        count == 8
+        and groups == 2
+        and heads % 4 == 0
+        and columns % 64 == 0
+        and 512 % columns == 0
+        and w_query.shape[0] % 16 == 0
+    )
     rank = lax.axis_index("seq")
 
     ids = lax.all_gather(segments, "seq", axis=1, tiled=True)
@@ -530,10 +873,6 @@
     cosine_own = lax.dynamic_slice_in_dim(cosine_all, rank * columns, columns)[None, :, None, :]
     sine_own = lax.dynamic_slice_in_dim(sine_all, rank * columns, columns)[None, :, None, :]
 
-    def turn(values):
-        shaped = values.reshape(groups, columns, heads, HEAD_DIM)
-        return shaped * cosine_own + jnp.roll(shaped, half, axis=-1) * sine_own
-
     def to_pairs(values):
         shaped = values.reshape(groups, columns, heads, HEAD_DIM)
         shaped = jnp.transpose(shaped, (0, 2, 1, 3)).reshape(groups * heads, columns, HEAD_DIM)
@@ -548,11 +887,29 @@
     def swap(values):
         return lax.all_to_all(values, "seq", 0, 0)
 
+    def whole(weight):
+        return lax.all_gather(weight, axes, axis=0, tiled=True)
+
     act_one = lower(layer_norm(inputs, norm1_gain, norm1_bias))
-    query_low = lower(turn(project(act_one, full_query)))
-    key_low = lower(turn(project(act_one, full_key)))
-    value_low = lower(project(act_one, full_value))
-    packed = swap(jnp.stack([to_pairs(query_low), to_pairs(key_low), to_pairs(value_low)], axis=2))
+    if fast:
+        tokens_one, heads_weight, (full_out,) = start(
+            plan, act_one, (w_query, w_key, w_value), (w_out,), 512, 2, 1
+        )
+        packed, turned_one = project_heads(tokens_one, heads_weight, cosine_all, sine_all)
+    else:
+        cosine_own = lax.dynamic_slice_in_dim(cosine_all, rank * columns, columns)[None, :, None, :]
+        sine_own = lax.dynamic_slice_in_dim(sine_all, rank * columns, columns)[None, :, None, :]
+
+        def turn(values):
+            shaped = values.reshape(groups, columns, heads, HEAD_DIM)
+            return shaped * cosine_own + jnp.roll(shaped, half, axis=-1) * sine_own
+
+        full_query, full_key, full_value, full_out = (whole(w) for w in (w_query, w_key, w_value, w_out))
+        query_low = lower(turn(project(act_one, full_query)))
+        key_low = lower(turn(project(act_one, full_key)))
+        value_low = lower(project(act_one, full_value))
+        packed = swap(jnp.stack([to_pairs(query_low), to_pairs(key_low), to_pairs(value_low)], axis=2))
+    full_up, full_down = whole(w_up), whole(w_down)
     mixed_pairs, mixed_t, lse = attend(packed, seg_col, seg_row)
     mixed_low = from_pairs(swap(mixed_pairs))
 
@@ -584,68 +941,56 @@
         turned = turned.reshape(every, -1, width // every, tokens)
         return jnp.transpose(turned, (1, 0, 2, 3)).reshape(-1, width, tokens)
 
-    def reduce_all(pairs, collective_id):
-        out = reduce_products(plan, pairs, width_piece, 2, collective_id)
+    def reduce_all(pairs, collective_id, beside=None):
+        out, *more = reduce_products(plan, pairs, width_piece, 2, collective_id, beside)
         results, at = [], 0
         for left, right in pairs:
             blocks, cols = left.shape[0], right.shape[1] // width_piece
             part = out[at : at + blocks * cols].reshape(blocks, cols, -1, width_piece)
             results.append(jnp.transpose(part, (0, 2, 1, 3)).reshape(-1, right.shape[1]))
             at += blocks * cols
-        return results
-
-    if own_kernels:
-        sums_one = reduce_all(
+        return results + more
+
+    work = AttendBack(
+        8 if fast else 0,
+        packed, swap(to_pairs(grad_mixed)), mixed_t, lse, seg_col, seg_row, cosine_all, sine_all,
+    )
+    gains_two = [gain_two_grad, offset_two_grad]
+    if fast:
+        down_grad, up_grad, out_grad, grads = reduce_all(
             [
                 (left_of(hidden_low), flat(grad_out_low)),
                 (left_of(act_two), flat(grad_upper)),
                 (left_of(mixed_low), flat(grad_attn_low)),
             ],
             2,
+            work,
         )
-
-    def reduce_last(norm_sums):
-        left = left_of(act_one)
-        stacked = jnp.pad(jnp.stack(norm_sums, axis=1), ((0, 0), (0, tokens - len(norm_sums))))
-        return reduce_all(
-            [
-                (left, flat(grad_query_low)),
-                (left, flat(grad_key_low)),
-                (left, flat(grad_value_low)),
-                (lower(stacked)[None], jnp.eye(tokens, width_piece, dtype=jnp.bfloat16)),
-            ],
-            3,
+        grad_input, heads_grad, norm_rows = finish(
+            plan, grads, turned_one, heads_weight, inputs, grad_first, norm1_gain[None],
+            jnp.stack(gains_two), 3,
         )
-
-    grads = attend_back(
-        packed, swap(to_pairs(grad_mixed)), mixed_t, lse, seg_col, seg_row, cosine_all, sine_all
-    )
-    grads = swap(grads)
-    grad_query_low, grad_key_low, grad_value_low = (from_pairs(grads[:, :, i]) for i in range(3))
-
-    grad_act_one = project_back(grad_query_low, full_query) + project_back(grad_key_low, full_key)
-    grad_act_one = grad_act_one + project_back(grad_value_low, full_value)
-    normed_again, norm_one_back = jax.vjp(layer_norm, inputs, norm1_gain, norm1_bias)
-    grad_input_norm, gain_one_grad, offset_one_grad = norm_one_back(grad_act_one)
-    grad_input = grad_first + grad_input_norm
-
-    norm_sums = [gain_one_grad, offset_one_grad, gain_two_grad, offset_two_grad]
-    if own_kernels:
-        first, second = sums_one, reduce_last(norm_sums)
-        down_grad, up_grad, out_grad = first
-        query_grad, key_grad, value_grad, norm_rows = second
+        query_grad, key_grad, value_grad = heads_grad[0], heads_grad[1], heads_grad[2]
         norm_rows = [norm_rows[:, i] for i in range(4)]
     else:
         def spread(values):
             return lax.psum_scatter(values, axes, scatter_dimension=0, tiled=True).astype(jnp.float32)
 
+        grads = attend_back_alone(work).reshape(3, count, columns, per, HEAD_DIM)
+        grads = swap(jnp.transpose(grads, (1, 3, 0, 2, 4)))
+        grad_query_low, grad_key_low, grad_value_low = (from_pairs(grads[:, :, i]) for i in range(3))
+        grad_act_one = project_back(grad_query_low, full_query) + project_back(grad_key_low, full_key)
+        grad_act_one = grad_act_one + project_back(grad_value_low, full_value)
+        normed_again, norm_one_back = jax.vjp(layer_norm, inputs, norm1_gain, norm1_bias)
+        grad_input_norm, gain_one_grad, offset_one_grad = norm_one_back(grad_act_one)
+        grad_input = grad_first + grad_input_norm
         down_grad = spread(lower(outer_sum(hidden_low, grad_out_low)))
         up_grad = spread(lower(outer_sum(act_two, grad_upper)))
         out_grad = spread(lower(outer_sum(mixed_low, grad_attn_low)))
         query_grad = spread(lower(outer_sum(act_one, grad_query_low)))
         key_grad = spread(lower(outer_sum(act_one, grad_key_low)))
         value_grad = spread(lower(outer_sum(act_one, grad_value_low)))
-        norm_rows = [spread(v) for v in norm_sums]
+        norm_rows = [spread(v) for v in [gain_one_grad, offset_one_grad] + gains_two]
 
     return (
         output,

time: 985 us -> 753 us (0.76)
  Pallas kernels: 599 us -> 479 us
  local copies, waits for them, and re-layouts: 103 us -> 51.1 us
  blocking collectives: 57.7 us -> 10.5 us
  waiting for transfers between devices: 34.7 us -> 75.6 us
  matrix products: 116 us -> 82.1 us
  other arithmetic: 43.5 us -> 21.6 us
  between operations: 1.69 us -> 14.8 us
    pallas_call x4, Pallas kernels: 575 us -> 454 us  [the longest x1 195 us: reduce_products(): pl.pallas_call(functools.partial(reduce_kernel, plan, jobs, count, lag, b...]
    all_gather x1, blocking collectives: 57.7 us -> 10.5 us  [shards(): ids = lax.all_gather(segments, 'seq', axis=1, tiled=True)]
    all_gather x0 -> x2, waiting for transfers between devices: none -> 43.1 us  [whole(): return lax.all_gather(weight, axes, axis=0, tiled=True)]
    dot_general x6 -> x3, matrix products: 59.6 us -> 41.1 us  [project(): jnp.einsum('gcd,de->gce', acts, weight, preferred_element_type=jnp.float32)]
    dot_general x6 -> x3, matrix products: 56.1 us -> 41 us  [project_back(): jnp.einsum('gce,de->gcd', grads, weight, preferred_element_type=jnp.float32)]
    reshape x2 -> x0, local copies, waits for them, and re-layouts: 13.3 us -> none  [gather(): return [o.reshape(-1, o.shape[-1]) for o in outs]]
    all_to_all x4 -> x2, waiting for transfers between devices: 34.7 us -> 31.1 us  [swap(): return lax.all_to_all(values, 'seq', 0, 0)]
  transfers between devices with their start and end apart: 4 -> 4, of which waited for: 2 -> 2; matrix products, arithmetic and copies ran while one was open for 7% -> 11% of each run, Pallas kernels for 21% -> 26%
where the time goes in v2:
time: 753 us; the launch traced here: 744 us
  Pallas kernels  479 us (64%)
  matrix products  82.1 us (11%)
  waiting for transfers between devices  75.6 us (10%)
  local copies, waits for them, and re-layouts  51.1 us (7%)
  other arithmetic  21.6 us (3%)
  between operations  14.8 us (2%)
  blocking collectives  10.5 us (1%)
  starting transfers between devices  9.06 us (1%)
    pallas_call x1, Pallas kernels, reduce_products(): pl.pallas_call(functools.partial(reduce_kernel, plan, jobs, count, lag, b...  195 us
    pallas_call x1, Pallas kernels, start(): pl.pallas_call(functools.partial(start_kernel, plan, splits, lag), out_sh...  154 us
    pallas_call x1, Pallas kernels, finish(): pl.pallas_call(functools.partial(finish_kernel, plan, parts), out_shape=[...  91 us
    all_gather x2, waiting for transfers between devices, whole(): return lax.all_gather(weight, axes, axis=0, tiled=True)  43.1 us
    dot_general x3, matrix products, project(): jnp.einsum('gcd,de->gce', acts, weight, preferred_element_type=jnp.float32)  41.1 us
    dot_general x3, matrix products, project_back(): jnp.einsum('gce,de->gcd', grads, weight, preferred_element_type=jnp.float32)  41 us
    all_to_all x2, waiting for transfers between devices, swap(): return lax.all_to_all(values, 'seq', 0, 0)  31.1 us
    pallas_call x1, Pallas kernels, attend(): pl.pallas_call(functools.partial(attend_kernel, block, parts), grid=(per,...  24.6 us
  transfers between devices with their start and end apart: 4, of which 2 were waited for; matrix products, arithmetic and copies ran while one was open for 11% of the time, Pallas kernels for 26%

profile of v2, /device:TPU:0, one launch (start us, length us, event | category | flops | bytes accessed | tf_op | source)
XLA Modules:
  0.0 743.8 jit_solution(12850439643440077240)
XLA Ops:
  8.7 10.5 %all_gather.9 = s32[2,2048]{1,0:T(2,128)S(1)} all-gather(s32[2,256]{1,0:T(2,128)} %param.14), channel_id=1, replica_groups=mesh['dp'=4,'seq'=8] {'seq'}, dimensions={1}, use_global_device_ids=true | all-gather | bytes 18432 | tf_op jit(solution)/shard_map/all_gather | solution.py:861
  24.4 154.1 %shard_map.220 = (bf16[2,2,2,256,1536]{4,3,2,1,0:T(8,128)(2,1)S(1)}, bf16[3,4,2,2,2,48,384]{6,5,4,3,2,1,0:T(8,128)(2,1)S(1)}, bf16[4,2,2,2,48,1536]{5,4,3,2,1,0:T(8,128)(2,1)S(1)}) custom-call(bf16[2,256,1536]{2,1,0:T(8,128)(2,1)S(1)} %add_convert_fusion.2.h_ref, bf16[48,1536]{1,0:T(8,128)(2,1)S(1)} %copy-done.3, bf16[48,1536]{1,0:T(8,128)(2,1)S(1)} %copy-done.4, ...), custom_call_target="tpu_custom_call" | custom-call | tf_op jit(solution)/shard_map/pallas_call | solution.py:517
  181.2 3.9 fusion.16
  187.0 14.4 %shard_map.221 = (bf16[8,3,3,256,128]{4,3,2,1,0:T(8,128)(2,1)}, bf16[1536,2048]{1,0:T(8,128)(2,1)}) custom-call(bf16[8,256,1536]{2,1,0:T(8,128)(2,1)} %bitcast.99, bf16[3,1536,384]{2,1,0:T(8,128)(2,1)} %bitcast.93, f32[2048,128]{1,0:T(8,128)} %get-tuple-element.61.cos_ref.refs_14_, f32[2048,128]{1,0:T(8,128)} %get-tuple-element.62.sin_ref.refs_15_), custom_call_target="tpu_custom_call" | custom-call | tf_op jit(solution)/shard_map/pallas_call | solution.py:565
  203.4 24.6 %shard_map.222 = (bf16[8,3,256,128]{3,2,1,0:T(8,128)(2,1)}, f32[3,4,128,512]{3,2,1,0:T(8,128)}, f32[3,4,512]{2,1,0:T(4,128)}) custom-call(bf16[8,3,3,256,128]{4,3,2,1,0:T(8,128)(2,1)} %get-tuple-element.27.q_ref.k_ref.v_ref.refs_6_.refs_7_.refs_8_, bf16[8,3,3,256,128]{4,3,2,1,0:T(8,128)(2,1)} %get-tuple-element.27.q_ref.k_ref.v_ref.refs_6_.refs_7_.refs_8_, ...), custom_call_target="tpu_custom_call" | custom-call | tf_op jit(solution)/shard_map/pallas_call | solution.py:134
  228.0 4.5 all-to-all-start
  233.1 3.2 convert_element_type.24
  236.4 31.1 %all-to-all-done = bf16[8,3,256,128]{3,2,1,0:T(8,128)(2,1)} async-done(((bf16[8,3,256,128]{3,2,1,0:T(8,128)(2,1)}), bf16[8,3,256,128]{3,2,1,0:T(8,128)(2,1)}, u32[]{:S(2)}, u32[]{:S(2)}) %all-to-all-start) | async-done | bytes 1572896 | tf_op jit(solution)/shard_map/all_to_all | solution.py:888
  270.1 5.3 fusion.21
  278.7 3.7 copy.37
  283.9 18.9 %multiply_convert_fusion = (bf16[2,256,6144]{2,1,0:T(8,128)(2,1)}, f32[2,256,6144]{2,1,0:T(8,128)}) fusion(bf16[2,256,1536]{2,1,0:T(8,128)(2,1)S(1)} %add_convert_fusion.1, bf16[1536,6144]{1,0:T(8,128)(2,1)} %all-gather.3.cloned.1.call-done), kind=kOutput, calls=%fused_computation.10 | convolution fusion | flops 9679405056 | bytes 39321600 | tf_op jit(solution)/shard_map/gcd,de->gce/dot_general | solution.py:816
  302.8 43.1 %all-gather.5.cloned.1.call-done = bf16[6144,1536]{1,0:T(8,128)(2,1)} async-done(((bf16[192,1536]{1,0:T(8,128)(2,1)}), bf16[6144,1536]{1,0:T(8,128)(2,1)}) %all-gather.5.cloned.1.call-update) | async-done | bytes 18874384 | tf_op jit(solution)/shard_map/all_gather | solution.py:891
  345.9 19.9 %add_convert_fusion = bf16[2,256,6144]{2,1,0:T(8,128)(2,1)} fusion(f32[2,256,6144]{2,1,0:T(8,128)} %get-tuple-element.58, bf16[2,256,1536]{2,1,0:T(8,128)(2,1)} %convert_element_type.24, bf16[6144,1536]{1,0:T(8,128)(2,1)} %all-gather.5.cloned.1.call-done), kind=kOutput, calls=%fused_computation.9 | convolution fusion | flops 9704570880 | bytes 39321600 | tf_op jit(solution)/shard_map/gce,de->gcd/dot_general | solution.py:820
  365.8 17.4 %multiply_reduce_fusion.1 = (f32[2,256]{1,0:T(2,128)S(1)}, f32[2,256,1536]{2,1,0:T(8,128)}) fusion(f32[2,256,1536]{2,1,0:T(8,128)S(1)} %copy-done.9, f32[1536]{0:T(1024)S(1)} %copy-done.15, f32[2,256]{1,0:T(2,128)S(1)} %broadcast_multiply_fusion, bf16[2,256,6144]{2,1,0:T(8,128)(2,1)} %add_convert_fusion, bf16[1536,6144]{1,0:T(8,128)(2,1)} %all-gather.3.cloned.1.call-done), kind=kOutput, calls=%fused_computation.18 | convolution fusion | flops 9666822144 | bytes 31467520 | tf_op jit(solution)/shard_map/gce,de->gcd/dot_general | solution.py:820
  383.2 3.0 multiply_reduce_fusion
  386.3 4.7 fusion.19
  392.2 3.7 convolution_convert_fusion
  401.1 4.5 all-to-all-start.1
  405.5 8.5 %copy.34 = bf16[512,6144]{0,1:T(8,128)(2,1)} copy(bf16[512,6144]{1,0:T(8,128)(2,1)} %bitcast.107) | data formatting | bytes 12582912 | tf_op jit(solution)/shard_map/reshape | solution.py:936
  414.1 6.0 copy.35
  420.7 16.8 %fusion.10 = f32[2,256,1536]{2,1,0:T(8,128)} fusion(f32[2,256,1536]{2,1,0:T(8,128)S(1)} %copy-done.9, bf16[2,256,6144]{2,1,0:T(8,128)(2,1)} %get-tuple-element.57, bf16[6144,1536]{1,0:T(8,128)(2,1)} %all-gather.5.cloned.1.call-done), kind=kOutput, calls=%fused_computation.14 | convolution fusion | flops 9664462848 | bytes 31457280 | tf_op jit(solution)/shard_map/gcd,de->gce/dot_general | solution.py:816
  437.5 194.9 %shard_map.223 = (f32[27,48,512]{2,1,0:T(8,128)}, bf16[3,2048,384]{2,1,0:T(8,128)(2,1)}) custom-call(bf16[4,1536,512]{2,1,0:T(8,128)(2,1)} %bitcast.101, bf16[1,1536,512]{2,1,0:T(8,128)(2,1)} %bitcast.103, bf16[1,1536,512]{2,1,0:T(8,128)(2,1)} %bitcast.104, bf16[512,1536]{1,0:T(8,128)(2,1)} %bitcast.105, bf16[512,6144]{1,0:T(8,128)(2,1)} %bitcast.113, ...), custom_call_target="tpu_custom_call" | custom-call | tf_op jit(solution)/shard_map/pallas_call | solution.py:382
  632.5 3.0 fusion.20
  636.4 91.0 %shard_map.224 = (f32[2,256,1536]{2,1,0:T(8,128)}, f32[3,48,1536]{2,1,0:T(8,128)}, f32[48,128]{1,0:T(8,128)}) custom-call(bf16[3,2048,384]{2,1,0:T(8,128)(2,1)} %get-tuple-element.32.g_any, bf16[1536,2048]{1,0:T(8,128)(2,1)} %get-tuple-element.33.t_any, bf16[3,1536,384]{2,1,0:T(8,128)(2,1)} %bitcast.94, f32[2,256,1536]{2,1,0:T(8,128)} %x_any.1, ...), custom_call_target="tpu_custom_call" | custom-call | tf_op jit(solution)/shard_map/pallas_call | solution.py:755
  (86 shorter events, 38.2 us)
Async XLA Ops:
  7.2 15.4 %copy-start.7 = (f32[2,256,1536]{2,1,0:T(8,128)S(1)}, f32[2,256,1536]{2,1,0:T(8,128)}, u32[]{:S(2)}) copy-start(f32[2,256,1536]{2,1,0:T(8,128)} %x_any.1) | copy-start | bytes 9437188
  7.2 276.7 %all-gather.3.cloned.1.call-start = ((), (), s32[]{:S(2)}) async-start(), calls=%async_computation.2 | async-start | bytes 19464192 | tf_op jit(solution)/shard_map/all_gather | solution.py:891
  7.9 338.0 %all-gather.5.cloned.1.call-start = ((), (), s32[]{:S(2)}) async-start(), calls=%async_computation.3 | async-start | bytes 19464192 | tf_op jit(solution)/shard_map/all_gather | solution.py:891
  22.6 0.7 copy-start.16
  22.6 0.8 copy-start.17
  23.3 0.9 copy-start.3
  23.3 1.0 copy-start.4
  23.3 1.0 copy-start.5
  23.3 1.1 copy-start.6
  178.5 2.6 copy-start.2
  181.2 5.8 copy-start
  181.2 5.8 copy-start.1
  187.0 14.4 %copy-start.10 = (s32[3,2048,1]{2,1,0:T(8,128)S(1)}, s32[3,2048,1]{2,1,0:T(8,128)}, u32[]{:S(2)}) copy-start(s32[3,2048,1]{2,1,0:T(8,128)} %copy.30) | copy-start | bytes 73732
  228.0 39.5 %all-to-all-start = ((bf16[8,3,256,128]{3,2,1,0:T(8,128)(2,1)}), bf16[8,3,256,128]{3,2,1,0:T(8,128)(2,1)}, u32[]{:S(2)}, u32[]{:S(2)}) async-start(bf16[8,3,256,128]{3,2,1,0:T(8,128)(2,1)} %get-tuple-element.28), calls=%async_computation | async-start | bytes 3145728 | tf_op jit(solution)/shard_map/all_to_all | solution.py:888
  275.4 1.7 copy-start.8
  275.5 0.8 copy-start.18
  345.9 19.9 %copy-start.9 = (f32[2,256,1536]{2,1,0:T(8,128)S(1)}, f32[2,256,1536]{2,1,0:T(8,128)}, u32[]{:S(2)}) copy-start(f32[2,256,1536]{2,1,0:T(8,128)} %copy-done.8) | copy-start | bytes 9437188
  383.2 8.9 %slice-start = ((s8[4718592]{0:T(1024)(128)(4,1)}), s8[4194304]{0:T(1024)(128)(4,1)S(1)}, s32[]{:S(2)}) async-start(s8[4718592]{0:T(1024)(128)(4,1)} %bitcast.96), calls=%async_computation.4 | async-start | bytes 8388608
  386.3 5.9 slice-start.1
  391.0 1.2 copy-start.11
  401.1 36.5 %all-to-all-start.1 = ((bf16[8,3,256,128]{3,2,1,0:T(8,128)(2,1)}), bf16[8,3,256,128]{3,2,1,0:T(8,128)(2,1)}, u32[]{:S(2)}, u32[]{:S(2)}) async-start(bf16[8,3,256,128]{3,2,1,0:T(8,128)(2,1)} %bitcast.108), calls=%async_computation.1 | async-start | bytes 3145728 | tf_op jit(solution)/shard_map/all_to_all | solution.py:888
  727.4 3.7 copy-start.13
  727.4 4.6 copy-start.14
  731.0 3.8 copy-start.12
  (1 other events, 0.7 us)
Sparse Core Ops, SparseCore 0:
  10.9 193.8 all-gather.2
  207.7 138.1 all-gather.4

commit v3 on v2

--- a/solution.py
+++ b/solution.py
@@ -3,6 +3,7 @@
 
 import jax
 import jax.numpy as jnp
+import numpy as np
 from jax import lax
 from jax.experimental import pallas as pl
 from jax.experimental.pallas import tpu as pltpu
@@ -32,45 +33,6 @@
     return (same & (key_at <= query_at)) | (key_at == query_at)
 
 
-def attend_kernel(block, parts, q_ref, k_ref, v_ref, col_ref, row_ref, o_ref, ot_ref, lse_ref, vt_ref):
-    step = pl.program_id(1)
-
-    @pl.when(step == 0)
-    def _():
-        whole = v_ref[...].reshape(-1, HEAD_DIM)
-        vt_ref[...] = whole.T
-
-    query = q_ref[pl.ds(step * parts, parts)].reshape(block, HEAD_DIM)
-    query_row = row_ref[0, pl.ds(step, 1), :]
-    unit = LOG2E / math.sqrt(HEAD_DIM)
-
-    def visit(j, carry, diagonal):
-        top, total, mixed = carry
-        key = k_ref[pl.ds(j * parts, parts)].reshape(block, HEAD_DIM)
-        at = pl.multiple_of(j * block, block)
-        key_col = col_ref[0, pl.ds(at, block), :]
-        scores = dot(key, query, NT) * unit
-        scores = jnp.where(allowed_pairs(key_col, query_row, diagonal), scores, MASKED)
-        above = jnp.maximum(top, jnp.max(scores, axis=0, keepdims=True))
-        expo = jnp.exp2(scores - above)
-        fade = jnp.exp2(top - above)
-        total = total * fade + jnp.sum(expo, axis=0, keepdims=True)
-        mixed = mixed * fade + dot(vt_ref[:, pl.ds(at, block)], expo.astype(jnp.bfloat16))
-        return above, total, mixed
-
-    start = (
-        jnp.full((1, block), MASKED, jnp.float32),
-        jnp.zeros((1, block), jnp.float32),
-        jnp.zeros((HEAD_DIM, block), jnp.float32),
-    )
-    carry = lax.fori_loop(0, step, lambda j, c: visit(j, c, False), start)
-    top, total, mixed = visit(step, carry, True)
-    mixed = mixed / total
-    ot_ref[0, 0] = mixed
-    lse_ref[0, pl.ds(step, 1), :] = top + jnp.log2(total)
-    o_ref[...] = mixed.T.astype(jnp.bfloat16).reshape(o_ref.shape)
-
-
 def attend_back_step(
     block, parts, step, last, q_ref, k_ref, v_ref, g_ref, ot_ref, lse_ref, col_ref, row_ref, cos_ref, sin_ref,
     out_ref, kt_ref, dk_ref, dv_ref,
@@ -85,7 +47,7 @@
 
     query = q_ref[pl.ds(step * parts, parts)].reshape(block, HEAD_DIM)
     grad = g_ref[pl.ds(step * parts, parts)].reshape(block, HEAD_DIM)
-    query_row = row_ref[0, pl.ds(step, 1), :]
+    query_row = row_ref[pl.ds(step, 1), :]
     lse = lse_ref[0, pl.ds(step, 1), :]
     delta = jnp.sum(ot_ref[0, 0] * grad.astype(jnp.float32).T, axis=0, keepdims=True)
     unit = LOG2E * scale
@@ -94,7 +56,7 @@
         at = pl.multiple_of(j * block, block)
         key = k_ref[pl.ds(j * parts, parts)].reshape(block, HEAD_DIM)
         value = v_ref[pl.ds(j * parts, parts)].reshape(block, HEAD_DIM)
-        key_col = col_ref[0, pl.ds(at, block), :]
+        key_col = col_ref[pl.ds(at, block), :]
         scores = dot(key, query, NT) * unit - lse
         probs = jnp.where(allowed_pairs(key_col, query_row, diagonal), jnp.exp2(scores), 0.0)
         grad_probs = dot(value, grad, NT)
@@ -122,54 +84,20 @@
         out_ref[2] = dv_ref[...].astype(jnp.bfloat16)
 
 
-def pair_spec(count, which, columns):
-    return pl.BlockSpec((count, None, None, columns, HEAD_DIM), lambda p, i: (0, p, which, 0, 0))
-
-
-def attend(packed, seg_col, seg_row):
-    count, per, _, columns, _ = packed.shape
-    length = count * columns
-    block = seg_row.shape[2]
-    steps, parts = length // block, block // columns
-    return pl.pallas_call(
-        functools.partial(attend_kernel, block, parts),
-        grid=(per, steps),
-        in_specs=[
-            pair_spec(count, 0, columns),
-            pair_spec(count, 1, columns),
-            pair_spec(count, 2, columns),
-            pl.BlockSpec((1, length, 1), lambda p, i: (p, 0, 0)),
-            pl.BlockSpec((1, steps, block), lambda p, i: (p, 0, 0)),
-        ],
-        out_specs=[
-            pl.BlockSpec((parts, None, columns, HEAD_DIM), lambda p, i: (i, p, 0, 0)),
-            pl.BlockSpec((1, 1, HEAD_DIM, block), lambda p, i: (p, i, 0, 0)),
-            pl.BlockSpec((1, steps, block), lambda p, i: (p, 0, 0)),
-        ],
-        out_shape=[
-            jax.ShapeDtypeStruct((count, per, columns, HEAD_DIM), jnp.bfloat16),
-            jax.ShapeDtypeStruct((per, steps, HEAD_DIM, block), jnp.float32),
-            jax.ShapeDtypeStruct((per, steps, block), jnp.float32),
-        ],
-        scratch_shapes=[pltpu.VMEM((HEAD_DIM, length), jnp.bfloat16)],
-        compiler_params=pltpu.CompilerParams(vmem_limit_bytes=56 << 20),
-    )(packed, packed, packed, seg_col, seg_row)
-
-
 class AttendBack:
     def __init__(self, first, packed, grads, mixed_t, lse, seg_col, seg_row, cosine, sine):
         count, per, _, columns, _ = packed.shape
         length = count * columns
-        self.block = seg_row.shape[2]
+        self.block = seg_row.shape[1]
         self.steps, self.parts = length // self.block, self.block // columns
-        self.first, self.ticks = first, per * self.steps
+        self.first, self.count, self.ticks = first, per * self.steps, first + per * self.steps
         self.operands = (packed, packed, packed, grads, mixed_t, lse, seg_col, seg_row, cosine, sine)
 
         def pair(t):
-            return lax.div(jnp.clip(t - first, 0, self.ticks - 1), self.steps)
+            return lax.div(jnp.clip(t - first, 0, self.count - 1), self.steps)
 
         def step(t):
-            return lax.rem(jnp.clip(t - first, 0, self.ticks - 1), self.steps)
+            return lax.rem(jnp.clip(t - first, 0, self.count - 1), self.steps)
 
         def whole(which):
             return pl.BlockSpec((count, None, None, columns, HEAD_DIM), lambda t: (0, pair(t), which, 0, 0))
@@ -183,8 +111,8 @@
             pl.BlockSpec((count, None, columns, HEAD_DIM), lambda t: (0, pair(t), 0, 0)),
             pl.BlockSpec((1, 1, HEAD_DIM, self.block), lambda t: (pair(t), step(t), 0, 0)),
             rows,
-            pl.BlockSpec((1, length, 1), lambda t: (pair(t), 0, 0)),
-            rows,
+            pl.BlockSpec((length, 1), lambda t: (0, 0)),
+            pl.BlockSpec((self.steps, self.block), lambda t: (0, 0)),
             table,
             table,
         ]
@@ -197,25 +125,10 @@
         ]
 
     def run(self, tick, refs):
-        @pl.when((tick >= self.first) & (tick < self.first + self.ticks))
+        @pl.when((tick >= self.first) & (tick < self.ticks))
         def _():
             step = lax.rem(tick - self.first, self.steps)
             attend_back_step(self.block, self.parts, step, self.steps - 1, *refs)
-
-
-def attend_back_alone(work):
-    def kernel(*refs):
-        work.run(pl.program_id(0), refs)
-
-    return pl.pallas_call(
-        kernel,
-        grid=(work.first + work.ticks,),
-        in_specs=work.in_specs,
-        out_specs=work.out_specs,
-        out_shape=work.out_shapes,
-        scratch_shapes=work.scratch,
-        compiler_params=pltpu.CompilerParams(vmem_limit_bytes=56 << 20),
-    )(*work.operands)[0]
 
 
 MESH = pl.DeviceIdType.MESH
@@ -256,17 +169,18 @@
     return lax.bitwise_and(lax.div(place()[1], bit), 1)
 
 
-def greet(plan):
+def greet(plan, everyone=False):
     barrier = pltpu.get_barrier_semaphore()
-    others = [partner_dp(plan, m) for m in plan.masks] + [partner_seq(b) for b in plan.bits]
+    others = [partner_dp(plan, m) for m in plan.masks]
+    others += [partner_seq(m) for m in (range(1, plan.n_seq) if everyone else plan.bits)]
     for other in others:
         pl.semaphore_signal(barrier, inc=1, device_id=other, device_id_type=MESH)
     pl.semaphore_wait(barrier, len(others))
 
 
-def reduce_kernel(plan, jobs, count, lag, beside, *refs):
-    k = len(jobs)
-    lefts, rights, refs = refs[:k], refs[k : 2 * k], refs[2 * k :]
+def reduce_kernel(plan, jobs, first, count, lag, beside, *refs):
+    k, given = len(jobs), sum(job[3] for job in jobs)
+    lefts, rights, refs = iter(refs[:given]), refs[given : given + k], refs[given + k :]
     more = [0, 0, 0] if beside is None else [len(beside.in_specs), len(beside.out_specs), len(beside.scratch)]
     extra, refs = refs[: more[0]], refs[more[0] :]
     out_ref, extra = refs[0], extra + refs[1 : 1 + more[1]]
@@ -285,24 +199,25 @@
 
     @pl.when(tick == 0)
     def _():
-        greet(plan)
+        greet(plan, getattr(beside, "everyone", False))
 
     def at_bit(h, stage, value):
         left = [b for b in plan.bits if b not in orders[h][:stage]]
         return (slice(None),) + tuple(value if b == orders[h][stage] else slice(None) for b in left)
 
     def copies(h, stage, slot):
+        kept = lax.rem(slot, lag)
         if stage < hops:
             bit = orders[h][stage]
             at = h * (hops + len(plan.masks)) + stage
             return [pltpu.make_async_remote_copy(
-                sums[h][stage].at[(slot,) + at_bit(h, stage, 1 - own_bit(bit))], got[h][stage].at[slot],
+                sums[h][stage].at[(kept,) + at_bit(h, stage, 1 - own_bit(bit))], got[h][stage].at[slot],
                 send.at[slot, at], recv.at[slot, at], device_id=partner_seq(bit), device_id_type=MESH)]
         out = []
         for n, mask in enumerate(plan.masks):
             at = h * (hops + len(plan.masks)) + hops + n
             out.append(pltpu.make_async_remote_copy(
-                sums[h][hops].at[slot, lax.bitwise_xor(dp, mask)], got[h][hops].at[slot, n],
+                sums[h][hops].at[kept, lax.bitwise_xor(dp, mask)], got[h][hops].at[slot, n],
                 send.at[slot, at], recv.at[slot, at], device_id=partner_dp(plan, mask), device_id_type=MESH))
         return out
 
@@ -310,39 +225,47 @@
         return values.astype(jnp.float32)
 
     for stage in reversed(range(1, hops + 2)):
-        u = tick - lag * stage
+        u = tick - first - lag * stage
 
         @pl.when((u >= 0) & (u < count))
         def _(stage=stage, u=u):
-            slot = lax.rem(u, slots)
+            slot, kept = lax.rem(u, slots), lax.rem(u, lag)
             for h in range(2):
                 for copy in copies(h, stage - 1, slot):
                     copy.wait()
                 if stage <= hops:
-                    mine = (slot,) + at_bit(h, stage - 1, own_bit(orders[h][stage - 1]))
+                    mine = (kept,) + at_bit(h, stage - 1, own_bit(orders[h][stage - 1]))
                     total = wide(sums[h][stage - 1][mine]) + wide(got[h][stage - 1][slot])
-                    sums[h][stage][slot] = total.astype(jnp.bfloat16)
+                    sums[h][stage][kept] = total.astype(jnp.bfloat16)
                     for copy in copies(h, stage, slot):
                         copy.start()
                 else:
-                    total = wide(sums[h][hops][slot, dp])
+                    total = wide(sums[h][hops][kept, dp])
                     for n in range(len(plan.masks)):
                         total = total + wide(got[h][hops][slot, n])
                     out_ref[0, :, h * half : (h + 1) * half] = total
 
-    for (start, stop, cols), left, right in zip(jobs, lefts, rights):
-
-        @pl.when((tick >= start) & (tick < stop))
-        def _(start=start, cols=cols, left=left, right=right):
-            slot = lax.rem(tick, slots)
-            which = lax.div(tick - start, cols)
-            step = rows * plan.n_seq
+    for (start, stop, cols, has_left), right in zip(jobs, rights):
+        if has_left:
+            left = next(lefts)
+
+            def left_rows(which, z, left=left):
+                step = rows * plan.n_seq
+                return left[which, z * step : (z + 1) * step, :]
+
+        else:
+            left_rows = functools.partial(beside.left, extra)
+
+        @pl.when((tick >= first + start) & (tick < first + stop))
+        def _(start=start, cols=cols, left_rows=left_rows, right=right):
+            u = tick - first
+            slot, kept = lax.rem(u, slots), lax.rem(u, lag)
+            which = lax.div(u - start, cols)
             for z in range(plan.n_dp):
-                part = lax.dot_general(left[which, z * step : (z + 1) * step, :], right[...],
-                    (((1,), (0,)), ((), ())), preferred_element_type=jnp.float32).astype(jnp.bfloat16)
+                part = dot(left_rows(which, z), right[...]).astype(jnp.bfloat16)
                 for h in range(2):
                     piece = part[:, h * half : (h + 1) * half]
-                    sums[h][0][slot, z] = piece.reshape(plan.lead()[1:] + (rows, half))
+                    sums[h][0][kept, z] = piece.reshape(plan.lead()[1:] + (rows, half))
             for h in range(2):
                 for copy in copies(h, 0, slot):
                     copy.start()
@@ -351,37 +274,38 @@
         beside.run(tick, extra)
 
 
-def reduce_products(plan, pairs, width, lag, collective_id, beside=None):
+def reduce_products(plan, pairs, rows, width, lag, collective_id, beside=None, first=0):
     jobs, start = [], 0
     left_specs, right_specs = [], []
     for left, right in pairs:
         cols = right.shape[1] // width
-        stop = start + left.shape[0] * cols
-        jobs.append((start, stop, cols))
-        left_specs.append(pl.BlockSpec(left.shape, lambda t: (0, 0, 0)))
+        blocks = left if isinstance(left, int) else left.shape[0]
+        stop = start + blocks * cols
+        jobs.append((start, stop, cols, left is not blocks))
+        if left is not blocks:
+            left_specs.append(pl.BlockSpec(left.shape, lambda t: (0, 0, 0)))
         right_specs.append(pl.BlockSpec(
             (right.shape[0], width),
-            functools.partial(lambda t, start, stop, cols: (0, lax.rem(jnp.clip(t, start, stop - 1) - start, cols)),
+            functools.partial(lambda t, start, stop, cols: (0, lax.rem(jnp.clip(t - first, start, stop - 1) - start, cols)),
                 start=start, stop=stop, cols=cols)))
         start = stop
     count = start
-    rows = pairs[0][0].shape[1] // (plan.n_dp * plan.n_seq)
     half = width // 2
     slots, hops = 2 * lag, plan.hops
     tail = lag * (hops + 1)
-    sums = [pltpu.VMEM((slots, plan.n_dp) + (2,) * (hops - s) + (rows, half), jnp.bfloat16) for s in range(hops + 1)]
+    sums = [pltpu.VMEM((lag, plan.n_dp) + (2,) * (hops - s) + (rows, half), jnp.bfloat16) for s in range(hops + 1)]
     got = [pltpu.VMEM((slots, plan.n_dp) + (2,) * (hops - 1 - s) + (rows, half), jnp.bfloat16) for s in range(hops)]
     got.append(pltpu.VMEM((slots, len(plan.masks), rows, half), jnp.bfloat16))
     each = 2 * (hops + len(plan.masks))
-    out_specs = [pl.BlockSpec((1, rows, width), lambda t: (jnp.maximum(t - tail, 0), 0, 0))]
+    out_specs = [pl.BlockSpec((1, rows, width), lambda t: (jnp.clip(t - first - tail, 0, count - 1), 0, 0))]
     out_shapes = [jax.ShapeDtypeStruct((count, rows, width), jnp.float32)]
     more_in, more_scratch, more_operands = [], [], []
     if beside is not None:
         more_in, more_scratch, more_operands = beside.in_specs, beside.scratch, beside.operands
         out_specs, out_shapes = out_specs + beside.out_specs, out_shapes + beside.out_shapes
     return pl.pallas_call(
-        functools.partial(reduce_kernel, plan, jobs, count, lag, beside),
-        grid=(count + tail,),
+        functools.partial(reduce_kernel, plan, jobs, first, count, lag, beside),
+        grid=(max(first + count + tail, 0 if beside is None else beside.ticks),),
         in_specs=left_specs + right_specs + more_in,
         out_specs=out_specs,
         out_shape=out_shapes,
@@ -391,7 +315,7 @@
         ],
         compiler_params=pltpu.CompilerParams(
             collective_id=collective_id, has_side_effects=True, vmem_limit_bytes=60 << 20),
-    )(*[p[0] for p in pairs], *[p[1] for p in pairs], *more_operands)
+    )(*[p[0] for p in pairs if not isinstance(p[0], int)], *[p[1] for p in pairs], *more_operands)
 
 
 class Copies:
@@ -427,14 +351,14 @@
 
 
 def start_kernel(
-    plan, splits, lag, h_ref, q_ref, k_ref, v_ref, *refs,
+    plan, splits, lag, h_ref, s_ref, q_ref, k_ref, v_ref, *refs,
 ):
     n = len(splits)
     ins, refs = refs[:n], refs[n:]
-    hs_ref, w_ref, outs = refs[0], refs[1], refs[2 : 2 + n]
-    hv, wv, halves = refs[2 + n : 5 + n]
-    held = refs[5 + n : 5 + 2 * n]
-    send, recv, local = refs[5 + 2 * n :]
+    hs_ref, ss_ref, w_ref, outs = refs[0], refs[1], refs[2], refs[3 : 3 + n]
+    hv, wv, halves = refs[3 + n : 6 + n]
+    held = refs[6 + n : 6 + 2 * n]
+    send, recv, local = refs[6 + 2 * n :]
     dp, seq = place()
     y, x, c = own_bit(4), own_bit(2), own_bit(1)
     loads = [pltpu.make_async_copy(h_ref.at[y], hv, local.at[0])]
@@ -447,6 +371,8 @@
         load.wait()
     own = pltpu.make_async_copy(hv, hs_ref.at[y, x, c], local.at[0])
     own.start()
+    named = pltpu.make_async_copy(s_ref.at[y], ss_ref.at[y, x, c], local.at[4 + n])
+    named.start()
     me = (y, x, c)
     keeps = [pltpu.make_async_copy(o, d.at[(dp,) + me], local.at[4 + i]) for i, (o, d) in enumerate(zip(held, outs))]
     for keep in keeps:
@@ -454,6 +380,11 @@
     run = Copies(send, recv)
     pieces = []
 
+    pieces.append((0, [
+        (None, [run.remote(s_ref.at[1 - y], ss_ref.at[y, x, c], partner_seq(4))]),
+        (named.wait, [run.remote(ss_ref.at[:, x, c], ss_ref.at[:, x, c], partner_seq(2))]),
+        (None, [run.remote(ss_ref.at[:, :, c], ss_ref.at[:, :, c], partner_seq(1))]),
+    ]))
     tokens = hv.shape[0]
     parts = 4
     for i in range(parts):
@@ -502,11 +433,11 @@
     run.run(pieces, lag)
 
 
-def start(plan, acts, weights, whole, piece, lag, collective_id):
+def start(plan, acts, segments, weights, whole, piece, lag, collective_id):
     groups, columns, width = acts.shape
     rows = weights[0].shape[0]
     quarter = width // 4
-    splits, copies = [], 4 * 3 + 3 * (3 + len(plan.masks))
+    splits, copies = [], 3 + 4 * 3 + 3 * (3 + len(plan.masks))
     for a in whole:
         count = max(1, a.shape[1] // piece)
         while a.shape[1] % (256 * count):
@@ -518,10 +449,11 @@
         functools.partial(start_kernel, plan, splits, lag),
         out_shape=[
             jax.ShapeDtypeStruct((2, 2, 2, columns, width), acts.dtype),
+            jax.ShapeDtypeStruct((2, 2, 2, 1, columns), jnp.int32),
             jax.ShapeDtypeStruct((3,) + plan.lead() + (rows, quarter), acts.dtype),
         ] + [jax.ShapeDtypeStruct(plan.lead() + a.shape, a.dtype) for a in whole],
-        in_specs=[hbm] * (4 + len(whole)),
-        out_specs=[hbm] * (2 + len(whole)),
+        in_specs=[hbm] * (5 + len(whole)),
+        out_specs=[hbm] * (3 + len(whole)),
         scratch_shapes=[
             pltpu.VMEM((columns, width), acts.dtype),
             pltpu.VMEM((3, rows, width), acts.dtype),
@@ -529,58 +461,18 @@
         ] + [pltpu.VMEM(a.shape, a.dtype) for a in whole] + [
             pltpu.SemaphoreType.DMA((copies,)),
             pltpu.SemaphoreType.DMA((copies,)),
-            pltpu.SemaphoreType.DMA((4 + len(whole),)),
+            pltpu.SemaphoreType.DMA((5 + len(whole),)),
         ],
         compiler_params=pltpu.CompilerParams(
             collective_id=collective_id, has_side_effects=True, vmem_limit_bytes=32 << 20),
-    )(acts, *weights, *whole)
-    tokens, projections = outs[0], outs[1]
+    )(acts, segments[:, None, :], *weights, *whole)
+    tokens, ids, projections = outs[:3]
     return (
         tokens.reshape(8, columns, width),
+        ids.reshape(8 * columns),
         projections.reshape(3, width, quarter),
-        [o.reshape(-1, o.shape[-1]) for o in outs[2:]],
-    )
-
-
-def project_kernel(x_ref, w_ref, cos_ref, sin_ref, out_ref, turned_ref):
-    parts, columns, width = x_ref.shape
-    acts = x_ref[...].reshape(parts * columns, width)
-    heads = out_ref.shape[1]
-    for kind in range(3):
-        made = dot(acts, w_ref[kind])
-        for p in range(heads):
-            head = made[:, p * HEAD_DIM : (p + 1) * HEAD_DIM]
-            if kind < 2:
-                head = head * cos_ref[...] + pltpu.roll(head, HEAD_DIM // 2, 1) * sin_ref[...]
-            out_ref[:, p, kind] = head.astype(jnp.bfloat16).reshape(parts, columns, HEAD_DIM)
-    turned_ref[...] = acts.T
-
-
-def project_heads(acts, weights, cosine, sine):
-    owners, columns, width = acts.shape
-    parts = 512 // columns
-    block = parts * columns
-    heads = weights.shape[2] // HEAD_DIM
-    table = pl.BlockSpec((block, HEAD_DIM), lambda i: (i, 0))
-    return pl.pallas_call(
-        project_kernel,
-        grid=(owners // parts,),
-        in_specs=[
-            pl.BlockSpec((parts, columns, width), lambda i: (i, 0, 0)),
-            pl.BlockSpec(weights.shape, lambda i: (0, 0, 0)),
-            table,
-            table,
-        ],
-        out_specs=[
-            pl.BlockSpec((parts, heads, 3, columns, HEAD_DIM), lambda i: (i, 0, 0, 0, 0)),
-            pl.BlockSpec((width, block), lambda i: (0, i)),
-        ],
-        out_shape=[
-            jax.ShapeDtypeStruct((owners, heads, 3, columns, HEAD_DIM), jnp.bfloat16),
-            jax.ShapeDtypeStruct((width, owners * columns), jnp.bfloat16),
-        ],
-        compiler_params=pltpu.CompilerParams(vmem_limit_bytes=56 << 20),
-    )(acts, weights, cosine, sine)
+        [o.reshape(-1, o.shape[-1]) for o in outs[3:]],
+    )
 
 
 def finish_kernel(
@@ -798,6 +690,489 @@
     )(grads, turned, weights, inputs, grad_first, gain, more)
 
 
+class Gather:
+    def __init__(self, plan, lag, shard, rows, cols):
+        self.plan, self.lag, self.rows, self.cols = plan, lag, rows, cols
+        self.across = shard.shape[1] // cols
+        self.pieces = shard.shape[0] // rows * self.across
+        self.ticks = self.pieces + lag * (plan.hops + 1)
+        self.out_shape = jax.ShapeDtypeStruct(plan.lead() + shard.shape, shard.dtype)
+        each = 2 * (len(plan.masks) + plan.hops)
+        self.scratch = [
+            pltpu.VMEM(shard.shape, shard.dtype),
+            pltpu.SemaphoreType.DMA((2 * lag, each)),
+            pltpu.SemaphoreType.DMA((2 * lag, each)),
+            pltpu.SemaphoreType.DMA((2,)),
+        ]
+
+    def copies(self, stage, u, full, held, send, recv):
+        plan = self.plan
+        dp, _ = place()
+        me = tuple(own_bit(b) for b in plan.bits)
+        slot = lax.rem(u, 2 * self.lag)
+        rows = pl.ds(pl.multiple_of(lax.div(u, self.across) * self.rows, 16), self.rows)
+        out = []
+        for h in range(2):
+            start = lax.rem(u, self.across) * self.cols + h * (self.cols // 2)
+            cols = pl.ds(pl.multiple_of(start, 128), self.cols // 2)
+            base = h * (len(plan.masks) + plan.hops)
+            if stage == 0:
+                for n, mask in enumerate(plan.masks):
+                    out.append(pltpu.make_async_remote_copy(
+                        held.at[rows, cols], full.at[(dp,) + me + (rows, cols)],
+                        send.at[slot, base + n], recv.at[slot, base + n],
+                        device_id=partner_dp(plan, mask), device_id_type=MESH))
+            else:
+                order = plan.orders[h]
+                where = tuple(slice(None) if b in order[: stage - 1] else m for b, m in zip(plan.bits, me))
+                part = full.at[(slice(None),) + where + (rows, cols)]
+                at = base + len(plan.masks) + stage - 1
+                out.append(pltpu.make_async_remote_copy(
+                    part, part, send.at[slot, at], recv.at[slot, at],
+                    device_id=partner_seq(order[stage - 1]), device_id_type=MESH))
+        return out
+
+    def run(self, tick, shard, full, held, send, recv, local):
+        plan, lag = self.plan, self.lag
+        dp, _ = place()
+        me = tuple(own_bit(b) for b in plan.bits)
+        own = pltpu.make_async_copy(held, full.at[(dp,) + me], local.at[0])
+
+        @pl.when(tick == 0)
+        def _():
+            load = pltpu.make_async_copy(shard, held, local.at[1])
+            load.start()
+            load.wait()
+            own.start()
+
+        @pl.when(tick == lag)
+        def _():
+            own.wait()
+
+        stages = plan.hops + 1
+        for stage in reversed(range(stages + 1)):
+            u = tick - lag * stage
+
+            @pl.when((u >= 0) & (u < self.pieces))
+            def _(stage=stage, u=u):
+                if stage > 0:
+                    for copy in self.copies(stage - 1, u, full, held, send, recv):
+                        copy.wait()
+                if stage < stages:
+                    for copy in self.copies(stage, u, full, held, send, recv):
+                        copy.start()
+
+
+def attend_step(block, parts, pair, step, packed, col_ref, row_ref, o_ref, ot_ref, lse_ref, vt_ref):
+    @pl.when(step == 0)
+    def _():
+        vt_ref[...] = packed[:, pair, 2].reshape(-1, HEAD_DIM).T
+
+    query = packed[pl.ds(step * parts, parts), pair, 0].reshape(block, HEAD_DIM)
+    query_row = row_ref[pl.ds(step, 1), :]
+    unit = LOG2E / math.sqrt(HEAD_DIM)
+
+    def visit(j, carry, diagonal):
+        top, total, mixed = carry
+        key = packed[pl.ds(j * parts, parts), pair, 1].reshape(block, HEAD_DIM)
+        at = pl.multiple_of(j * block, block)
+        scores = dot(key, query, NT) * unit
+        scores = jnp.where(allowed_pairs(col_ref[pl.ds(at, block), :], query_row, diagonal), scores, MASKED)
+        above = jnp.maximum(top, jnp.max(scores, axis=0, keepdims=True))
+        expo = jnp.exp2(scores - above)
+        fade = jnp.exp2(top - above)
+        total = total * fade + jnp.sum(expo, axis=0, keepdims=True)
+        mixed = mixed * fade + dot(vt_ref[:, pl.ds(at, block)], expo.astype(jnp.bfloat16))
+        return above, total, mixed
+
+    start = (
+        jnp.full((1, block), MASKED, jnp.float32),
+        jnp.zeros((1, block), jnp.float32),
+        jnp.zeros((HEAD_DIM, block), jnp.float32),
+    )
+    carry = lax.fori_loop(0, step, lambda j, c: visit(j, c, False), start)
+    top, total, mixed = visit(step, carry, True)
+    mixed = mixed / total
+    ot_ref[0, 0] = mixed
+    lse_ref[0, pl.ds(step, 1), :] = top + jnp.log2(total)
+    o_ref[...] = mixed.T.astype(jnp.bfloat16).reshape(o_ref.shape)
+
+
+def attention_kernel(
+    plan, gather, block, first, x_ref, w_ref, cos_ref, sin_ref, col_ref, row_ref, shard,
+    packed, turned_ref, o_ref, ot_ref, lse_ref, full, vt_ref, *more,
+):
+    tick = pl.program_id(0)
+
+    @pl.when(tick == 0)
+    def _():
+        greet(plan)
+
+    gather.run(tick, shard, full, *more)
+    parts, columns, width = x_ref.shape
+    heads = packed.shape[1]
+
+    @pl.when(tick < first)
+    def _():
+        acts = x_ref[...].reshape(block, width)
+        for kind in range(3):
+            made = dot(acts, w_ref[kind])
+            for p in range(heads):
+                head = made[:, p * HEAD_DIM : (p + 1) * HEAD_DIM]
+                if kind < 2:
+                    head = head * cos_ref[...] + pltpu.roll(head, HEAD_DIM // 2, 1) * sin_ref[...]
+                packed[pl.ds(tick * parts, parts), p, kind] = head.astype(jnp.bfloat16).reshape(parts, columns, HEAD_DIM)
+        turned_ref[...] = acts.T
+
+    @pl.when((tick >= first) & (tick < first * (1 + heads)))
+    def _():
+        pair, step = lax.div(tick - first, first), lax.rem(tick - first, first)
+        attend_step(block, parts, pair, step, packed, col_ref, row_ref, o_ref, ot_ref, lse_ref, vt_ref)
+
+
+def attention(plan, acts, weights, cosine, sine, seg_col, seg_row, shard, lag, collective_id):
+    owners, columns, width = acts.shape
+    heads = weights.shape[2] // HEAD_DIM
+    steps, block = seg_row.shape
+    parts, length = block // columns, owners * columns
+    gather = Gather(plan, lag, shard, shard.shape[0], 512)
+    low = jnp.bfloat16
+
+    def at(t):
+        return jnp.clip(t, 0, steps - 1)
+
+    def pair(t):
+        return lax.div(jnp.clip(t - steps, 0, steps * heads - 1), steps)
+
+    def step(t):
+        return lax.rem(jnp.clip(t - steps, 0, steps * heads - 1), steps)
+
+    def fixed(shape):
+        return pl.BlockSpec(shape, lambda t: (0,) * len(shape))
+
+    hbm = pl.BlockSpec(memory_space=pl.ANY)
+    table = pl.BlockSpec((block, HEAD_DIM), lambda t: (at(t), 0))
+    packed_shape = (owners, heads, 3, columns, HEAD_DIM)
+    return pl.pallas_call(
+        functools.partial(attention_kernel, plan, gather, block, steps),
+        grid=(max(gather.ticks, steps * (1 + heads)),),
+        in_specs=[
+            pl.BlockSpec((parts, columns, width), lambda t: (at(t), 0, 0)),
+            fixed(weights.shape),
+            table,
+            table,
+            fixed((length, 1)),
+            fixed((steps, block)),
+            hbm,
+        ],
+        out_specs=[
+            fixed(packed_shape),
+            pl.BlockSpec((width, block), lambda t: (0, at(t))),
+            pl.BlockSpec((parts, None, columns, HEAD_DIM), lambda t: (step(t), pair(t), 0, 0)),
+            pl.BlockSpec((1, 1, HEAD_DIM, block), lambda t: (pair(t), step(t), 0, 0)),
+            pl.BlockSpec((1, steps, block), lambda t: (pair(t), 0, 0)),
+            hbm,
+        ],
+        out_shape=[
+            jax.ShapeDtypeStruct(packed_shape, low),
+            jax.ShapeDtypeStruct((width, length), low),
+            jax.ShapeDtypeStruct((owners, heads, columns, HEAD_DIM), low),
+            jax.ShapeDtypeStruct((heads, steps, HEAD_DIM, block), jnp.float32),
+            jax.ShapeDtypeStruct((heads, steps, block), jnp.float32),
+            gather.out_shape,
+        ],
+        scratch_shapes=[pltpu.VMEM((HEAD_DIM, length), low)] + gather.scratch,
+        compiler_params=pltpu.CompilerParams(
+            collective_id=collective_id, has_side_effects=True, vmem_limit_bytes=56 << 20),
+    )(acts, weights, cosine, sine, seg_col, seg_row, shard)
+
+
+class Mlp:
+    def __init__(self, plan, lag, mixed, w_out, inputs, gain, offset, w_up, grad, cotangent, shard):
+        tokens, width = inputs.shape
+        hidden = w_up.shape[1]
+        self.plan, self.lag = plan, lag
+        self.blocks = 2 * plan.n_dp
+        self.block = hidden // self.blocks
+        self.rows = width // (plan.n_dp * plan.n_seq)
+        self.gather = Gather(plan, lag, shard, self.rows, 512)
+        self.meet = 4
+        self.up = self.meet + 1
+        self.back = max(self.gather.ticks, self.up + self.blocks)
+        self.norm = self.back + self.blocks
+        self.ticks = self.norm + 5
+        self.operands = (mixed, w_out, inputs, gain, offset, w_up, grad, cotangent, shard)
+        blocks, back, up = self.blocks, self.back, self.up
+
+        def up_block(t):
+            later = jnp.clip(t - (up + blocks) + 1, 0, 1)
+            return (0, jnp.clip(t - up, 0, blocks - 1) * (1 - later) + jnp.clip(t - back, 0, blocks - 1) * later)
+
+        once = pl.BlockSpec((tokens, width), lambda t: (0, 0), pipeline_mode=pl.Buffered(1))
+        row = pl.BlockSpec((1, width), lambda t: (0, 0))
+        hbm = pl.BlockSpec(memory_space=pl.ANY)
+        self.in_specs = [hbm, hbm, hbm, row, row, pl.BlockSpec((width, self.block), up_block), once, hbm, hbm]
+        self.out_specs = [
+            hbm,
+            hbm,
+            hbm,
+            hbm,
+            hbm,
+            hbm,
+            pl.BlockSpec((tokens, self.block), lambda t: (0, jnp.clip(t - back, 0, blocks - 1))),
+            hbm,
+            pl.BlockSpec((8, width), lambda t: (0, 0)),
+            hbm,
+        ]
+        low = jnp.bfloat16
+        flat = jax.ShapeDtypeStruct((tokens, width), jnp.float32)
+        self.out_shapes = [
+            flat,
+            flat,
+            flat,
+            jax.ShapeDtypeStruct((tokens, width), low),
+            jax.ShapeDtypeStruct((width, tokens), low),
+            jax.ShapeDtypeStruct((width, tokens), low),
+            jax.ShapeDtypeStruct((tokens, hidden), low),
+            jax.ShapeDtypeStruct(mixed.shape, low),
+            jax.ShapeDtypeStruct((8, width), jnp.float32),
+            self.gather.out_shape,
+        ]
+        self.chunk = 64
+        self.scratch = [
+            pltpu.VMEM((tokens, hidden), low),
+            pltpu.VMEM((hidden, tokens), low),
+            pltpu.VMEM((tokens, hidden), low),
+            pltpu.VMEM((2, 2, 2) + shard.shape, low),
+            pltpu.VMEM((tokens, width), jnp.float32),
+            pltpu.VMEM((tokens, width), jnp.float32),
+            pltpu.VMEM((tokens, width), low),
+            pltpu.VMEM(mixed.shape, low),
+            pltpu.VMEM((2, 2, self.chunk, width), jnp.float32),
+            pltpu.SemaphoreType.DMA((2, 2, plan.n_seq)),
+            pltpu.SemaphoreType.DMA((16,)),
+            pltpu.SemaphoreType.DMA((2, 2)),
+            pltpu.SemaphoreType.DMA((2,)),
+        ] + self.gather.scratch
+
+    everyone = True
+
+    def left(self, refs, which, z):
+        turned, n = refs[20], self.plan.n_seq
+        every = turned.shape[0] // (n * self.plan.n_dp)
+        return jnp.concatenate(
+            [
+                turned[pl.ds(pl.multiple_of((z * n + d) * every + which * self.rows, 16), self.rows), :]
+                for d in range(n)
+            ],
+            axis=0,
+        )
+
+    def run(self, tick, refs):
+        mixed_hbm, w_out, inputs, gain_ref, offset_ref, up_ref, grad_ref, cotangent, shard = refs[:9]
+        output, first_sum, grad_first, grad_low, mixed_turned, acts_turned, gu_ref, back_pairs, sums_ref, full = refs[9:19]
+        hidden_ref, turned_ref, slope_ref, down_ref, out_ref, back_ref, acts_ref, pairs, chunks = refs[19:28]
+        swaps, local, loads, fetch = refs[28:32]
+        plan, block = self.plan, self.block
+        dp, seq = place()
+        count, heads, columns, _ = pairs.shape
+        tokens, width = acts_ref.shape
+        low = jnp.bfloat16
+        third = 512
+        thirds = width // third
+        self.gather.run(tick, shard, full, *refs[32:])
+
+        def exchange(which, src, dst):
+            return [
+                pltpu.make_async_remote_copy(
+                    src.at[lax.bitwise_xor(seq, m)], dst.at[seq], swaps.at[which, 0, m], swaps.at[which, 1, m],
+                    device_id=partner_seq(m), device_id_type=MESH)
+                for m in range(1, count)
+            ]
+
+        there = exchange(0, mixed_hbm, pairs)
+        here = pltpu.make_async_copy(mixed_hbm.at[seq], pairs.at[seq], local.at[0])
+        based = pltpu.make_async_copy(inputs, out_ref, local.at[1])
+        outs = [
+            pltpu.make_async_copy(
+                w_out.at[:, pl.ds(n * third, third)], turned_ref.at[pl.ds(n * width, width), :], local.at[2 + n])
+            for n in range(thirds)
+        ]
+        kept = pltpu.make_async_copy(out_ref, first_sum, local.at[5])
+        turns = []
+        for n in range(thirds):
+            rows = pl.ds(n * third, third)
+            base = slope_ref.shape[1] - 2 * width + n * third
+            turns.append(pltpu.make_async_copy(slope_ref.at[:, pl.ds(base, third)], mixed_turned.at[rows, :], local.at[6 + n]))
+            turns.append(pltpu.make_async_copy(
+                slope_ref.at[:, pl.ds(base + width, third)], acts_turned.at[rows, :], local.at[9 + n]))
+
+        @pl.when(tick == 0)
+        def _():
+            for copy in there + [here, based] + outs:
+                copy.start()
+
+        @pl.when(tick == self.meet)
+        def _():
+            for copy in there + [here, based] + outs:
+                copy.wait()
+            per = width // (heads * HEAD_DIM)
+            for s in range(count // per):
+                for g in range(per):
+                    for p in range(heads):
+                        at = (g * heads + p) * HEAD_DIM
+                        acts_ref[s * columns : (s + 1) * columns, at : at + HEAD_DIM] = pairs[s * per + g, p]
+            for n in range(thirds):
+                part = slice(n * third, (n + 1) * third)
+                out_ref[:, part] += dot(acts_ref[...], turned_ref[n * width : (n + 1) * width, :])
+                base = slope_ref.shape[1] - 2 * width + n * third
+                slope_ref[:, base : base + third] = acts_ref[:, part].T
+            kept.start()
+
+            def norm(i, carry):
+                rows = pl.ds(pl.multiple_of(i * self.chunk, self.chunk), self.chunk)
+                values = out_ref[rows, :]
+                centre = values - jnp.mean(values, axis=-1, keepdims=True)
+                spread = lax.rsqrt(jnp.mean(centre * centre, axis=-1, keepdims=True) + EPSILON)
+                acts_ref[rows, :] = (centre * spread * gain_ref[...] + offset_ref[...]).astype(low)
+                return carry
+
+            lax.fori_loop(0, tokens // self.chunk, norm, 0)
+            for n in range(thirds):
+                base = slope_ref.shape[1] - width + n * third
+                slope_ref[:, base : base + third] = acts_ref[:, n * third : (n + 1) * third].T
+            for copy in turns:
+                copy.start()
+
+        @pl.when(tick == self.up + 2)
+        def _():
+            for copy in turns + [kept]:
+                copy.wait()
+
+        def block_at(i):
+            return pl.ds(pl.multiple_of(i * block, 128), block)
+
+        @pl.when((tick >= self.up) & (tick < self.up + self.blocks))
+        def _():
+            step = 256
+            for n in range(block // step):
+                upper = dot(acts_ref[...], up_ref[:, n * step : (n + 1) * step])
+                share = 0.5 + 0.5 * lax.erf(upper * (1.0 / math.sqrt(2.0)))
+                density = jnp.exp(upper * upper * -0.5) * (1.0 / math.sqrt(2.0 * math.pi))
+                made = (upper * share).astype(low)
+                at = pl.multiple_of((tick - self.up) * block + n * step, 128)
+                hidden_ref[:, pl.ds(at, step)] = made
+                turned_ref[pl.ds(at, step), :] = made.T
+                slope_ref[:, pl.ds(at, step)] = (share + upper * density).astype(low)
+
+        def fetched(i):
+            z, y = lax.div(i, 2), lax.rem(i, 2)
+            return pltpu.make_async_copy(full.at[z, y], down_ref.at[y], fetch.at[y])
+
+        i = tick - self.back
+
+        @pl.when((i >= -1) & (i < self.blocks - 1))
+        def _():
+            fetched(i + 1).start()
+
+        @pl.when((i >= 0) & (i < self.blocks))
+        def _():
+            fetched(i).wait()
+            down = down_ref[lax.rem(i, 2)].reshape(block, -1)
+
+            @pl.when(i == 0)
+            def _():
+                back_ref[...] = jnp.zeros_like(back_ref)
+
+            grad = dot(grad_ref[...], down, NT) * slope_ref[:, block_at(i)].astype(jnp.float32)
+            gu_ref[...] = grad.astype(low)
+            for n in range(thirds):
+                part = slice(n * third, (n + 1) * third)
+                out_ref[:, part] += dot(hidden_ref[:, block_at(i)], down[:, part])
+                back_ref[:, part] += dot(gu_ref[...], up_ref[part, :], NT)
+
+        done = pltpu.make_async_copy(out_ref, output, local.at[12])
+        first_out = pltpu.make_async_copy(back_ref, grad_first, local.at[13])
+        low_out = pltpu.make_async_copy(acts_ref, grad_low, local.at[14])
+        chunk = self.chunk
+
+        def chunk_loads(j, slot):
+            rows = pl.ds(pl.multiple_of(j * chunk, chunk), chunk)
+            return [
+                pltpu.make_async_copy(src.at[rows, :], chunks.at[slot, n], loads.at[slot, n])
+                for n, src in enumerate((first_sum, cotangent))
+            ]
+
+        @pl.when(tick == self.norm - 1)
+        def _():
+            for copy in outs:
+                copy.start()
+
+        @pl.when(tick == self.norm)
+        def _():
+            done.start()
+            sums_ref[...] = jnp.zeros_like(sums_ref)
+            for copy in chunk_loads(0, 0):
+                copy.start()
+            total = tokens // chunk
+
+            def norm_back(j, carry):
+                slot = lax.rem(j, 2)
+
+                @pl.when(j + 1 < total)
+                def _():
+                    for copy in chunk_loads(j + 1, 1 - slot):
+                        copy.start()
+
+                for copy in chunk_loads(j, slot):
+                    copy.wait()
+                rows = pl.ds(pl.multiple_of(j * chunk, chunk), chunk)
+                values = chunks[slot, 0]
+                centre = values - jnp.mean(values, axis=-1, keepdims=True)
+                spread = lax.rsqrt(jnp.mean(centre * centre, axis=-1, keepdims=True) + EPSILON)
+                normed = centre * spread
+                grad = back_ref[rows, :]
+                grown = grad * gain_ref[...]
+                mean_one = jnp.mean(grown, axis=-1, keepdims=True)
+                mean_two = jnp.mean(grown * normed, axis=-1, keepdims=True)
+                made = chunks[slot, 1] + (grown - mean_one - normed * mean_two) * spread
+                sums_ref[0:1] += jnp.sum(grad * normed, axis=0, keepdims=True)
+                sums_ref[1:2] += jnp.sum(grad, axis=0, keepdims=True)
+                back_ref[rows, :] = made
+                acts_ref[rows, :] = made.astype(low)
+                return carry
+
+            lax.fori_loop(0, total, norm_back, 0)
+            first_out.start()
+            low_out.start()
+
+        again = exchange(1, pairs, back_pairs)
+        home = pltpu.make_async_copy(pairs.at[seq], back_pairs.at[seq], local.at[0])
+
+        @pl.when(tick == self.norm + 1)
+        def _():
+            for copy in outs:
+                copy.wait()
+            per = width // (heads * HEAD_DIM)
+            step = heads * HEAD_DIM
+            for g in range(per):
+                made = sum(
+                    dot(acts_ref[:, n * third : (n + 1) * third],
+                        turned_ref[n * width + g * step : n * width + (g + 1) * step, :], NT)
+                    for n in range(thirds)
+                ).astype(low)
+                for s in range(count // per):
+                    for p in range(heads):
+                        pairs[s * per + g, p] = made[s * columns : (s + 1) * columns, p * HEAD_DIM : (p + 1) * HEAD_DIM]
+            for copy in again + [home]:
+                copy.start()
+
+        @pl.when(tick == self.ticks - 1)
+        def _():
+            for copy in again + [home, done, first_out, low_out]:
+                copy.wait()
+
+
 def layer_norm(values, gain, offset):
     centre = values - jnp.mean(values, axis=-1, keepdims=True)
     spread = jnp.mean(centre * centre, axis=-1, keepdims=True)
@@ -808,6 +1183,22 @@
     return 0.5 * values * (1.0 + lax.erf(values * (1.0 / math.sqrt(2.0))))
 
 
+def angles(positions):
+    half = HEAD_DIM // 2
+    rates = jnp.exp(jnp.arange(half, dtype=jnp.float32) * (-math.log(10000.0) / half))
+    turned = positions.astype(jnp.float32)[:, None] * rates[None, :]
+    return (jnp.cos(turned)[:, None, :], jnp.sin(turned)[:, None, :])
+
+
+def rotary(values, cosine, sine):
+    half = values.shape[-1] // 2
+    first = values[..., :half]
+    second = values[..., half:]
+    return jnp.concatenate(
+        [first * cosine - second * sine, second * cosine + first * sine], axis=-1
+    )
+
+
 def lower(values):
     return values.astype(jnp.bfloat16)
 
@@ -822,6 +1213,221 @@
 
 def outer_sum(left, right):
     return jnp.einsum("gci,gcj->ij", left, right, preferred_element_type=jnp.float32)
+
+
+def plain_shards(
+    inputs,
+    segments,
+    norm1_gain,
+    norm1_bias,
+    w_query,
+    w_key,
+    w_value,
+    w_out,
+    norm2_gain,
+    norm2_bias,
+    w_up,
+    w_down,
+    cotangent,
+):
+    groups, columns, width = inputs.shape
+    heads_count = width // HEAD_DIM
+    scale = 1.0 / math.sqrt(HEAD_DIM)
+    full_query, full_key, full_value, full_out, full_up, full_down = (
+        lax.all_gather(w_query, ("dp", "seq"), axis=0, tiled=True),
+        lax.all_gather(w_key, ("dp", "seq"), axis=0, tiled=True),
+        lax.all_gather(w_value, ("dp", "seq"), axis=0, tiled=True),
+        lax.all_gather(w_out, ("dp", "seq"), axis=0, tiled=True),
+        lax.all_gather(w_up, ("dp", "seq"), axis=0, tiled=True),
+        lax.all_gather(w_down, ("dp", "seq"), axis=0, tiled=True),
+    )
+    key_ids = lax.all_gather(segments, "seq", axis=1, tiled=True)
+    length = key_ids.shape[1]
+    rank = lax.axis_index("seq")
+    places = rank * columns + jnp.arange(columns, dtype=jnp.int32)
+    key_places = jnp.arange(length, dtype=jnp.int32)
+    cosine, sine = angles(places)
+
+    def turn(values):
+        shaped = values.reshape(groups, columns, heads_count, HEAD_DIM)
+        return rotary(shaped, cosine, sine).reshape(groups, columns, width)
+
+    def permitted(segment_row, key_row):
+        same = segment_row[:, None] == key_row[None, :]
+        causal = key_places[None, :] <= places[:, None]
+        live = (key_row[None, :] >= 0) | (key_places[None, :] == places[:, None])
+        return same & causal & live
+
+    def scores_of(query_row, key_block, segment_row, key_row):
+        heads_query = query_row.reshape(columns, heads_count, HEAD_DIM)
+        heads_key = key_block.reshape(length, heads_count, HEAD_DIM)
+        raw = (
+            jnp.einsum("chd,lhd->hcl", heads_query, heads_key, preferred_element_type=jnp.float32)
+            * scale
+        )
+        return jnp.where(permitted(segment_row, key_row)[None], raw, MASKED)
+
+    normed_one = layer_norm(inputs, norm1_gain, norm1_bias)
+    act_one = lower(normed_one)
+    query_zero = project(act_one, full_query)
+    key_zero = project(act_one, full_key)
+    value_low = lower(project(act_one, full_value))
+    query_low = lower(turn(query_zero))
+    key_low = lower(turn(key_zero))
+    keys_all, values_all = (
+        lax.all_gather(key_low, "seq", axis=1, tiled=True),
+        lax.all_gather(value_low, "seq", axis=1, tiled=True),
+    )
+
+    def attend(items):
+        query_row, key_block, value_block, segment_row, key_row = items
+        scores = scores_of(query_row, key_block, segment_row, key_row)
+        top = jnp.max(scores, axis=-1, keepdims=True)
+        expo = jnp.exp(scores - top)
+        total = jnp.sum(expo, axis=-1, keepdims=True)
+        probs = lower(expo / total)
+        heads_value = value_block.reshape(length, heads_count, HEAD_DIM)
+        mixed = jnp.einsum("hcl,lhd->chd", probs, heads_value, preferred_element_type=jnp.float32)
+        return (mixed.reshape(columns, width), top[..., 0] + jnp.log(total[..., 0]))
+
+    mixed_all, log_totals = lax.map(attend, (query_low, keys_all, values_all, segments, key_ids))
+    mixed_low = lower(mixed_all)
+    first_sum = inputs + project(mixed_low, full_out)
+    act_two = lower(layer_norm(first_sum, norm2_gain, norm2_bias))
+    upper = project(act_two, full_up)
+    hidden_low = lower(gelu(upper))
+    output = first_sum + project(hidden_low, full_down)
+    half_width = width // 2
+    half_hidden = full_up.shape[1] // 2
+    grad_out_low = lower(cotangent)
+    down_left = outer_sum(hidden_low, grad_out_low[..., :half_width])
+    down_right = outer_sum(hidden_low, grad_out_low[..., half_width:])
+    grad_hidden = project_back(grad_out_low, full_down)
+    gelu_values, gelu_back = jax.vjp(gelu, upper)
+    grad_upper = lower(gelu_back(grad_hidden)[0])
+    up_left = outer_sum(act_two, grad_upper[..., :half_hidden])
+    up_right = outer_sum(act_two, grad_upper[..., half_hidden:])
+    grad_act_two = project_back(grad_upper, full_up)
+    normed_two, norm_two_back = jax.vjp(layer_norm, first_sum, norm2_gain, norm2_bias)
+    grad_first_norm, gain_two_grad, offset_two_grad = norm_two_back(grad_act_two)
+    grad_first = cotangent + grad_first_norm
+    grad_attn_low = lower(grad_first)
+    out_grad = outer_sum(mixed_low, grad_attn_low)
+    grad_mixed = lower(project_back(grad_attn_low, full_out))
+    heads_mixed = mixed_all.reshape(groups, columns, heads_count, HEAD_DIM)
+    heads_gm = grad_mixed.astype(jnp.float32).reshape(groups, columns, heads_count, HEAD_DIM)
+    deltas = jnp.transpose(jnp.sum(heads_mixed * heads_gm, axis=-1), (0, 2, 1))
+    key_source, value_source = (key_low, value_low)
+
+    def attend_back(carry, items):
+        query_row, grad_row, log_row, delta_row, segment_row, key_row, key_part, value_part = items
+        queries_all, grads_all = (
+            lax.all_gather(query_row, "seq", axis=0, tiled=True),
+            lax.all_gather(grad_row, "seq", axis=0, tiled=True),
+        )
+        logs_all, deltas_all = (
+            lax.all_gather(log_row, "seq", axis=1, tiled=True),
+            lax.all_gather(delta_row, "seq", axis=1, tiled=True),
+        )
+        own_mask = (segment_row[None, :] == key_row[:, None]) & (
+            places[None, :] <= key_places[:, None]
+        )
+        own_mask = own_mask & (
+            (segment_row[None, :] >= 0) | (places[None, :] == key_places[:, None])
+        )
+        heads_query = queries_all.reshape(length, heads_count, HEAD_DIM)
+        heads_grad = grads_all.reshape(length, heads_count, HEAD_DIM)
+        heads_key = key_part.reshape(columns, heads_count, HEAD_DIM)
+        heads_value = value_part.reshape(columns, heads_count, HEAD_DIM)
+        raw = (
+            jnp.einsum("lhd,chd->hlc", heads_query, heads_key, preferred_element_type=jnp.float32)
+            * scale
+        )
+        scores = jnp.where(own_mask[None], raw, MASKED)
+        probs = jnp.exp(scores - logs_all[..., None])
+        grad_probs = jnp.einsum(
+            "lhd,chd->hlc", heads_grad, heads_value, preferred_element_type=jnp.float32
+        )
+        grad_scores = lower(probs * (grad_probs - deltas_all[..., None]))
+        grad_values = jnp.einsum(
+            "hlc,lhd->chd", lower(probs), heads_grad, preferred_element_type=jnp.float32
+        )
+        grad_keys = (
+            jnp.einsum("hlc,lhd->chd", grad_scores, heads_query, preferred_element_type=jnp.float32)
+            * scale
+        )
+        partial_query = (
+            jnp.einsum("hlc,chd->lhd", grad_scores, heads_key, preferred_element_type=jnp.float32)
+            * scale
+        )
+        grad_query = lax.psum_scatter(
+            partial_query.reshape(length, width).astype(jnp.bfloat16),
+            "seq",
+            scatter_dimension=0,
+            tiled=True,
+        ).astype(jnp.float32)
+        return (
+            carry,
+            (grad_query, grad_keys.reshape(columns, width), grad_values.reshape(columns, width)),
+        )
+
+    start_carry = jnp.zeros((), jnp.float32)
+    end_carry, grads_seq = lax.scan(
+        attend_back,
+        start_carry,
+        (query_low, grad_mixed, log_totals, deltas, segments, key_ids, key_source, value_source),
+    )
+    grad_query_all, grad_key_all, grad_value_all = grads_seq
+    turned_query, turn_back = jax.vjp(turn, query_zero)
+    grad_query_low = lower(turn_back(grad_query_all)[0])
+    grad_key_low = lower(turn_back(grad_key_all)[0])
+    grad_value_low = lower(grad_value_all)
+    query_grad = outer_sum(act_one, grad_query_low)
+    key_grad = outer_sum(act_one, grad_key_low)
+    value_grad = outer_sum(act_one, grad_value_low)
+    grad_act_one = project_back(grad_query_low, full_query) + project_back(grad_key_low, full_key)
+    grad_act_one = grad_act_one + project_back(grad_value_low, full_value)
+    normed_again, norm_one_back = jax.vjp(layer_norm, inputs, norm1_gain, norm1_bias)
+    grad_input_norm, gain_one_grad, offset_one_grad = norm_one_back(grad_act_one)
+    grad_input = grad_first + grad_input_norm
+    summed = (
+        lax.psum_scatter(query_grad, ("dp", "seq"), scatter_dimension=0, tiled=True),
+        lax.psum_scatter(key_grad, ("dp", "seq"), scatter_dimension=0, tiled=True),
+        lax.psum_scatter(value_grad, ("dp", "seq"), scatter_dimension=0, tiled=True),
+        lax.psum_scatter(out_grad, ("dp", "seq"), scatter_dimension=0, tiled=True),
+        lax.psum_scatter(up_left, ("dp", "seq"), scatter_dimension=0, tiled=True),
+        lax.psum_scatter(up_right, ("dp", "seq"), scatter_dimension=0, tiled=True),
+        lax.psum_scatter(down_left, ("dp", "seq"), scatter_dimension=0, tiled=True),
+        lax.psum_scatter(down_right, ("dp", "seq"), scatter_dimension=0, tiled=True),
+        lax.psum_scatter(gain_one_grad, ("dp", "seq"), scatter_dimension=0, tiled=True),
+        lax.psum_scatter(offset_one_grad, ("dp", "seq"), scatter_dimension=0, tiled=True),
+        lax.psum_scatter(gain_two_grad, ("dp", "seq"), scatter_dimension=0, tiled=True),
+        lax.psum_scatter(offset_two_grad, ("dp", "seq"), scatter_dimension=0, tiled=True),
+    )
+    query_grad, key_grad, value_grad, out_grad = (summed[0], summed[1], summed[2], summed[3])
+    up_left, up_right, down_left, down_right = (summed[4], summed[5], summed[6], summed[7])
+    gain_one_grad, offset_one_grad, gain_two_grad, offset_two_grad = (
+        summed[8],
+        summed[9],
+        summed[10],
+        summed[11],
+    )
+    up_grad = jnp.concatenate([up_left, up_right], axis=1)
+    down_grad = jnp.concatenate([down_left, down_right], axis=1)
+    return (
+        output,
+        grad_input,
+        gain_one_grad,
+        offset_one_grad,
+        query_grad,
+        key_grad,
+        value_grad,
+        out_grad,
+        gain_two_grad,
+        offset_two_grad,
+        up_grad,
+        down_grad,
+    )
 
 
 def shards(
@@ -841,170 +1447,83 @@
     *,
     plan,
 ):
-    count = plan.n_seq
-    axes = ("dp", "seq")
     groups, columns, width = inputs.shape
-    heads = width // HEAD_DIM
-    length = columns * count
+    length = columns * plan.n_seq
     block = min(512, length)
-    per = -(-groups * heads // count)
-    fast = (
-        count == 8
-        and groups == 2
-        and heads % 4 == 0
-        and columns % 64 == 0
-        and 512 % columns == 0
-        and w_query.shape[0] % 16 == 0
-    )
-    rank = lax.axis_index("seq")
-
-    ids = lax.all_gather(segments, "seq", axis=1, tiled=True)
-    pair_at = jnp.minimum(rank * per + jnp.arange(per, dtype=jnp.int32), groups * heads - 1)
-    pair_ids = ids[pair_at // heads]
-    seg_row = pair_ids.reshape(per, length // block, block)
-    seg_col = jnp.where(pair_ids < 0, -2, pair_ids)[..., None]
+    lag, piece = 2, 512
+    every = plan.n_dp * plan.n_seq
 
     half = HEAD_DIM // 2
-    rates = jnp.exp(jnp.arange(half, dtype=jnp.float32) * (-math.log(10000.0) / half))
-    turned = jnp.arange(length, dtype=jnp.float32)[:, None] * rates[None, :]
-    cosine, sine = jnp.cos(turned), jnp.sin(turned)
-    cosine_all = jnp.concatenate([cosine, cosine], axis=1)
-    sine_all = jnp.concatenate([-sine, sine], axis=1)
-    cosine_own = lax.dynamic_slice_in_dim(cosine_all, rank * columns, columns)[None, :, None, :]
-    sine_own = lax.dynamic_slice_in_dim(sine_all, rank * columns, columns)[None, :, None, :]
-
-    def to_pairs(values):
-        shaped = values.reshape(groups, columns, heads, HEAD_DIM)
-        shaped = jnp.transpose(shaped, (0, 2, 1, 3)).reshape(groups * heads, columns, HEAD_DIM)
-        shaped = jnp.pad(shaped, ((0, count * per - groups * heads), (0, 0), (0, 0)))
-        return shaped.reshape(count, per, columns, HEAD_DIM)
-
-    def from_pairs(values):
-        shaped = values.reshape(count * per, columns, HEAD_DIM)[: groups * heads]
-        shaped = shaped.reshape(groups, heads, columns, HEAD_DIM)
-        return jnp.transpose(shaped, (0, 2, 1, 3)).reshape(groups, columns, width)
-
-    def swap(values):
-        return lax.all_to_all(values, "seq", 0, 0)
-
-    def whole(weight):
-        return lax.all_gather(weight, axes, axis=0, tiled=True)
+    rates = np.exp(np.arange(half, dtype=np.float32) * np.float32(-math.log(10000.0) / half))
+    angle = (np.arange(length, dtype=np.float32)[:, None] * rates[None, :]).astype(np.float32)
+    cosine = jnp.asarray(np.concatenate([np.cos(angle), np.cos(angle)], axis=1), jnp.float32)
+    sine = jnp.asarray(np.concatenate([-np.sin(angle), np.sin(angle)], axis=1), jnp.float32)
+
+    def flat(values):
+        return values.reshape(groups * columns, width)
 
     act_one = lower(layer_norm(inputs, norm1_gain, norm1_bias))
-    if fast:
-        tokens_one, heads_weight, (full_out,) = start(
-            plan, act_one, (w_query, w_key, w_value), (w_out,), 512, 2, 1
-        )
-        packed, turned_one = project_heads(tokens_one, heads_weight, cosine_all, sine_all)
-    else:
-        cosine_own = lax.dynamic_slice_in_dim(cosine_all, rank * columns, columns)[None, :, None, :]
-        sine_own = lax.dynamic_slice_in_dim(sine_all, rank * columns, columns)[None, :, None, :]
-
-        def turn(values):
-            shaped = values.reshape(groups, columns, heads, HEAD_DIM)
-            return shaped * cosine_own + jnp.roll(shaped, half, axis=-1) * sine_own
-
-        full_query, full_key, full_value, full_out = (whole(w) for w in (w_query, w_key, w_value, w_out))
-        query_low = lower(turn(project(act_one, full_query)))
-        key_low = lower(turn(project(act_one, full_key)))
-        value_low = lower(project(act_one, full_value))
-        packed = swap(jnp.stack([to_pairs(query_low), to_pairs(key_low), to_pairs(value_low)], axis=2))
-    full_up, full_down = whole(w_up), whole(w_down)
-    mixed_pairs, mixed_t, lse = attend(packed, seg_col, seg_row)
-    mixed_low = from_pairs(swap(mixed_pairs))
-
-    first_sum = inputs + project(mixed_low, full_out)
-    act_two = lower(layer_norm(first_sum, norm2_gain, norm2_bias))
-    upper = project(act_two, full_up)
-    hidden_low = lower(gelu(upper))
-    output = first_sum + project(hidden_low, full_down)
-    grad_out_low = lower(cotangent)
-    grad_hidden = project_back(grad_out_low, full_down)
-    gelu_values, gelu_back = jax.vjp(gelu, upper)
-    grad_upper = lower(gelu_back(grad_hidden)[0])
-    grad_act_two = project_back(grad_upper, full_up)
-    normed_two, norm_two_back = jax.vjp(layer_norm, first_sum, norm2_gain, norm2_bias)
-    grad_first_norm, gain_two_grad, offset_two_grad = norm_two_back(grad_act_two)
-    grad_first = cotangent + grad_first_norm
-    grad_attn_low = lower(grad_first)
-    grad_mixed = lower(project_back(grad_attn_low, full_out))
-
-    tokens = groups * columns
-    width_piece = 512
-
-    def flat(values):
-        return values.reshape(tokens, -1)
-
-    def left_of(values):
-        turned = flat(values).T
-        every = plan.n_dp * plan.n_seq
-        turned = turned.reshape(every, -1, width // every, tokens)
-        return jnp.transpose(turned, (1, 0, 2, 3)).reshape(-1, width, tokens)
-
-    def reduce_all(pairs, collective_id, beside=None):
-        out, *more = reduce_products(plan, pairs, width_piece, 2, collective_id, beside)
+    tokens_one, ids, heads_weight, (full_out,) = start(
+        plan, act_one, segments, (w_query, w_key, w_value), (w_out,), piece, lag, 1
+    )
+    seg_row = ids.reshape(length // block, block)
+    seg_col = jnp.where(ids < 0, -2, ids)[:, None]
+    packed, turned_one, mixed, mixed_t, lse, full_up = attention(
+        plan, tokens_one, heads_weight, cosine, sine, seg_col, seg_row, w_up, lag, 2
+    )
+    grad_low = lower(flat(cotangent))
+    mlp = Mlp(
+        plan, lag, mixed, full_out, flat(inputs), norm2_gain[None], norm2_bias[None],
+        full_up.reshape(width, -1), grad_low, flat(cotangent), w_down,
+    )
+    rows = width // every
+
+    def reduce_all(pairs, collective_id, beside, first=0):
+        out, *more = reduce_products(plan, pairs, rows, piece, lag, collective_id, beside, first)
         results, at = [], 0
         for left, right in pairs:
-            blocks, cols = left.shape[0], right.shape[1] // width_piece
-            part = out[at : at + blocks * cols].reshape(blocks, cols, -1, width_piece)
+            blocks = left if isinstance(left, int) else left.shape[0]
+            cols = right.shape[1] // piece
+            part = out[at : at + blocks * cols].reshape(blocks, cols, -1, piece)
             results.append(jnp.transpose(part, (0, 2, 1, 3)).reshape(-1, right.shape[1]))
             at += blocks * cols
         return results + more
 
-    work = AttendBack(
-        8 if fast else 0,
-        packed, swap(to_pairs(grad_mixed)), mixed_t, lse, seg_col, seg_row, cosine_all, sine_all,
-    )
-    gains_two = [gain_two_grad, offset_two_grad]
-    if fast:
-        down_grad, up_grad, out_grad, grads = reduce_all(
-            [
-                (left_of(hidden_low), flat(grad_out_low)),
-                (left_of(act_two), flat(grad_upper)),
-                (left_of(mixed_low), flat(grad_attn_low)),
-            ],
-            2,
-            work,
-        )
-        grad_input, heads_grad, norm_rows = finish(
-            plan, grads, turned_one, heads_weight, inputs, grad_first, norm1_gain[None],
-            jnp.stack(gains_two), 3,
-        )
-        query_grad, key_grad, value_grad = heads_grad[0], heads_grad[1], heads_grad[2]
-        norm_rows = [norm_rows[:, i] for i in range(4)]
-    else:
-        def spread(values):
-            return lax.psum_scatter(values, axes, scatter_dimension=0, tiled=True).astype(jnp.float32)
-
-        grads = attend_back_alone(work).reshape(3, count, columns, per, HEAD_DIM)
-        grads = swap(jnp.transpose(grads, (1, 3, 0, 2, 4)))
-        grad_query_low, grad_key_low, grad_value_low = (from_pairs(grads[:, :, i]) for i in range(3))
-        grad_act_one = project_back(grad_query_low, full_query) + project_back(grad_key_low, full_key)
-        grad_act_one = grad_act_one + project_back(grad_value_low, full_value)
-        normed_again, norm_one_back = jax.vjp(layer_norm, inputs, norm1_gain, norm1_bias)
-        grad_input_norm, gain_one_grad, offset_one_grad = norm_one_back(grad_act_one)
-        grad_input = grad_first + grad_input_norm
-        down_grad = spread(lower(outer_sum(hidden_low, grad_out_low)))
-        up_grad = spread(lower(outer_sum(act_two, grad_upper)))
-        out_grad = spread(lower(outer_sum(mixed_low, grad_attn_low)))
-        query_grad = spread(lower(outer_sum(act_one, grad_query_low)))
-        key_grad = spread(lower(outer_sum(act_one, grad_key_low)))
-        value_grad = spread(lower(outer_sum(act_one, grad_value_low)))
-        norm_rows = [spread(v) for v in [gain_one_grad, offset_one_grad] + gains_two]
-
+    (
+        down_grad, output, _, grad_first, grad_first_low, mixed_turned, acts_turned, grad_upper, grad_pairs,
+        sums_two, _,
+    ) = reduce_all([(w_down.shape[0] // rows, grad_low)], 3, mlp, 14)
+    work = AttendBack(2, packed, grad_pairs, mixed_t, lse, seg_col, seg_row, cosine, sine)
+    up_grad, out_grad, grads = reduce_all(
+        [(acts_turned[None], grad_upper), (mixed_turned[None], grad_first_low)], 4, work
+    )
+    grad_input, heads_grad, norm_rows = finish(
+        plan, grads, turned_one, heads_weight, inputs, grad_first.reshape(inputs.shape), norm1_gain[None],
+        sums_two[:2], 5,
+    )
     return (
-        output,
+        output.reshape(inputs.shape),
         grad_input,
-        norm_rows[0],
-        norm_rows[1],
-        query_grad,
-        key_grad,
-        value_grad,
+        norm_rows[:, 0],
+        norm_rows[:, 1],
+        heads_grad[0],
+        heads_grad[1],
+        heads_grad[2],
         out_grad,
-        norm_rows[2],
-        norm_rows[3],
+        norm_rows[:, 2],
+        norm_rows[:, 3],
         up_grad,
         down_grad,
+    )
+
+
+def fits(mesh, groups, columns, width, rows):
+    return (
+        mesh.shape["seq"] == 8
+        and groups == 2
+        and width % (4 * HEAD_DIM) == 0
+        and columns == 256
+        and rows % 16 == 0
     )
 
 
@@ -1024,8 +1543,16 @@
         P(("dp", "seq"), None),
         P("dp", "seq", None),
     )
+    plan = Plan(mesh)
+
+    def layer(inputs, segments, *rest):
+        groups, columns, width = inputs.shape
+        if fits(mesh, groups, columns, width, rest[2].shape[0]):
+            return shards(inputs, segments, *rest, plan=plan)
+        return plain_shards(inputs, segments, *rest)
+
     return jax.shard_map(
-        functools.partial(shards, plan=Plan(mesh)),
+        layer,
         mesh=mesh,
         in_specs=placed,
         out_specs=(

time: 753 us -> 648 us (0.86)
  Pallas kernels: 479 us -> 611 us
  matrix products: 82.1 us -> 0 us
  waiting for transfers between devices: 75.6 us -> 0 us
  local copies, waits for them, and re-layouts: 51.1 us -> 24.6 us
  other arithmetic: 21.6 us -> 5.7 us
  between operations: 14.8 us -> 1.06 us
  blocking collectives: 10.5 us -> 0 us
  starting transfers between devices: 9.06 us -> 0 us
    pallas_call x3, Pallas kernels: 234 us -> 419 us  [the longest x2 315 us: reduce_products(): pl.pallas_call(functools.partial(reduce_kernel, plan, jobs, first, count,...]
    dot_general x6 -> x0, matrix products: 82.1 us -> none  [the longest x3 41.1 us: project(): jnp.einsum('gcd,de->gce', acts, weight, preferred_element_type=jnp.float32)]
    pallas_call x1, Pallas kernels: 154 us -> 100 us  [start(): pl.pallas_call(functools.partial(start_kernel, plan, splits, lag), out_sh...]
    all_gather x2 -> x0, waiting for transfers between devices: 43.1 us -> none  [whole(): return lax.all_gather(weight, axes, axis=0, tiled=True)]
    all_to_all x2 -> x0, waiting for transfers between devices: 31.1 us -> none  [swap(): return lax.all_to_all(values, 'seq', 0, 0)]
    transpose x3 -> x0, local copies, waits for them, and re-layouts: 12.3 us -> none  [the longest x1 5.97 us: left_of(): return jnp.transpose(turned, (1, 0, 2, 3)).reshape(-1, width, tokens)]
    reshape x4 -> x2, local copies, waits for them, and re-layouts: 12.9 us -> 1.17 us  [the longest x1 0.81 us: reduce_all(): part = out[at:at + blocks * cols].reshape(blocks, cols, -1, piece)]
    all_gather x1 -> x0, blocking collectives: 10.5 us -> none  [shards(): ids = lax.all_gather(segments, 'seq', axis=1, tiled=True)]
  transfers between devices with their start and end apart: 4 -> 0, of which waited for: 2 -> 0; matrix products, arithmetic and copies ran while one was open for 11% -> 0% of each run, Pallas kernels for 26% -> 0%
where the time goes in v3:
time: 648 us; the launch traced here: 642 us
  Pallas kernels  611 us (94%)
  local copies, waits for them, and re-layouts  24.6 us (4%)
    pallas_call x2, Pallas kernels, reduce_products(): pl.pallas_call(functools.partial(reduce_kernel, plan, jobs, first, count,...  315 us
    pallas_call x1, Pallas kernels, attention(): pl.pallas_call(functools.partial(attention_kernel, plan, gather, block, s...  104 us
    pallas_call x1, Pallas kernels, start(): pl.pallas_call(functools.partial(start_kernel, plan, splits, lag), out_sh...  100 us
    pallas_call x1, Pallas kernels, finish(): pl.pallas_call(functools.partial(finish_kernel, plan, parts), out_shape=[...  91.2 us
    unnamed x43, local copies, waits for them, and re-layouts  16.3 us

profile of v3, /device:TPU:0, one launch (start us, length us, event | category | flops | bytes accessed | tf_op | source)
XLA Modules:
  0.0 642.2 jit_solution(8679083833714502048)
XLA Ops:
  0.7 2.3 reduce_sum.18
  5.1 100.4 %shard_map.238 = (bf16[2,2,2,256,1536]{4,3,2,1,0:T(8,128)(2,1)S(1)}, s32[2,2,2,1,256]{4,3,2,1,0:T(1,128)S(1)}, bf16[3,4,2,2,2,48,384]{6,5,4,3,2,1,0:T(8,128)(2,1)S(1)}, bf16[4,2,2,2,48,1536]{5,4,3,2,1,0:T(8,128)(2,1)S(1)}) custom-call(bf16[2,256,1536]{2,1,0:T(8,128)(2,1)S(1)} %add_convert_fusion.h_ref, s32[2,1,256]{2,1,0:T(1,128)S(1)} %broadcast_in_dim.27.s_ref, ...), custom_call_target="tpu_custom_call" | custom-call | tf_op jit(solution)/shard_map/pallas_call | solution.py:448
  105.5 1.7 copy-done
  107.3 2.6 copy-done.1
  109.8 2.1 copy-done.2
  112.3 1.1 compare_select_fusion.col_ref.refs_10_
  113.4 0.6 copy.33
  114.1 104.1 %shard_map.239 = (bf16[8,3,3,256,128]{4,3,2,1,0:T(8,128)(2,1)}, bf16[1536,2048]{1,0:T(8,128)(2,1)}, bf16[8,3,256,128]{3,2,1,0:T(8,128)(2,1)}, f32[3,4,128,512]{3...) custom-call(bf16[8,256,1536]{2,1,0:T(8,128)(2,1)} %bitcast.46, ...), custom_call_target="tpu_custom_call" | custom-call | tf_op jit(solution)/shard_map/pallas_call | solution.py:856
  218.2 1.3 bitcast_convert_fusion.refs_0_.refs_7_
  219.5 0.6 broadcast_in_dim.29.refs_4_
  220.1 0.6 broadcast_in_dim.30.refs_5_
  220.7 197.3 %shard_map.240 = (f32[12,48,512]{2,1,0:T(8,128)}, f32[512,1536]{1,0:T(8,128)}, f32[512,1536]{1,0:T(8,128)}, f32[512,1536]{1,0:T(8,128)}, bf16[512,1536]{1,0:T(8,...) custom-call(bf16[512,1536]{1,0:T(8,128)(2,1)} %bitcast_convert_fusio, ...), custom_call_target="tpu_custom_call" | custom-call | tf_op jit(solution)/shard_map/pallas_call | solution.py:306
  418.0 117.8 %shard_map.241 = (f32[15,48,512]{2,1,0:T(8,128)}, bf16[3,2048,384]{2,1,0:T(8,128)(2,1)}) custom-call(bf16[1,1536,512]{2,1,0:T(8,128)(2,1)} %bitcast.56, bf16[1,1536,512]{2,1,0:T(8,128)(2,1)} %bitcast.55, bf16[512,6144]{1,0:T(8,128)(2,1)} %get-tuple-element.45.refs_2_, bf16[512,1536]{1,0:T(8,128)(2,1)} %get-tuple-element.46.refs_3_, ...), custom_call_target="tpu_custom_call" | custom-call | tf_op jit(solution)/shard_map/pallas_call | solution.py:306
  535.8 1.4 slice.30.more_ref
  537.8 91.2 %shard_map.242 = (f32[2,256,1536]{2,1,0:T(8,128)}, f32[3,48,1536]{2,1,0:T(8,128)}, f32[48,128]{1,0:T(8,128)}) custom-call(bf16[3,2048,384]{2,1,0:T(8,128)(2,1)} %get-tuple-element.51.g_any, bf16[1536,2048]{1,0:T(8,128)(2,1)} %get-tuple-element.52.t_any, bf16[3,1536,384]{2,1,0:T(8,128)(2,1)} %bitcast.45, f32[2,256,1536]{2,1,0:T(8,128)} %x_any.1, ...), custom_call_target="tpu_custom_call" | custom-call | tf_op jit(solution)/shard_map/pallas_call | solution.py:647
  629.0 2.1 slice_bitcast_fusion.2
  631.0 1.7 slice_reduce_fusion
  632.8 1.1 copy.35
  634.2 0.8 copy.34
  635.0 0.8 copy.32
  635.8 1.5 copy.36
  637.3 1.7 copy.40
  638.9 1.4 copy-done.10
  640.3 1.7 copy.41
  (43 shorter events, 3.4 us)
Async XLA Ops:
  0.6 2.8 copy-start.7
  0.7 3.3 copy-start.13
  0.7 3.3 copy-start.14
  3.9 0.7 copy-start.17
  3.9 0.9 copy-start.3
  4.0 1.0 copy-start.4
  4.0 1.0 copy-start.5
  4.0 1.1 copy-start.6
  105.5 1.7 copy-start
  107.3 2.6 copy-start.1
  109.8 2.1 copy-start.2
  114.1 104.2 %copy-start.8 = (f32[2,256,1536]{2,1,0:T(8,128)S(1)}, f32[2,256,1536]{2,1,0:T(8,128)}, u32[]{:S(2)}) copy-start(f32[2,256,1536]{2,1,0:T(8,128)} %param.27) | copy-start | bytes 9437188
  218.2 1.3 copy-start.15
  218.2 1.9 copy-start.16
  537.8 94.9 %copy-start.11 = (f32[15,48,512]{2,1,0:T(8,128)S(1)}, f32[15,48,512]{2,1,0:T(8,128)}, u32[]{:S(2)}) copy-start(f32[15,48,512]{2,1,0:T(8,128)} %get-tuple-element.58) | copy-start | bytes 4423684
  632.7 2.3 copy-start.12
  634.2 3.1 copy-start.9
  637.3 3.0 copy-start.10

commit v4 on v3

--- a/solution.py
+++ b/solution.py
@@ -34,7 +34,7 @@
 
 
 def attend_back_step(
-    block, parts, step, last, q_ref, k_ref, v_ref, g_ref, ot_ref, lse_ref, col_ref, row_ref, cos_ref, sin_ref,
+    block, parts, pair, step, last, q_ref, k_ref, v_ref, g_ref, ot_ref, lse_ref, col_ref, row_ref, cos_ref, sin_ref,
     out_ref, kt_ref, dk_ref, dv_ref,
 ):
     scale = 1.0 / math.sqrt(HEAD_DIM)
@@ -75,60 +75,13 @@
 
     at = pl.multiple_of(step * block, block)
     dq = turn_back(dqt.T * scale, cos_ref[pl.ds(at, block), :], sin_ref[pl.ds(at, block), :])
-    out_ref[0, pl.ds(at, block), :] = dq.astype(jnp.bfloat16)
+    out_ref[pair, pl.ds(at, block), :HEAD_DIM] = dq.astype(jnp.bfloat16)
 
     @pl.when(step == last)
     def _():
         dk = turn_back(dk_ref[...] * scale, cos_ref[...], sin_ref[...])
-        out_ref[1] = dk.astype(jnp.bfloat16)
-        out_ref[2] = dv_ref[...].astype(jnp.bfloat16)
-
-
-class AttendBack:
-    def __init__(self, first, packed, grads, mixed_t, lse, seg_col, seg_row, cosine, sine):
-        count, per, _, columns, _ = packed.shape
-        length = count * columns
-        self.block = seg_row.shape[1]
-        self.steps, self.parts = length // self.block, self.block // columns
-        self.first, self.count, self.ticks = first, per * self.steps, first + per * self.steps
-        self.operands = (packed, packed, packed, grads, mixed_t, lse, seg_col, seg_row, cosine, sine)
-
-        def pair(t):
-            return lax.div(jnp.clip(t - first, 0, self.count - 1), self.steps)
-
-        def step(t):
-            return lax.rem(jnp.clip(t - first, 0, self.count - 1), self.steps)
-
-        def whole(which):
-            return pl.BlockSpec((count, None, None, columns, HEAD_DIM), lambda t: (0, pair(t), which, 0, 0))
-
-        rows = pl.BlockSpec((1, self.steps, self.block), lambda t: (pair(t), 0, 0))
-        table = pl.BlockSpec((length, HEAD_DIM), lambda t: (0, 0))
-        self.in_specs = [
-            whole(0),
-            whole(1),
-            whole(2),
-            pl.BlockSpec((count, None, columns, HEAD_DIM), lambda t: (0, pair(t), 0, 0)),
-            pl.BlockSpec((1, 1, HEAD_DIM, self.block), lambda t: (pair(t), step(t), 0, 0)),
-            rows,
-            pl.BlockSpec((length, 1), lambda t: (0, 0)),
-            pl.BlockSpec((self.steps, self.block), lambda t: (0, 0)),
-            table,
-            table,
-        ]
-        self.out_specs = [pl.BlockSpec((3, length, HEAD_DIM), lambda t: (0, 0, pair(t)))]
-        self.out_shapes = [jax.ShapeDtypeStruct((3, length, per * HEAD_DIM), jnp.bfloat16)]
-        self.scratch = [
-            pltpu.VMEM((HEAD_DIM, length), jnp.bfloat16),
-            pltpu.VMEM((length, HEAD_DIM), jnp.float32),
-            pltpu.VMEM((length, HEAD_DIM), jnp.float32),
-        ]
-
-    def run(self, tick, refs):
-        @pl.when((tick >= self.first) & (tick < self.ticks))
-        def _():
-            step = lax.rem(tick - self.first, self.steps)
-            attend_back_step(self.block, self.parts, step, self.steps - 1, *refs)
+        out_ref[pair, :, HEAD_DIM : 2 * HEAD_DIM] = dk.astype(jnp.bfloat16)
+        out_ref[pair, :, 2 * HEAD_DIM :] = dv_ref[...].astype(jnp.bfloat16)
 
 
 MESH = pl.DeviceIdType.MESH
@@ -146,6 +99,15 @@
             self.orders = (tuple(bits), tuple(bits[turn:] + bits[:turn]))
         self.hops = len(bits)
         self.masks = range(1, self.n_dp)
+        straight = [("dp",) + order for order in self.orders]
+        self.routes = {
+            "even": [straight, straight],
+            "late": [straight, [order[:1] + ("dp",) + order[1:] for order in self.orders]],
+            "x": [straight, [("dp",) + self.orders[1]] * 2],
+        }
+
+    def sems(self, route, stage):
+        return sum(len(self.masks) if entry == "dp" else 1 for entry in route[:stage])
 
     def lead(self):
         return (self.n_dp,) + (2,) * self.hops
@@ -178,7 +140,7 @@
     pl.semaphore_wait(barrier, len(others))
 
 
-def reduce_kernel(plan, jobs, first, count, lag, beside, *refs):
+def reduce_kernel(plan, jobs, first, count, lag, routes, beside, *refs):
     k, given = len(jobs), sum(job[3] for job in jobs)
     lefts, rights, refs = iter(refs[:given]), refs[given : given + k], refs[given + k :]
     more = [0, 0, 0] if beside is None else [len(beside.in_specs), len(beside.out_specs), len(beside.scratch)]
@@ -187,63 +149,91 @@
     scratch = refs[1 + more[1] :]
     extra, scratch = extra + scratch[: more[2]], scratch[more[2] :]
     hops, slots = plan.hops, 2 * lag
-    sums = [scratch[h * (hops + 1) : (h + 1) * (hops + 1)] for h in range(2)]
-    scratch = scratch[2 * (hops + 1) :]
-    got = [scratch[h * (hops + 1) : (h + 1) * (hops + 1)] for h in range(2)]
-    send, recv = scratch[2 * (hops + 1) :]
+    stages = hops + 1
+    kinds = 1 if routes[0] == routes[1] else 2
+    sums, got = [], []
+    for h in range(2):
+        more = (kinds - 1, 2 * (kinds - 1))
+        sums.append(scratch[: stages + more[0]])
+        got.append(scratch[stages + more[0] : 2 * stages + sum(more)])
+        scratch = scratch[2 * stages + sum(more) :]
+    send, recv = scratch
     tick = pl.program_id(0)
     half = out_ref.shape[-1] // 2
     rows = out_ref.shape[-2]
-    orders = [order[::-1] for order in plan.orders]
     dp, _ = place()
 
     @pl.when(tick == 0)
     def _():
         greet(plan, getattr(beside, "everyone", False))
 
-    def at_bit(h, stage, value):
-        left = [b for b in plan.bits if b not in orders[h][:stage]]
-        return (slice(None),) + tuple(value if b == orders[h][stage] else slice(None) for b in left)
-
-    def copies(h, stage, slot):
-        kept = lax.rem(slot, lag)
-        if stage < hops:
-            bit = orders[h][stage]
-            at = h * (hops + len(plan.masks)) + stage
+    def sums_at(h, kind, stage, u):
+        if stage < stages - 1 or kinds == 1:
+            return sums[h][stage], lax.rem(u, lag)
+        return sums[h][stage + kind], 0
+
+    def got_at(h, kind, stage, u):
+        if stage < stages - 2 or kinds == 1:
+            return got[h][stage], lax.rem(u, slots)
+        return got[h][stage + 2 * kind], lax.rem(lax.div(u, 2), lag)
+
+    def at_entry(h, kind, stage, value):
+        route = routes[kind][h]
+        left = [d for d in ("dp",) + tuple(plan.bits) if d not in route[:stage]]
+        return tuple(value if d == route[stage] else slice(None) for d in left)
+
+    def own(entry):
+        return dp if entry == "dp" else own_bit(entry)
+
+    def copies(h, kind, stage, u):
+        route = routes[kind][h]
+        entry = route[stage]
+        src, kept = sums_at(h, kind, stage, u)
+        dst, slot = got_at(h, kind, stage, u)
+        at = h * (hops + len(plan.masks)) + plan.sems(route, stage)
+        sem = lax.rem(u, slots)
+        if entry != "dp":
             return [pltpu.make_async_remote_copy(
-                sums[h][stage].at[(kept,) + at_bit(h, stage, 1 - own_bit(bit))], got[h][stage].at[slot],
-                send.at[slot, at], recv.at[slot, at], device_id=partner_seq(bit), device_id_type=MESH)]
-        out = []
-        for n, mask in enumerate(plan.masks):
-            at = h * (hops + len(plan.masks)) + hops + n
-            out.append(pltpu.make_async_remote_copy(
-                sums[h][hops].at[kept, lax.bitwise_xor(dp, mask)], got[h][hops].at[slot, n],
-                send.at[slot, at], recv.at[slot, at], device_id=partner_dp(plan, mask), device_id_type=MESH))
-        return out
+                src.at[(kept,) + at_entry(h, kind, stage, 1 - own(entry))], dst.at[slot],
+                send.at[sem, at], recv.at[sem, at], device_id=partner_seq(entry), device_id_type=MESH)]
+        return [
+            pltpu.make_async_remote_copy(
+                src.at[(kept,) + at_entry(h, kind, stage, lax.bitwise_xor(dp, mask))], dst.at[slot, n],
+                send.at[sem, at + n], recv.at[sem, at + n], device_id=partner_dp(plan, mask), device_id_type=MESH)
+            for n, mask in enumerate(plan.masks)
+        ]
 
     def wide(values):
         return values.astype(jnp.float32)
 
-    for stage in reversed(range(1, hops + 2)):
+    for stage in reversed(range(1, stages + 1)):
         u = tick - first - lag * stage
-
-        @pl.when((u >= 0) & (u < count))
-        def _(stage=stage, u=u):
-            slot, kept = lax.rem(u, slots), lax.rem(u, lag)
-            for h in range(2):
-                for copy in copies(h, stage - 1, slot):
-                    copy.wait()
-                if stage <= hops:
-                    mine = (kept,) + at_bit(h, stage - 1, own_bit(orders[h][stage - 1]))
-                    total = wide(sums[h][stage - 1][mine]) + wide(got[h][stage - 1][slot])
-                    sums[h][stage][kept] = total.astype(jnp.bfloat16)
-                    for copy in copies(h, stage, slot):
+        for kind in range(kinds):
+            due = (u >= 0) & (u < count)
+            if kinds > 1:
+                due = due & (lax.rem(u, 2) == kind)
+
+            @pl.when(due)
+            def _(stage=stage, kind=kind, u=u):
+                for h in range(2):
+                    for copy in copies(h, kind, stage - 1, u):
+                        copy.wait()
+                    entry = routes[kind][h][stage - 1]
+                    src, kept = sums_at(h, kind, stage - 1, u)
+                    dst, slot = got_at(h, kind, stage - 1, u)
+                    total = wide(src[(kept,) + at_entry(h, kind, stage - 1, own(entry))])
+                    if entry == "dp":
+                        for n in range(len(plan.masks)):
+                            total = total + wide(dst[slot, n])
+                    else:
+                        total = total + wide(dst[slot])
+                    if stage == stages:
+                        out_ref[0, :, h * half : (h + 1) * half] = total
+                        continue
+                    to, at = sums_at(h, kind, stage, u)
+                    to[at] = total.astype(jnp.bfloat16)
+                    for copy in copies(h, kind, stage, u):
                         copy.start()
-                else:
-                    total = wide(sums[h][hops][kept, dp])
-                    for n in range(len(plan.masks)):
-                        total = total + wide(got[h][hops][slot, n])
-                    out_ref[0, :, h * half : (h + 1) * half] = total
 
     for (start, stop, cols, has_left), right in zip(jobs, rights):
         if has_left:
@@ -259,7 +249,7 @@
         @pl.when((tick >= first + start) & (tick < first + stop))
         def _(start=start, cols=cols, left_rows=left_rows, right=right):
             u = tick - first
-            slot, kept = lax.rem(u, slots), lax.rem(u, lag)
+            kept = lax.rem(u, lag)
             which = lax.div(u - start, cols)
             for z in range(plan.n_dp):
                 part = dot(left_rows(which, z), right[...]).astype(jnp.bfloat16)
@@ -267,14 +257,14 @@
                     piece = part[:, h * half : (h + 1) * half]
                     sums[h][0][kept, z] = piece.reshape(plan.lead()[1:] + (rows, half))
             for h in range(2):
-                for copy in copies(h, 0, slot):
+                for copy in copies(h, 0, 0, u):
                     copy.start()
 
     if beside is not None:
         beside.run(tick, extra)
 
 
-def reduce_products(plan, pairs, rows, width, lag, collective_id, beside=None, first=0):
+def reduce_products(plan, pairs, rows, width, lag, routes, collective_id, beside=None, first=0):
     jobs, start = [], 0
     left_specs, right_specs = [], []
     for left, right in pairs:
@@ -283,7 +273,7 @@
         stop = start + blocks * cols
         jobs.append((start, stop, cols, left is not blocks))
         if left is not blocks:
-            left_specs.append(pl.BlockSpec(left.shape, lambda t: (0, 0, 0)))
+            left_specs.append(pl.BlockSpec(left.shape, lambda t: (0, 0, 0), pipeline_mode=pl.Buffered(1)))
         right_specs.append(pl.BlockSpec(
             (right.shape[0], width),
             functools.partial(lambda t, start, stop, cols: (0, lax.rem(jnp.clip(t - first, start, stop - 1) - start, cols)),
@@ -293,9 +283,29 @@
     half = width // 2
     slots, hops = 2 * lag, plan.hops
     tail = lag * (hops + 1)
-    sums = [pltpu.VMEM((lag, plan.n_dp) + (2,) * (hops - s) + (rows, half), jnp.bfloat16) for s in range(hops + 1)]
-    got = [pltpu.VMEM((slots, plan.n_dp) + (2,) * (hops - 1 - s) + (rows, half), jnp.bfloat16) for s in range(hops)]
-    got.append(pltpu.VMEM((slots, len(plan.masks), rows, half), jnp.bfloat16))
+    n_dp, masks = plan.n_dp, len(plan.masks)
+    low = jnp.bfloat16
+
+    def room(*shape):
+        return pltpu.VMEM(shape + (rows, half), low)
+
+    routes = [[route[::-1] for route in kind] for kind in plan.routes[routes]]
+
+    def left(kind, stage):
+        return [n_dp if d == "dp" else 2 for d in ("dp",) + tuple(plan.bits) if d not in routes[kind][0][:stage]]
+
+    def arriving(kind, stage):
+        return [masks] * (routes[kind][0][stage] == "dp") + left(kind, stage + 1)
+
+    buffers = []
+    for _ in range(2):
+        if routes[0] == routes[1]:
+            buffers += [room(lag, *left(0, s)) for s in range(hops + 1)]
+            buffers += [room(slots, *arriving(0, s)) for s in range(hops + 1)]
+            continue
+        buffers += [room(lag, *left(0, s)) for s in range(hops)] + [room(1, *left(k, hops)) for k in range(2)]
+        buffers += [room(slots, *arriving(0, s)) for s in range(hops - 1)]
+        buffers += [room(lag, *arriving(k, s)) for k in range(2) for s in (hops - 1, hops)]
     each = 2 * (hops + len(plan.masks))
     out_specs = [pl.BlockSpec((1, rows, width), lambda t: (jnp.clip(t - first - tail, 0, count - 1), 0, 0))]
     out_shapes = [jax.ShapeDtypeStruct((count, rows, width), jnp.float32)]
@@ -304,17 +314,17 @@
         more_in, more_scratch, more_operands = beside.in_specs, beside.scratch, beside.operands
         out_specs, out_shapes = out_specs + beside.out_specs, out_shapes + beside.out_shapes
     return pl.pallas_call(
-        functools.partial(reduce_kernel, plan, jobs, first, count, lag, beside),
+        functools.partial(reduce_kernel, plan, jobs, first, count, lag, routes, beside),
         grid=(max(first + count + tail, 0 if beside is None else beside.ticks),),
         in_specs=left_specs + right_specs + more_in,
         out_specs=out_specs,
         out_shape=out_shapes,
-        scratch_shapes=more_scratch + sums + sums + got + got + [
+        scratch_shapes=more_scratch + buffers + [
             pltpu.SemaphoreType.DMA((slots, each)),
             pltpu.SemaphoreType.DMA((slots, each)),
         ],
         compiler_params=pltpu.CompilerParams(
-            collective_id=collective_id, has_side_effects=True, vmem_limit_bytes=60 << 20),
+            collective_id=collective_id, has_side_effects=True, vmem_limit_bytes=63 << 20),
     )(*[p[0] for p in pairs if not isinstance(p[0], int)], *[p[1] for p in pairs], *more_operands)
 
 
@@ -328,58 +338,54 @@
         return pltpu.make_async_remote_copy(
             src, dst, self.send.at[at], self.recv.at[at], device_id=device, device_id_type=MESH)
 
-    def run(self, pieces, lag):
+    def run(self, pieces, lag, tick=None):
         last = max(start + lag * len(stages) for start, stages in pieces)
-        for tick in range(last + 1):
-            for stage in reversed(range(max(len(stages) for _, stages in pieces) + 1)):
-                for start, stages in pieces:
-                    if start + lag * stage != tick or stage > len(stages):
-                        continue
+        for now in range(min(start for start, _ in pieces), last + 1):
+            due = [
+                (start, stages, stage)
+                for stage in reversed(range(max(len(stages) for _, stages in pieces) + 1))
+                for start, stages in pieces
+                if start + lag * stage == now and stage <= len(stages)
+            ]
+
+            def step(due=due, now=now):
+                for start, stages, stage in due:
                     if stage > 0:
                         for copy in stages[stage - 1][1]:
-                            copy.wait_recv()
+                            copy.wait()
                     if stage < len(stages):
                         ahead, copies = stages[stage]
                         if ahead is not None:
                             ahead()
                         for copy in copies:
                             copy.start()
-        for _, stages in pieces:
-            for _, copies in stages:
-                for copy in copies:
-                    copy.wait_send()
-
-
-def start_kernel(
-    plan, splits, lag, h_ref, s_ref, q_ref, k_ref, v_ref, *refs,
-):
-    n = len(splits)
-    ins, refs = refs[:n], refs[n:]
-    hs_ref, ss_ref, w_ref, outs = refs[0], refs[1], refs[2], refs[3 : 3 + n]
-    hv, wv, halves = refs[3 + n : 6 + n]
-    held = refs[6 + n : 6 + 2 * n]
-    send, recv, local = refs[6 + 2 * n :]
+
+            if tick is None:
+                step()
+            elif due:
+                pl.when(tick == now)(step)
+        return last
+
+
+def arrive(plan, lag, tick, h_ref, s_ref, weights, hs_ref, ss_ref, w_ref, hv, wv, halves, send, recv, local):
     dp, seq = place()
     y, x, c = own_bit(4), own_bit(2), own_bit(1)
     loads = [pltpu.make_async_copy(h_ref.at[y], hv, local.at[0])]
-    loads += [pltpu.make_async_copy(r, wv.at[i], local.at[1 + i]) for i, r in enumerate((q_ref, k_ref, v_ref))]
-    loads += [pltpu.make_async_copy(r, o, local.at[4 + i]) for i, (r, o) in enumerate(zip(ins, held))]
-    for load in loads:
-        load.start()
-    greet(plan)
-    for load in loads:
-        load.wait()
+    loads += [pltpu.make_async_copy(r, wv.at[i], local.at[1 + i]) for i, r in enumerate(weights)]
     own = pltpu.make_async_copy(hv, hs_ref.at[y, x, c], local.at[0])
-    own.start()
-    named = pltpu.make_async_copy(s_ref.at[y], ss_ref.at[y, x, c], local.at[4 + n])
-    named.start()
-    me = (y, x, c)
-    keeps = [pltpu.make_async_copy(o, d.at[(dp,) + me], local.at[4 + i]) for i, (o, d) in enumerate(zip(held, outs))]
-    for keep in keeps:
-        keep.start()
+    named = pltpu.make_async_copy(s_ref.at[y], ss_ref.at[y, x, c], local.at[4])
+
+    @pl.when(tick == 0)
+    def _():
+        for load in loads:
+            load.start()
+        named.start()
+        for load in loads:
+            load.wait()
+        own.start()
+
     run = Copies(send, recv)
     pieces = []
-
     pieces.append((0, [
         (None, [run.remote(s_ref.at[1 - y], ss_ref.at[y, x, c], partner_seq(4))]),
         (named.wait, [run.remote(ss_ref.at[:, x, c], ss_ref.at[:, x, c], partner_seq(2))]),
@@ -409,269 +415,98 @@
         to_z = [run.remote(w_ref.at[i, dp, y], w_ref.at[i, dp, y], partner_dp(plan, m)) for m in plan.masks]
         to_y = [run.remote(w_ref.at[i, :, y], w_ref.at[i, :, y], partner_seq(4))]
         pieces.append((i, [(None, to_x), (cut, to_core), (mine.wait, to_z), (None, to_y)]))
-
-    tick = parts
-    for src, dst, keep, (count, size) in zip(held, outs, keeps, splits):
-        for j in range(count):
-            stages = []
-            for stage in range(plan.hops + 1):
-                copies = []
-                for h in range(2):
-                    cols = pl.ds(j * size + h * (size // 2), size // 2)
-                    if stage == 0:
-                        for m in plan.masks:
-                            copies.append(run.remote(
-                                src.at[:, cols], dst.at[(dp,) + me + (slice(None), cols)], partner_dp(plan, m)))
-                    else:
-                        order = plan.orders[h]
-                        where = tuple(slice(None) if b in order[: stage - 1] else m for b, m in zip(plan.bits, me))
-                        part = dst.at[(slice(None),) + where + (slice(None), cols)]
-                        copies.append(run.remote(part, part, partner_seq(order[stage - 1])))
-                stages.append((keep.wait if stage == 1 and j == 0 else None, copies))
-            pieces.append((tick, stages))
-            tick += 1
-    run.run(pieces, lag)
-
-
-def start(plan, acts, segments, weights, whole, piece, lag, collective_id):
-    groups, columns, width = acts.shape
-    rows = weights[0].shape[0]
-    quarter = width // 4
-    splits, copies = [], 3 + 4 * 3 + 3 * (3 + len(plan.masks))
-    for a in whole:
-        count = max(1, a.shape[1] // piece)
-        while a.shape[1] % (256 * count):
-            count -= 1
-        splits.append((count, a.shape[1] // count))
-        copies += count * 2 * (len(plan.masks) + plan.hops)
-    hbm = pl.BlockSpec(memory_space=pl.ANY)
-    outs = pl.pallas_call(
-        functools.partial(start_kernel, plan, splits, lag),
-        out_shape=[
-            jax.ShapeDtypeStruct((2, 2, 2, columns, width), acts.dtype),
-            jax.ShapeDtypeStruct((2, 2, 2, 1, columns), jnp.int32),
-            jax.ShapeDtypeStruct((3,) + plan.lead() + (rows, quarter), acts.dtype),
-        ] + [jax.ShapeDtypeStruct(plan.lead() + a.shape, a.dtype) for a in whole],
-        in_specs=[hbm] * (5 + len(whole)),
-        out_specs=[hbm] * (3 + len(whole)),
-        scratch_shapes=[
-            pltpu.VMEM((columns, width), acts.dtype),
-            pltpu.VMEM((3, rows, width), acts.dtype),
-            pltpu.VMEM((3, 2, rows, width // 2), acts.dtype),
-        ] + [pltpu.VMEM(a.shape, a.dtype) for a in whole] + [
-            pltpu.SemaphoreType.DMA((copies,)),
-            pltpu.SemaphoreType.DMA((copies,)),
-            pltpu.SemaphoreType.DMA((5 + len(whole),)),
-        ],
-        compiler_params=pltpu.CompilerParams(
-            collective_id=collective_id, has_side_effects=True, vmem_limit_bytes=32 << 20),
-    )(acts, segments[:, None, :], *weights, *whole)
-    tokens, ids, projections = outs[:3]
-    return (
-        tokens.reshape(8, columns, width),
-        ids.reshape(8 * columns),
-        projections.reshape(3, width, quarter),
-        [o.reshape(-1, o.shape[-1]) for o in outs[3:]],
-    )
-
-
-def finish_kernel(
-    plan, parts, g_any, t_any, w_any, x_any, gx_any, gain_ref, more_ref,
-    dx_ref, dw_ref, dn_ref,
-    g_ref, t_ref, w_ref, x_ref, gx_ref,
-    made, made_y, sum_y, made_z, sum_z, sides, made_x,
-    acts, acts_c, sum_c, acts_x, sum_x, acts_y,
-    totals, norms, norms_c, norms_sc, norms_x, norms_sx, norms_y, norms_sy, norms_z,
-    send, recv, local,
-):
-    dp, _ = place()
-    y, x, c = own_bit(4), own_bit(2), own_bit(1)
-    loads = [
-        pltpu.make_async_copy(src, dst, local.at[i])
-        for i, (src, dst) in enumerate(
-            ((g_any, g_ref), (w_any, w_ref), (t_any, t_ref), (x_any, x_ref), (gx_any, gx_ref)))
-    ]
-    for load in loads:
-        load.start()
-    greet(plan)
-    for load in loads[:2]:
-        load.wait()
-    run = Copies(send, recv)
-    columns, width = x_ref.shape[1:]
-    quarter = w_ref.shape[2]
-    half = 2 * quarter
-    rows = dw_ref.shape[1]
-    size = columns // parts
-    low = jnp.bfloat16
-
-    def wide(values):
-        return values.astype(jnp.float32)
-
-    def product(i):
-        def go():
-            if i == 0:
-                loads[2].wait()
-            step = 8 * rows
-            for z in range(plan.n_dp):
-                part = dot(t_ref[z * step : (z + 1) * step, :], g_ref[i])
-                made[i, z] = part.astype(low).reshape(2, 2, 2, rows, quarter)
-        return go
-
-    def product_y(i):
-        def go():
-            sum_y[i] = (wide(made[i, :, y]) + wide(made_y[i])).astype(low)
-        return go
-
-    def product_z(i):
-        def go():
-            total = wide(sum_y[i, dp])
-            for n in range(len(plan.masks)):
-                total = total + wide(made_z[i, n])
-            sum_z[i] = total.astype(low)
-        return go
-
-    def product_c(i):
-        def go():
-            sides[i, :, :, pl.ds(pl.multiple_of(c * quarter, 128), quarter)] = sum_z[i, :, c]
-        return go
-
-    def product_x(i):
-        def go():
-            dw_ref[i, :, pl.ds(pl.multiple_of(x * half, 128), half)] = wide(sides[i, x])
-            dw_ref[i, :, pl.ds(pl.multiple_of((1 - x) * half, 128), half)] = wide(made_x[i])
-        return go
-
-    def back(i):
-        def go():
-            pieces = [g_ref[k].reshape(8, columns, quarter)[:, i * size : (i + 1) * size].reshape(8 * size, quarter)
-                      for k in range(3)]
-            step = 512
-            for n in range(width // step):
-                total = sum(dot(pieces[k], w_ref[k, n * step : (n + 1) * step, :], NT) for k in range(3))
-                acts[i, :, :, :, :, n * step : (n + 1) * step] = total.astype(low).reshape(2, 2, 2, size, step)
-        return go
-
-    def back_c(i):
-        def go():
-            sum_c[i] = (wide(acts[i, :, :, c]) + wide(acts_c[i])).astype(low)
-        return go
-
-    def back_x(i):
-        def go():
-            sum_x[i] = (wide(sum_c[i, :, x]) + wide(acts_x[i])).astype(low)
-        return go
-
-    def norm_back(i):
-        def go():
-            if i == 0:
-                for load in loads[3:]:
-                    load.wait()
-                totals[...] = jnp.zeros_like(totals)
-            gain = gain_ref[...]
-            for s in range(2):
-                mine = wide(sum_x[i, s])
-                grad = jnp.where(y == s, mine, wide(acts_y[i]))
-                at = pl.ds(i * size, size)
-                values = x_ref[s, at]
-                centre = values - jnp.mean(values, axis=-1, keepdims=True)
-                spread = lax.rsqrt(jnp.mean(centre * centre, axis=-1, keepdims=True) + EPSILON)
-                normed = centre * spread
-                grown = grad * gain
-                mean_one = jnp.mean(grown, axis=-1, keepdims=True)
-                mean_two = jnp.mean(grown * normed, axis=-1, keepdims=True)
-                dx_ref[s, at] = gx_ref[s, at] + (grown - mean_one - normed * mean_two) * spread
-                totals[0:1] += jnp.sum(grad * normed, axis=0, keepdims=True)
-                totals[1:2] += jnp.sum(grad, axis=0, keepdims=True)
-        return go
-
-    pieces = []
-    for i in range(parts):
-        pieces.append((i if i < 2 else 2 * i - 1, [
-            (back(i), [run.remote(acts.at[i, :, :, 1 - c], acts_c.at[i], partner_seq(1))]),
-            (back_c(i), [run.remote(sum_c.at[i, :, 1 - x], acts_x.at[i], partner_seq(2))]),
-            (back_x(i), [run.remote(sum_x.at[i, 1 - y], acts_y.at[i], partner_seq(4))]),
-            (norm_back(i), []),
-        ]))
-    for i in range(3):
-        pieces.append((2 * i + 2, [
-            (product(i), [run.remote(made.at[i, :, 1 - y], made_y.at[i], partner_seq(4))]),
-            (product_y(i), [
-                run.remote(sum_y.at[i, lax.bitwise_xor(dp, m)], made_z.at[i, n], partner_dp(plan, m))
-                for n, m in enumerate(plan.masks)]),
-            (product_z(i), [run.remote(
-                sum_z.at[i, :, 1 - c], sides.at[i, :, :, pl.ds(c * quarter, quarter)], partner_seq(1))]),
-            (product_c(i), [run.remote(sides.at[i, 1 - x], made_x.at[i], partner_seq(2))]),
-            (product_x(i), []),
-        ]))
-
-    def norms_start():
-        totals[2:4] = more_ref[...]
-        turned = totals[...].T.astype(low)
-        norms[...] = turned.reshape(norms.shape)
-
-    def norms_add(total, kept, got):
-        def go():
-            total[...] = (wide(kept()) + wide(got[...])).astype(low)
-        return go
-
-    def norms_end():
-        total = wide(norms_sy[dp])
-        for n in range(len(plan.masks)):
-            total = total + wide(norms_z[n])
-        dn_ref[...] = total
-
-    end = max(start + 2 * (len(stages) - 1) for start, stages in pieces if len(stages) == 4) + 1
-    pieces.append((end, [
-        (norms_start, [run.remote(norms.at[:, :, :, 1 - c], norms_c, partner_seq(1))]),
-        (norms_add(norms_sc, lambda: norms[:, :, :, c], norms_c), [run.remote(norms_sc.at[:, :, 1 - x], norms_x, partner_seq(2))]),
-        (norms_add(norms_sx, lambda: norms_sc[:, :, x], norms_x), [run.remote(norms_sx.at[:, 1 - y], norms_y, partner_seq(4))]),
-        (norms_add(norms_sy, lambda: norms_sx[:, y], norms_y), [
-            run.remote(norms_sy.at[lax.bitwise_xor(dp, m)], norms_z.at[n], partner_dp(plan, m))
-            for n, m in enumerate(plan.masks)]),
-        (norms_end, []),
-    ]))
-    run.run(pieces, 2)
-
-
-def finish(plan, grads, turned, weights, inputs, grad_first, gain, more, collective_id):
-    _, columns, width = inputs.shape
-    quarter = weights.shape[2]
-    n_dp, masks = plan.n_dp, len(plan.masks)
-    rows = width // (8 * n_dp)
-    parts = 4
-    size = columns // parts
-    low = jnp.bfloat16
-    hbm = pl.BlockSpec(memory_space=pl.ANY)
-    vmem = pl.BlockSpec(memory_space=pltpu.VMEM)
-    copies = 3 * (3 + masks) + 3 * parts + 3 + masks
-    return pl.pallas_call(
-        functools.partial(finish_kernel, plan, parts),
-        out_shape=[
+    run.run(pieces, ARRIVE_LAG, tick)
+
+
+ARRIVE_LAG = 2
+ARRIVED = max(3 + 3 * ARRIVE_LAG, 2 + 4 * ARRIVE_LAG)
+
+
+class Finish:
+    def __init__(
+        self, plan, first, packed, grads, mixed_t, lse, seg_col, seg_row, cosine, sine, turned, weights, inputs, grad_first, gain, more
+    ):
+        count, per, _, columns, _ = packed.shape
+        length = count * columns
+        self.plan, self.first = plan, first
+        self.block = seg_row.shape[1]
+        self.steps, self.parts = length // self.block, self.block // columns
+        self.count = per * self.steps
+        self.begin = first + self.count
+        self.split = 4
+        self.operands = (
+            packed, packed, packed, grads, mixed_t, lse, seg_col, seg_row, cosine, sine, turned, weights, inputs, grad_first, gain, more
+        )
+        width, quarter = turned.shape[0], weights.shape[2]
+        n_dp, masks = plan.n_dp, len(plan.masks)
+        rows = width // (8 * n_dp)
+        size = columns // self.split
+        low = jnp.bfloat16
+
+        def pair(t):
+            return lax.div(jnp.clip(t - first, 0, self.count - 1), self.steps)
+
+        def step(t):
+            return lax.rem(jnp.clip(t - first, 0, self.count - 1), self.steps)
+
+        def whole(which):
+            return pl.BlockSpec(
+                (count, None, None, columns, HEAD_DIM), lambda t: (0, pair(t), which, 0, 0), pipeline_mode=pl.Buffered(1))
+
+        def fixed(shape):
+            return pl.BlockSpec(shape, lambda t: (0,) * len(shape), pipeline_mode=pl.Buffered(1))
+
+        hbm = pl.BlockSpec(memory_space=pl.ANY)
+        self.in_specs = [
+            whole(0),
+            whole(1),
+            whole(2),
+            pl.BlockSpec((count, None, columns, HEAD_DIM), lambda t: (0, pair(t), 0, 0), pipeline_mode=pl.Buffered(1)),
+            pl.BlockSpec((1, 1, HEAD_DIM, self.block), lambda t: (pair(t), step(t), 0, 0)),
+            pl.BlockSpec((1, self.steps, self.block), lambda t: (pair(t), 0, 0)),
+            fixed((length, 1)),
+            fixed((self.steps, self.block)),
+            fixed((length, HEAD_DIM)),
+            fixed((length, HEAD_DIM)),
+            hbm,
+            hbm,
+            hbm,
+            hbm,
+            fixed((1, width)),
+            fixed((8, width)),
+        ]
+        self.out_specs = [
+            hbm,
+            pl.BlockSpec((3, rows, width), lambda t: (0, 0, 0)),
+            pl.BlockSpec((rows, 128), lambda t: (0, 0)),
+        ]
+        self.out_shapes = [
             jax.ShapeDtypeStruct(inputs.shape, jnp.float32),
             jax.ShapeDtypeStruct((3, rows, width), jnp.float32),
             jax.ShapeDtypeStruct((rows, 128), jnp.float32),
-        ],
-        in_specs=[hbm] * 5 + [vmem] * 2,
-        out_specs=[vmem] * 3,
-        scratch_shapes=[
-            pltpu.VMEM(grads.shape, low),
+        ]
+        self.copies = 3 * (3 + masks) + 3 * self.split + 3 + masks
+        self.scratch = [
+            pltpu.VMEM((HEAD_DIM, length), low),
+            pltpu.VMEM((length, HEAD_DIM), jnp.float32),
+            pltpu.VMEM((length, HEAD_DIM), jnp.float32),
+            pltpu.VMEM((3, length, quarter), low),
             pltpu.VMEM(turned.shape, low),
             pltpu.VMEM(weights.shape, low),
-            pltpu.VMEM(inputs.shape, jnp.float32),
-            pltpu.VMEM(inputs.shape, jnp.float32),
-            pltpu.VMEM((3, n_dp, 2, 2, 2, rows, quarter), low),
-            pltpu.VMEM((3, n_dp, 2, 2, rows, quarter), low),
+            pltpu.VMEM((2, 2, size, width), jnp.float32),
+            pltpu.VMEM((2, 2, size, width), jnp.float32),
+            pltpu.VMEM((2, n_dp, 2, 2, 2, rows, quarter), low),
             pltpu.VMEM((3, n_dp, 2, 2, rows, quarter), low),
             pltpu.VMEM((3, masks, 2, 2, rows, quarter), low),
             pltpu.VMEM((3, 2, 2, rows, quarter), low),
             pltpu.VMEM((3, 2, rows, 2 * quarter), low),
             pltpu.VMEM((3, rows, 2 * quarter), low),
-            pltpu.VMEM((parts, 2, 2, 2, size, width), low),
-            pltpu.VMEM((parts, 2, 2, size, width), low),
-            pltpu.VMEM((parts, 2, 2, size, width), low),
-            pltpu.VMEM((parts, 2, size, width), low),
-            pltpu.VMEM((parts, 2, size, width), low),
-            pltpu.VMEM((parts, size, width), low),
+            pltpu.VMEM((2, 2, 2, 2, size, width), low),
+            pltpu.VMEM((2, 2, 2, size, width), low),
+            pltpu.VMEM((2, 2, 2, size, width), low),
+            pltpu.VMEM((2, 2, size, width), low),
+            pltpu.VMEM((2, 2, size, width), low),
+            pltpu.VMEM((2, size, width), low),
             pltpu.VMEM((128, width), jnp.float32),
             pltpu.VMEM((n_dp, 2, 2, 2, rows, 128), low),
             pltpu.VMEM((n_dp, 2, 2, rows, 128), low),
@@ -681,18 +516,234 @@
             pltpu.VMEM((n_dp, rows, 128), low),
             pltpu.VMEM((n_dp, rows, 128), low),
             pltpu.VMEM((masks, rows, 128), low),
-            pltpu.SemaphoreType.DMA((copies,)),
-            pltpu.SemaphoreType.DMA((copies,)),
-            pltpu.SemaphoreType.DMA((5,)),
-        ],
-        compiler_params=pltpu.CompilerParams(
-            collective_id=collective_id, has_side_effects=True, vmem_limit_bytes=62 << 20),
-    )(grads, turned, weights, inputs, grad_first, gain, more)
+            pltpu.SemaphoreType.DMA((self.copies,)),
+            pltpu.SemaphoreType.DMA((self.copies,)),
+            pltpu.SemaphoreType.DMA((2,)),
+            pltpu.SemaphoreType.DMA((2, 3)),
+        ]
+        backs, products = [2 * i for i in range(self.split)], [(i - per + 1) * self.steps for i in range(per)]
+        self.starts = backs, products
+        self.last_norm = backs[-1] + 2 * 3 + 1
+        self.ticks = self.begin + self.last_norm + 2 * 4 + 1
+
+    def run(self, tick, refs):
+        ins, (dx_ref, dw_ref, dn_ref), scratch = refs[:16], refs[16:19], refs[19:]
+        turned_any, weights_any, inputs_any, first_any, gain_ref, more_ref = ins[10:16]
+        kt_ref, dk_ref, dv_ref, g_ref, t_ref, w_ref, x_ref, gx_ref = scratch[:8]
+        made, made_y, made_z, sum_z, sides, made_x = scratch[8:14]
+        acts, acts_c, sum_c, acts_x, sum_x, acts_y = scratch[14:20]
+        totals, norms, norms_c, norms_sc, norms_x, norms_sx, norms_y, norms_sy, norms_z = scratch[20:29]
+        send, recv, local, chunked = scratch[29:]
+        plan, parts = self.plan, self.split
+        dp, _ = place()
+        y, x, c = own_bit(4), own_bit(2), own_bit(1)
+        width, length = t_ref.shape
+        quarter = w_ref.shape[2]
+        columns = length // 8
+        half = 2 * quarter
+        rows = dw_ref.shape[1]
+        size = columns // parts
+        low = jnp.bfloat16
+        loads = [
+            pltpu.make_async_copy(weights_any, w_ref, local.at[0]),
+            pltpu.make_async_copy(turned_any, t_ref, local.at[1]),
+        ]
+
+        @pl.when(tick == 1)
+        def _():
+            for load in loads:
+                load.start()
+
+        @pl.when((tick >= self.first) & (tick < self.begin))
+        def _():
+            pair, step = lax.div(tick - self.first, self.steps), lax.rem(tick - self.first, self.steps)
+            attend_back_step(self.block, self.parts, pair, step, self.steps - 1, *ins[:10], g_ref, kt_ref, dk_ref, dv_ref)
+
+        masks = len(plan.masks)
+        now = tick - self.begin
+
+        def wide(values):
+            return values.astype(jnp.float32)
+
+        def stream(starts, stages, base, most):
+            gap = starts[1] - starts[0]
+            for stage in reversed(range(len(stages))):
+                since = now - starts[0] - 2 * stage
+                i = lax.div(since, gap)
+
+                @pl.when((since >= 0) & (since <= starts[-1] - starts[0]) & (lax.rem(since, gap) == 0))
+                def _(stage=stage, i=i):
+                    def made_copies(n):
+                        at = base + i * most + sum(len(c(0)) for _, c in stages[:n])
+                        return [
+                            pltpu.make_async_remote_copy(
+                                src, dst, send.at[at + k], recv.at[at + k], device_id=other, device_id_type=MESH)
+                            for k, (src, dst, other) in enumerate(stages[n][1](i))
+                        ]
+
+                    if stage > 0:
+                        for copy in made_copies(stage - 1):
+                            copy.wait()
+                    stages[stage][0](i)
+                    for copy in made_copies(stage):
+                        copy.start()
+
+        def product(i):
+            @pl.when(i == 0)
+            def _():
+                loads[1].wait()
+
+            step = 8 * rows
+            for z in range(plan.n_dp):
+                part = dot(t_ref[z * step : (z + 1) * step, :], g_ref[i])
+                made[lax.rem(i, 2), z] = part.astype(low).reshape(2, 2, 2, rows, quarter)
+
+        def product_y(i):
+            made_y[i] = (wide(made[lax.rem(i, 2), :, y]) + wide(made_y[i])).astype(low)
+
+        def product_z(i):
+            total = wide(made_y[i, dp])
+            for n in range(masks):
+                total = total + wide(made_z[i, n])
+            sum_z[i] = total.astype(low)
+
+        def product_c(i):
+            sides[i, :, :, pl.ds(pl.multiple_of(c * quarter, 128), quarter)] = sum_z[i, :, c]
+
+        def product_x(i):
+            for side, values in ((x, sides.at[i, x]), (1 - x, made_x.at[i])):
+                for core in range(2):
+                    for kind in range(3):
+                        start = core * quarter + kind * HEAD_DIM
+                        lanes = pl.ds(pl.multiple_of(side * half + core * quarter + i * HEAD_DIM, HEAD_DIM), HEAD_DIM)
+                        dw_ref[kind, :, lanes] = wide(values[:, start : start + HEAD_DIM])
+
+        def back(i):
+            @pl.when(i == 0)
+            def _():
+                loads[0].wait()
+
+            slot = lax.rem(i, 2)
+            pieces = []
+            for k in range(3):
+                blocks = []
+                for n in range(8):
+                    at = pl.ds(pl.multiple_of(n * columns + i * size, size), size)
+                    blocks.append(jnp.concatenate(
+                        [g_ref[p, at, k * HEAD_DIM : (k + 1) * HEAD_DIM] for p in range(3)], axis=1))
+                pieces.append(jnp.concatenate(blocks, axis=0))
+            step = 512
+            for n in range(width // step):
+                total = sum(dot(pieces[k], w_ref[k, n * step : (n + 1) * step, :], NT) for k in range(3))
+                acts[slot, :, :, :, :, n * step : (n + 1) * step] = total.astype(low).reshape(2, 2, 2, size, step)
+
+        def back_c(i):
+            slot = lax.rem(i, 2)
+            sum_c[slot] = (wide(acts[slot, :, :, c]) + wide(acts_c[slot])).astype(low)
+
+        def chunk(i):
+            slot, at = lax.rem(i, 2), pl.ds(pl.multiple_of(i * size, size), size)
+            return [
+                pltpu.make_async_copy(inputs_any.at[:, at], x_ref.at[slot], chunked.at[slot, 0]),
+                pltpu.make_async_copy(first_any.at[:, at], gx_ref.at[slot], chunked.at[slot, 1]),
+            ]
+
+        def chunk_out(i):
+            slot, at = lax.rem(i, 2), pl.ds(pl.multiple_of(i * size, size), size)
+            return pltpu.make_async_copy(gx_ref.at[slot], dx_ref.at[:, at], chunked.at[slot, 2])
+
+        def back_x(i):
+            slot = lax.rem(i, 2)
+
+            @pl.when(i >= 2)
+            def _():
+                chunk_out(i - 2).wait()
+
+            for load in chunk(i):
+                load.start()
+            sum_x[slot] = (wide(sum_c[slot, :, x]) + wide(acts_x[slot])).astype(low)
+
+        def norm_back(i):
+            slot = lax.rem(i, 2)
+            for load in chunk(i):
+                load.wait()
+
+            @pl.when(i == 0)
+            def _():
+                totals[...] = jnp.zeros_like(totals)
+
+            gain = gain_ref[...]
+
+            def one(s, carry):
+                grad = jnp.where(y == s, wide(sum_x[slot, s]), wide(acts_y[slot]))
+                values = x_ref[slot, s]
+                centre = values - jnp.mean(values, axis=-1, keepdims=True)
+                spread = lax.rsqrt(jnp.mean(centre * centre, axis=-1, keepdims=True) + EPSILON)
+                normed = centre * spread
+                grown = grad * gain
+                mean_one = jnp.mean(grown, axis=-1, keepdims=True)
+                mean_two = jnp.mean(grown * normed, axis=-1, keepdims=True)
+                gx_ref[slot, s] = gx_ref[slot, s] + (grown - mean_one - normed * mean_two) * spread
+                totals[0:1] += jnp.sum(grad * normed, axis=0, keepdims=True)
+                totals[1:2] += jnp.sum(grad, axis=0, keepdims=True)
+                return carry
+
+            lax.fori_loop(0, 2, one, 0)
+            chunk_out(i).start()
+
+        stream(self.starts[0], [
+            (back, lambda i: [(acts.at[lax.rem(i, 2), :, :, 1 - c], acts_c.at[lax.rem(i, 2)], partner_seq(1))]),
+            (back_c, lambda i: [(sum_c.at[lax.rem(i, 2), :, 1 - x], acts_x.at[lax.rem(i, 2)], partner_seq(2))]),
+            (back_x, lambda i: [(sum_x.at[lax.rem(i, 2), 1 - y], acts_y.at[lax.rem(i, 2)], partner_seq(4))]),
+            (norm_back, lambda i: []),
+        ], 0, 3)
+        stream(self.starts[1], [
+            (product, lambda i: [(made.at[lax.rem(i, 2), :, 1 - y], made_y.at[i], partner_seq(4))]),
+            (product_y, lambda i: [
+                (made_y.at[i, lax.bitwise_xor(dp, m)], made_z.at[i, n], partner_dp(plan, m))
+                for n, m in enumerate(plan.masks)]),
+            (product_z, lambda i: [
+                (sum_z.at[i, :, 1 - c], sides.at[i, :, :, pl.ds(c * quarter, quarter)], partner_seq(1))]),
+            (product_c, lambda i: [(sides.at[i, 1 - x], made_x.at[i], partner_seq(2))]),
+            (product_x, lambda i: []),
+        ], 3 * parts, 3 + masks)
+        run = Copies(send, recv)
+        run.count = 3 * parts + 3 * (3 + masks)
+        pieces = []
+
+        def norms_start():
+            totals[2:4] = more_ref[0:2]
+            norms[...] = totals[...].T.astype(low).reshape(norms.shape)
+
+        def norms_add(total, kept, got):
+            def go():
+                total[...] = (wide(kept()) + wide(got[...])).astype(low)
+            return go
+
+        def norms_end():
+            total = wide(norms_sy[dp])
+            for n in range(len(plan.masks)):
+                total = total + wide(norms_z[n])
+            dn_ref[...] = total
+            for i in range(parts - 2, parts):
+                chunk_out(i).wait()
+
+        pieces.append((self.last_norm, [
+            (norms_start, [run.remote(norms.at[:, :, :, 1 - c], norms_c, partner_seq(1))]),
+            (norms_add(norms_sc, lambda: norms[:, :, :, c], norms_c), [run.remote(norms_sc.at[:, :, 1 - x], norms_x, partner_seq(2))]),
+            (norms_add(norms_sx, lambda: norms_sc[:, :, x], norms_x), [run.remote(norms_sx.at[:, 1 - y], norms_y, partner_seq(4))]),
+            (norms_add(norms_sy, lambda: norms_sx[:, y], norms_y), [
+                run.remote(norms_sy.at[lax.bitwise_xor(dp, m)], norms_z.at[n], partner_dp(plan, m))
+                for n, m in enumerate(plan.masks)]),
+            (norms_end, []),
+        ]))
+        run.run(pieces, 2, now)
 
 
 class Gather:
-    def __init__(self, plan, lag, shard, rows, cols):
+    def __init__(self, plan, lag, shard, rows, cols, routes):
         self.plan, self.lag, self.rows, self.cols = plan, lag, rows, cols
+        self.routes = plan.routes[routes]
         self.across = shard.shape[1] // cols
         self.pieces = shard.shape[0] // rows * self.across
         self.ticks = self.pieces + lag * (plan.hops + 1)
@@ -705,31 +756,26 @@
             pltpu.SemaphoreType.DMA((2,)),
         ]
 
-    def copies(self, stage, u, full, held, send, recv):
+    def copies(self, kind, stage, u, full, held, send, recv):
         plan = self.plan
         dp, _ = place()
-        me = tuple(own_bit(b) for b in plan.bits)
         slot = lax.rem(u, 2 * self.lag)
         rows = pl.ds(pl.multiple_of(lax.div(u, self.across) * self.rows, 16), self.rows)
         out = []
         for h in range(2):
             start = lax.rem(u, self.across) * self.cols + h * (self.cols // 2)
             cols = pl.ds(pl.multiple_of(start, 128), self.cols // 2)
-            base = h * (len(plan.masks) + plan.hops)
-            if stage == 0:
-                for n, mask in enumerate(plan.masks):
-                    out.append(pltpu.make_async_remote_copy(
-                        held.at[rows, cols], full.at[(dp,) + me + (rows, cols)],
-                        send.at[slot, base + n], recv.at[slot, base + n],
-                        device_id=partner_dp(plan, mask), device_id_type=MESH))
-            else:
-                order = plan.orders[h]
-                where = tuple(slice(None) if b in order[: stage - 1] else m for b, m in zip(plan.bits, me))
-                part = full.at[(slice(None),) + where + (rows, cols)]
-                at = base + len(plan.masks) + stage - 1
+            route = self.routes[kind][h]
+            entry, done = route[stage], route[:stage]
+            where = (slice(None) if "dp" in done else dp,)
+            where += tuple(slice(None) if b in done else own_bit(b) for b in plan.bits)
+            part = full.at[where + (rows, cols)]
+            src = part if stage else held.at[rows, cols]
+            at = h * (len(plan.masks) + plan.hops) + plan.sems(route, stage)
+            others = [partner_dp(plan, m) for m in plan.masks] if entry == "dp" else [partner_seq(entry)]
+            for n, other in enumerate(others):
                 out.append(pltpu.make_async_remote_copy(
-                    part, part, send.at[slot, at], recv.at[slot, at],
-                    device_id=partner_seq(order[stage - 1]), device_id_type=MESH))
+                    src, part, send.at[slot, at + n], recv.at[slot, at + n], device_id=other, device_id_type=MESH))
         return out
 
     def run(self, tick, shard, full, held, send, recv, local):
@@ -752,15 +798,17 @@
         stages = plan.hops + 1
         for stage in reversed(range(stages + 1)):
             u = tick - lag * stage
-
-            @pl.when((u >= 0) & (u < self.pieces))
-            def _(stage=stage, u=u):
-                if stage > 0:
-                    for copy in self.copies(stage - 1, u, full, held, send, recv):
-                        copy.wait()
-                if stage < stages:
-                    for copy in self.copies(stage, u, full, held, send, recv):
-                        copy.start()
+            kinds = 1 if self.routes[0] == self.routes[1] else 2
+            for kind in range(kinds):
+
+                @pl.when((u >= 0) & (u < self.pieces) & (lax.rem(u, 2) == kind if kinds > 1 else True))
+                def _(stage=stage, u=u, kind=kind):
+                    if stage > 0:
+                        for copy in self.copies(kind, stage - 1, u, full, held, send, recv):
+                            copy.wait()
+                    if stage < stages:
+                        for copy in self.copies(kind, stage, u, full, held, send, recv):
+                            copy.start()
 
 
 def attend_step(block, parts, pair, step, packed, col_ref, row_ref, o_ref, ot_ref, lse_ref, vt_ref):
@@ -799,8 +847,9 @@
 
 
 def attention_kernel(
-    plan, gather, block, first, x_ref, w_ref, cos_ref, sin_ref, col_ref, row_ref, shard,
-    packed, turned_ref, o_ref, ot_ref, lse_ref, full, vt_ref, *more,
+    plan, lag, gathers, block, steps, h_ref, s_ref, q_ref, k_ref, v_ref, cos_ref, sin_ref, out_shard, up_shard,
+    packed, turned_ref, o_ref, ot_ref, lse_ref, col_ref, row_ref, hs_ref, ss_ref, w_ref, full_out, full_up,
+    vt_ref, x_ref, weights_ref, ids_ref, hv, wv, halves, send, recv, local, fetch, *more,
 ):
     tick = pl.program_id(0)
 
@@ -808,44 +857,84 @@
     def _():
         greet(plan)
 
-    gather.run(tick, shard, full, *more)
-    parts, columns, width = x_ref.shape
+    arrive(plan, lag, tick, h_ref, s_ref, (q_ref, k_ref, v_ref), hs_ref, ss_ref, w_ref, hv, wv, halves, send, recv, local)
+    for (first, gather), shard, full, held in zip(
+        gathers, (out_shard, up_shard), (full_out, full_up), (more[:4], more[4:])
+    ):
+        gather.run(tick - first, shard, full, *held)
+    _, parts, columns, width = x_ref.shape
     heads = packed.shape[1]
-
-    @pl.when(tick < first)
+    first = ARRIVED + 1
+
+    def acts_load(i):
+        return pltpu.make_async_copy(hs_ref.at[lax.div(i, 2), lax.rem(i, 2)], x_ref.at[lax.rem(i, 2)], fetch.at[lax.rem(i, 2)])
+
+    weights_load = pltpu.make_async_copy(w_ref, weights_ref, fetch.at[2])
+    ids_load = pltpu.make_async_copy(ss_ref, ids_ref, fetch.at[3])
+
+    @pl.when(tick == ARRIVED)
     def _():
-        acts = x_ref[...].reshape(block, width)
+        ids_load.start()
+        weights_load.start()
+        acts_load(0).start()
+        ids_load.wait()
+        ids = ids_ref[...].reshape(2 * steps, columns)
+        for i in range(2 * steps):
+            row_ref[i // parts : i // parts + 1, (i % parts) * columns : (i % parts + 1) * columns] = ids[i : i + 1]
+        turned = ids.astype(jnp.float32).T.astype(jnp.int32)
+        for i in range(2 * steps):
+            mine = turned[:, i : i + 1]
+            col_ref[i * columns : (i + 1) * columns, :] = jnp.where(mine < 0, -2, mine)
+        weights_load.wait()
+
+    at = tick - first
+
+    @pl.when((at >= 0) & (at < steps))
+    def _():
+        @pl.when(at + 1 < steps)
+        def _():
+            acts_load(at + 1).start()
+
+        acts_load(at).wait()
+        acts = x_ref[lax.rem(at, 2)].reshape(block, width)
         for kind in range(3):
-            made = dot(acts, w_ref[kind])
+            made = dot(acts, weights_ref[kind].reshape(width, heads * HEAD_DIM))
             for p in range(heads):
                 head = made[:, p * HEAD_DIM : (p + 1) * HEAD_DIM]
                 if kind < 2:
                     head = head * cos_ref[...] + pltpu.roll(head, HEAD_DIM // 2, 1) * sin_ref[...]
-                packed[pl.ds(tick * parts, parts), p, kind] = head.astype(jnp.bfloat16).reshape(parts, columns, HEAD_DIM)
+                packed[pl.ds(at * parts, parts), p, kind] = head.astype(jnp.bfloat16).reshape(parts, columns, HEAD_DIM)
         turned_ref[...] = acts.T
 
-    @pl.when((tick >= first) & (tick < first * (1 + heads)))
+    @pl.when((at >= steps) & (at < steps * (1 + heads)))
     def _():
-        pair, step = lax.div(tick - first, first), lax.rem(tick - first, first)
+        pair, step = lax.div(at - steps, steps), lax.rem(at - steps, steps)
         attend_step(block, parts, pair, step, packed, col_ref, row_ref, o_ref, ot_ref, lse_ref, vt_ref)
 
 
-def attention(plan, acts, weights, cosine, sine, seg_col, seg_row, shard, lag, collective_id):
-    owners, columns, width = acts.shape
-    heads = weights.shape[2] // HEAD_DIM
-    steps, block = seg_row.shape
-    parts, length = block // columns, owners * columns
-    gather = Gather(plan, lag, shard, shard.shape[0], 512)
+def attention(plan, acts, segments, weights, cosine, sine, out_shard, up_shard, lag, collective_id):
+    _, columns, width = acts.shape
+    rows = weights[0].shape[0]
+    quarter = width // 4
+    heads = quarter // HEAD_DIM
+    owners = 8
+    length, block = owners * columns, 2 * columns
+    steps, parts = length // block, 2
+    gathers = (
+        (0, Gather(plan, lag, out_shard, out_shard.shape[0], 512, "late")),
+        (3, Gather(plan, lag, up_shard, up_shard.shape[0], 512, "late")),
+    )
     low = jnp.bfloat16
+    begin = ARRIVED + 1
 
     def at(t):
-        return jnp.clip(t, 0, steps - 1)
+        return jnp.clip(t - begin, 0, steps - 1)
 
     def pair(t):
-        return lax.div(jnp.clip(t - steps, 0, steps * heads - 1), steps)
+        return lax.div(jnp.clip(t - begin - steps, 0, steps * heads - 1), steps)
 
     def step(t):
-        return lax.rem(jnp.clip(t - steps, 0, steps * heads - 1), steps)
+        return lax.rem(jnp.clip(t - begin - steps, 0, steps * heads - 1), steps)
 
     def fixed(shape):
         return pl.BlockSpec(shape, lambda t: (0,) * len(shape))
@@ -853,24 +942,27 @@
     hbm = pl.BlockSpec(memory_space=pl.ANY)
     table = pl.BlockSpec((block, HEAD_DIM), lambda t: (at(t), 0))
     packed_shape = (owners, heads, 3, columns, HEAD_DIM)
+    acts_shape = (2, 2, 2, columns, width)
+    ids_shape = (2, 2, 2, 1, columns)
+    weights_shape = (3,) + plan.lead() + (rows, quarter)
+    copies = 3 + 4 * 3 + 3 * (3 + len(plan.masks))
+    ticks = max([begin + steps * (1 + heads)] + [first + gather.ticks for first, gather in gathers])
     return pl.pallas_call(
-        functools.partial(attention_kernel, plan, gather, block, steps),
-        grid=(max(gather.ticks, steps * (1 + heads)),),
-        in_specs=[
-            pl.BlockSpec((parts, columns, width), lambda t: (at(t), 0, 0)),
-            fixed(weights.shape),
-            table,
-            table,
-            fixed((length, 1)),
-            fixed((steps, block)),
-            hbm,
-        ],
+        functools.partial(attention_kernel, plan, lag, gathers, block, steps),
+        grid=(ticks,),
+        in_specs=[hbm] * 5 + [table, table, hbm, hbm],
         out_specs=[
             fixed(packed_shape),
             pl.BlockSpec((width, block), lambda t: (0, at(t))),
             pl.BlockSpec((parts, None, columns, HEAD_DIM), lambda t: (step(t), pair(t), 0, 0)),
             pl.BlockSpec((1, 1, HEAD_DIM, block), lambda t: (pair(t), step(t), 0, 0)),
             pl.BlockSpec((1, steps, block), lambda t: (pair(t), 0, 0)),
+            fixed((length, 1)),
+            fixed((steps, block)),
+            hbm,
+            hbm,
+            hbm,
+            hbm,
             hbm,
         ],
         out_shape=[
@@ -879,12 +971,30 @@
             jax.ShapeDtypeStruct((owners, heads, columns, HEAD_DIM), low),
             jax.ShapeDtypeStruct((heads, steps, HEAD_DIM, block), jnp.float32),
             jax.ShapeDtypeStruct((heads, steps, block), jnp.float32),
-            gather.out_shape,
+            jax.ShapeDtypeStruct((length, 1), jnp.int32),
+            jax.ShapeDtypeStruct((steps, block), jnp.int32),
+            jax.ShapeDtypeStruct(acts_shape, low),
+            jax.ShapeDtypeStruct(ids_shape, jnp.int32),
+            jax.ShapeDtypeStruct(weights_shape, low),
+            gathers[0][1].out_shape,
+            gathers[1][1].out_shape,
         ],
-        scratch_shapes=[pltpu.VMEM((HEAD_DIM, length), low)] + gather.scratch,
+        scratch_shapes=[
+            pltpu.VMEM((HEAD_DIM, length), low),
+            pltpu.VMEM((2, parts, columns, width), low),
+            pltpu.VMEM(weights_shape, low),
+            pltpu.VMEM(ids_shape, jnp.int32),
+            pltpu.VMEM((columns, width), low),
+            pltpu.VMEM((3, rows, width), low),
+            pltpu.VMEM((3, 2, rows, width // 2), low),
+            pltpu.SemaphoreType.DMA((copies,)),
+            pltpu.SemaphoreType.DMA((copies,)),
+            pltpu.SemaphoreType.DMA((5,)),
+            pltpu.SemaphoreType.DMA((4,)),
+        ] + gathers[0][1].scratch + gathers[1][1].scratch,
         compiler_params=pltpu.CompilerParams(
             collective_id=collective_id, has_side_effects=True, vmem_limit_bytes=56 << 20),
-    )(acts, weights, cosine, sine, seg_col, seg_row, shard)
+    )(acts, segments[:, None, :], *weights, cosine, sine, out_shard, up_shard)
 
 
 class Mlp:
@@ -895,7 +1005,7 @@
         self.blocks = 2 * plan.n_dp
         self.block = hidden // self.blocks
         self.rows = width // (plan.n_dp * plan.n_seq)
-        self.gather = Gather(plan, lag, shard, self.rows, 512)
+        self.gather = Gather(plan, lag, shard, self.rows, 512, "even")
         self.meet = 4
         self.up = self.meet + 1
         self.back = max(self.gather.ticks, self.up + self.blocks)
@@ -1449,7 +1559,6 @@
 ):
     groups, columns, width = inputs.shape
     length = columns * plan.n_seq
-    block = min(512, length)
     lag, piece = 2, 512
     every = plan.n_dp * plan.n_seq
 
@@ -1463,23 +1572,18 @@
         return values.reshape(groups * columns, width)
 
     act_one = lower(layer_norm(inputs, norm1_gain, norm1_bias))
-    tokens_one, ids, heads_weight, (full_out,) = start(
-        plan, act_one, segments, (w_query, w_key, w_value), (w_out,), piece, lag, 1
-    )
-    seg_row = ids.reshape(length // block, block)
-    seg_col = jnp.where(ids < 0, -2, ids)[:, None]
-    packed, turned_one, mixed, mixed_t, lse, full_up = attention(
-        plan, tokens_one, heads_weight, cosine, sine, seg_col, seg_row, w_up, lag, 2
+    packed, turned_one, mixed, mixed_t, lse, seg_col, seg_row, _, _, heads_weight, full_out, full_up = attention(
+        plan, act_one, segments, (w_query, w_key, w_value), cosine, sine, w_out, w_up, lag, 1
     )
     grad_low = lower(flat(cotangent))
     mlp = Mlp(
-        plan, lag, mixed, full_out, flat(inputs), norm2_gain[None], norm2_bias[None],
+        plan, lag, mixed, full_out.reshape(width, width), flat(inputs), norm2_gain[None], norm2_bias[None],
         full_up.reshape(width, -1), grad_low, flat(cotangent), w_down,
     )
     rows = width // every
 
-    def reduce_all(pairs, collective_id, beside, first=0):
-        out, *more = reduce_products(plan, pairs, rows, piece, lag, collective_id, beside, first)
+    def reduce_all(pairs, routes, collective_id, beside, first=0):
+        out, *more = reduce_products(plan, pairs, rows, piece, lag, routes, collective_id, beside, first)
         results, at = [], 0
         for left, right in pairs:
             blocks = left if isinstance(left, int) else left.shape[0]
@@ -1492,14 +1596,13 @@
     (
         down_grad, output, _, grad_first, grad_first_low, mixed_turned, acts_turned, grad_upper, grad_pairs,
         sums_two, _,
-    ) = reduce_all([(w_down.shape[0] // rows, grad_low)], 3, mlp, 14)
-    work = AttendBack(2, packed, grad_pairs, mixed_t, lse, seg_col, seg_row, cosine, sine)
-    up_grad, out_grad, grads = reduce_all(
-        [(acts_turned[None], grad_upper), (mixed_turned[None], grad_first_low)], 4, work
-    )
-    grad_input, heads_grad, norm_rows = finish(
-        plan, grads, turned_one, heads_weight, inputs, grad_first.reshape(inputs.shape), norm1_gain[None],
-        sums_two[:2], 5,
+    ) = reduce_all([(w_down.shape[0] // rows, grad_low)], "even", 3, mlp, 14)
+    work = Finish(
+        plan, 0, packed, grad_pairs, mixed_t, lse, seg_col, seg_row, cosine, sine, turned_one,
+        heads_weight.reshape(3, width, -1), inputs, grad_first.reshape(inputs.shape), norm1_gain[None], sums_two,
+    )
+    up_grad, out_grad, grad_input, heads_grad, norm_rows = reduce_all(
+        [(acts_turned[None], grad_upper), (mixed_turned[None], grad_first_low)], "even", 4, work
     )
     return (
         output.reshape(inputs.shape),

time: 648 us -> 599 us (0.924)
  Pallas kernels: 611 us -> 576 us
  local copies, waits for them, and re-layouts: 24.6 us -> 16.1 us
    pallas_call x3 -> x1, Pallas kernels: 296 us -> 180 us  [attention(): pl.pallas_call(functools.partial(attention_kernel, plan, lag, gathers, bl...]
    pallas_call x2, Pallas kernels: 315 us -> 396 us  [reduce_products(): pl.pallas_call(functools.partial(reduce_kernel, plan, jobs, first, count,...]
    unnamed x43 -> x30, local copies, waits for them, and re-layouts: 16.3 us -> 10.1 us
where the time goes in v4:
time: 599 us
  Pallas kernels  576 us (96%)
  local copies, waits for them, and re-layouts  16.1 us (3%)
    pallas_call x2, Pallas kernels, reduce_products(): pl.pallas_call(functools.partial(reduce_kernel, plan, jobs, first, count,...  396 us
    pallas_call x1, Pallas kernels, attention(): pl.pallas_call(functools.partial(attention_kernel, plan, lag, gathers, bl...  180 us

profile of v4, /device:TPU:0, one launch (start us, length us, event | category | flops | bytes accessed | tf_op | source)
XLA Modules:
  0.0 598.6 jit_solution(7554437129576604049)
XLA Ops:
  0.7 2.3 reduce_sum.18
  2.9 0.5 copy-done
  3.5 0.4 multiply_reduce_fusion
  4.0 1.7 add_convert_fusion.h_ref
  5.7 0.6 broadcast_in_dim.22.s_ref
  6.3 179.7 %shard_map.238 = (bf16[8,3,3,256,128]{4,3,2,1,0:T(8,128)(2,1)}, bf16[1536,2048]{1,0:T(8,128)(2,1)}, bf16[8,3,256,128]{3,2,1,0:T(8,128)(2,1)}, f32[3,4,128,512]{3...) custom-call(bf16[2,256,1536]{2,1,0:T(8,128)(2,1)} %add_convert_fusio, ...), custom_call_target="tpu_custom_call" | custom-call | tf_op jit(solution)/shard_map/pallas_call | solution.py:950
  186.1 1.3 bitcast_convert_fusion.refs_0_.refs_7_
  187.4 0.6 broadcast_in_dim.23.refs_4_
  188.0 0.6 broadcast_in_dim.24.refs_5_
  188.6 199.2 %shard_map.239 = (f32[12,48,512]{2,1,0:T(8,128)}, f32[512,1536]{1,0:T(8,128)}, f32[512,1536]{1,0:T(8,128)}, f32[512,1536]{1,0:T(8,128)}, bf16[512,1536]{1,0:T(8,...) custom-call(bf16[512,1536]{1,0:T(8,128)(2,1)} %bitcast_convert_fusio, ...), custom_call_target="tpu_custom_call" | custom-call | tf_op jit(solution)/shard_map/pallas_call | solution.py:316
  387.8 0.6 broadcast_in_dim.27.refs_18_
  388.4 197.0 %shard_map.240 = (f32[15,48,512]{2,1,0:T(8,128)}, f32[2,256,1536]{2,1,0:T(8,128)}, f32[3,48,1536]{2,1,0:T(8,128)}, f32[48,128]{1,0:T(8,128)}) custom-call(bf16[1,1536,512]{2,1,0:T(8,128)(2,1)} %bitcast.48, bf16[1,1536,512]{2,1,0:T(8,128)(2,1)} %bitcast.47, bf16[512,6144]{1,0:T(8,128)(2,1)} %get-tuple-element.41.refs_2_, ...), custom_call_target="tpu_custom_call" | custom-call | tf_op jit(solution)/shard_map/pallas_call | solution.py:316
  585.4 1.4 fusion
  586.8 1.1 copy.32
  588.0 1.0 slice_bitcast_fusion.1
  588.9 0.2 copy.28
  589.1 0.8 copy.31
  590.0 0.9 slice_bitcast_fusion.2
  590.9 0.7 slice_reduce_fusion
  591.6 0.8 copy.30
  592.4 1.5 copy.33
  593.9 1.7 copy.37
  595.6 1.4 copy-done.3
  597.0 1.7 copy.38
  (24 shorter events, 0.1 us)
Async XLA Ops:
  0.6 2.8 copy-start
  0.7 3.3 copy-start.7
  0.7 3.3 copy-start.8
  3.9 1.8 copy-start.11
  5.7 180.4 %copy-start.1 = (f32[2,256,1536]{2,1,0:T(8,128)S(1)}, f32[2,256,1536]{2,1,0:T(8,128)}, u32[]{:S(2)}) copy-start(f32[2,256,1536]{2,1,0:T(8,128)} %param.27) | copy-start | bytes 9437188
  186.0 1.3 copy-start.9
  186.0 1.9 copy-start.10
  585.4 4.6 copy-start.5
  586.8 4.1 copy-start.6
  586.8 4.8 copy-start.4
  590.9 3.0 copy-start.2
  593.9 3.0 copy-start.3

commit v5 on v4

--- a/solution.py
+++ b/solution.py
@@ -103,7 +103,10 @@
         self.routes = {
             "even": [straight, straight],
             "late": [straight, [order[:1] + ("dp",) + order[1:] for order in self.orders]],
-            "x": [straight, [("dp",) + self.orders[1]] * 2],
+            "x late": [
+                [("dp",) + self.orders[1]] * 2,
+                [order[:1] + ("dp",) + order[1:] for order in self.orders],
+            ],
         }
 
     def sems(self, route, stage):
@@ -398,7 +401,7 @@
         first = run.remote(h_ref.at[1 - y, rows], hs_ref.at[y, x, c, rows], partner_seq(4))
         second = [run.remote(hs_ref.at[:, x, c, rows], hs_ref.at[:, x, c, rows], partner_seq(2))]
         third = [run.remote(hs_ref.at[:, :, c, rows], hs_ref.at[:, :, c, rows], partner_seq(1))]
-        pieces.append((i, [(None, [first]), (own.wait if i == 0 else None, second), (None, third)]))
+        pieces.append((ACTS_AT + i, [(None, [first]), (own.wait if i == 0 else None, second), (None, third)]))
 
     half, quarter = halves.shape[-1], w_ref.shape[-1]
     for i in range(3):
@@ -414,15 +417,18 @@
             halves.at[i, :, :, pl.ds((1 - c) * quarter, quarter)], w_ref.at[i, dp, y, :, c], partner_seq(1))]
         to_z = [run.remote(w_ref.at[i, dp, y], w_ref.at[i, dp, y], partner_dp(plan, m)) for m in plan.masks]
         to_y = [run.remote(w_ref.at[i, :, y], w_ref.at[i, :, y], partner_seq(4))]
-        pieces.append((i, [(None, to_x), (cut, to_core), (mine.wait, to_z), (None, to_y)]))
+        pieces.append((WEIGHTS_AT[i], [(None, to_x), (cut, to_core), (mine.wait, to_z), (None, to_y)]))
     run.run(pieces, ARRIVE_LAG, tick)
 
 
 ARRIVE_LAG = 2
-ARRIVED = max(3 + 3 * ARRIVE_LAG, 2 + 4 * ARRIVE_LAG)
+ACTS_AT, WEIGHTS_AT = 2, (0, 2, 3)
+ARRIVED = max(ACTS_AT + 3 + 3 * ARRIVE_LAG, WEIGHTS_AT[-1] + 4 * ARRIVE_LAG)
 
 
 class Finish:
+    everyone = True
+
     def __init__(
         self, plan, first, packed, grads, mixed_t, lse, seg_col, seg_row, cosine, sine, turned, weights, inputs, grad_first, gain, more
     ):
@@ -472,7 +478,7 @@
             hbm,
             hbm,
             hbm,
-            fixed((1, width)),
+            pl.BlockSpec((width,), lambda t: (0,), pipeline_mode=pl.Buffered(1)),
             fixed((8, width)),
         ]
         self.out_specs = [
@@ -485,7 +491,7 @@
             jax.ShapeDtypeStruct((3, rows, width), jnp.float32),
             jax.ShapeDtypeStruct((rows, 128), jnp.float32),
         ]
-        self.copies = 3 * (3 + masks) + 3 * self.split + 3 + masks
+        self.copies = 3 * (3 + masks) + 3 * self.split + 7 + masks
         self.scratch = [
             pltpu.VMEM((HEAD_DIM, length), low),
             pltpu.VMEM((length, HEAD_DIM), jnp.float32),
@@ -509,11 +515,7 @@
             pltpu.VMEM((2, size, width), low),
             pltpu.VMEM((128, width), jnp.float32),
             pltpu.VMEM((n_dp, 2, 2, 2, rows, 128), low),
-            pltpu.VMEM((n_dp, 2, 2, rows, 128), low),
-            pltpu.VMEM((n_dp, 2, 2, rows, 128), low),
-            pltpu.VMEM((n_dp, 2, rows, 128), low),
-            pltpu.VMEM((n_dp, 2, rows, 128), low),
-            pltpu.VMEM((n_dp, rows, 128), low),
+            pltpu.VMEM((7, n_dp, rows, 128), low),
             pltpu.VMEM((n_dp, rows, 128), low),
             pltpu.VMEM((masks, rows, 128), low),
             pltpu.SemaphoreType.DMA((self.copies,)),
@@ -521,10 +523,10 @@
             pltpu.SemaphoreType.DMA((2,)),
             pltpu.SemaphoreType.DMA((2, 3)),
         ]
-        backs, products = [2 * i for i in range(self.split)], [(i - per + 1) * self.steps for i in range(per)]
+        backs, products = [2 * i for i in range(self.split)], [(i - per + 1) * self.steps + 4 for i in range(per)]
         self.starts = backs, products
         self.last_norm = backs[-1] + 2 * 3 + 1
-        self.ticks = self.begin + self.last_norm + 2 * 4 + 1
+        self.ticks = self.begin + max(self.last_norm + 2 * 2, products[-1] + 4 * 4) + 1
 
     def run(self, tick, refs):
         ins, (dx_ref, dw_ref, dn_ref), scratch = refs[:16], refs[16:19], refs[19:]
@@ -532,8 +534,8 @@
         kt_ref, dk_ref, dv_ref, g_ref, t_ref, w_ref, x_ref, gx_ref = scratch[:8]
         made, made_y, made_z, sum_z, sides, made_x = scratch[8:14]
         acts, acts_c, sum_c, acts_x, sum_x, acts_y = scratch[14:20]
-        totals, norms, norms_c, norms_sc, norms_x, norms_sx, norms_y, norms_sy, norms_z = scratch[20:29]
-        send, recv, local, chunked = scratch[29:]
+        totals, norms, norms_c, norms_sy, norms_z = scratch[20:25]
+        send, recv, local, chunked = scratch[25:]
         plan, parts = self.plan, self.split
         dp, _ = place()
         y, x, c = own_bit(4), own_bit(2), own_bit(1)
@@ -565,10 +567,10 @@
         def wide(values):
             return values.astype(jnp.float32)
 
-        def stream(starts, stages, base, most):
+        def stream(starts, stages, lag, base, most):
             gap = starts[1] - starts[0]
             for stage in reversed(range(len(stages))):
-                since = now - starts[0] - 2 * stage
+                since = now - starts[0] - lag * stage
                 i = lax.div(since, gap)
 
                 @pl.when((since >= 0) & (since <= starts[-1] - starts[0]) & (lax.rem(since, gap) == 0))
@@ -672,7 +674,7 @@
             def _():
                 totals[...] = jnp.zeros_like(totals)
 
-            gain = gain_ref[...]
+            gain = gain_ref[...][None]
 
             def one(s, carry):
                 grad = jnp.where(y == s, wide(sum_x[slot, s]), wide(acts_y[slot]))
@@ -696,7 +698,7 @@
             (back_c, lambda i: [(sum_c.at[lax.rem(i, 2), :, 1 - x], acts_x.at[lax.rem(i, 2)], partner_seq(2))]),
             (back_x, lambda i: [(sum_x.at[lax.rem(i, 2), 1 - y], acts_y.at[lax.rem(i, 2)], partner_seq(4))]),
             (norm_back, lambda i: []),
-        ], 0, 3)
+        ], 2, 0, 3)
         stream(self.starts[1], [
             (product, lambda i: [(made.at[lax.rem(i, 2), :, 1 - y], made_y.at[i], partner_seq(4))]),
             (product_y, lambda i: [
@@ -706,7 +708,7 @@
                 (sum_z.at[i, :, 1 - c], sides.at[i, :, :, pl.ds(c * quarter, quarter)], partner_seq(1))]),
             (product_c, lambda i: [(sides.at[i, 1 - x], made_x.at[i], partner_seq(2))]),
             (product_x, lambda i: []),
-        ], 3 * parts, 3 + masks)
+        ], 4, 3 * parts, 3 + masks)
         run = Copies(send, recv)
         run.count = 3 * parts + 3 * (3 + masks)
         pieces = []
@@ -714,11 +716,6 @@
         def norms_start():
             totals[2:4] = more_ref[0:2]
             norms[...] = totals[...].T.astype(low).reshape(norms.shape)
-
-        def norms_add(total, kept, got):
-            def go():
-                total[...] = (wide(kept()) + wide(got[...])).astype(low)
-            return go
 
         def norms_end():
             total = wide(norms_sy[dp])
@@ -728,11 +725,20 @@
             for i in range(parts - 2, parts):
                 chunk_out(i).wait()
 
+        _, seq = place()
+
+        def norms_to(m):
+            return norms.at[(slice(None),) + tuple(lax.bitwise_xor(own_bit(b), int(m & b > 0)) for b in plan.bits)]
+
+        def norms_seq():
+            total = wide(norms[:, y, x, c])
+            for m in range(1, 8):
+                total = total + wide(norms_c[m - 1])
+            norms_sy[...] = total.astype(low)
+
         pieces.append((self.last_norm, [
-            (norms_start, [run.remote(norms.at[:, :, :, 1 - c], norms_c, partner_seq(1))]),
-            (norms_add(norms_sc, lambda: norms[:, :, :, c], norms_c), [run.remote(norms_sc.at[:, :, 1 - x], norms_x, partner_seq(2))]),
-            (norms_add(norms_sx, lambda: norms_sc[:, :, x], norms_x), [run.remote(norms_sx.at[:, 1 - y], norms_y, partner_seq(4))]),
-            (norms_add(norms_sy, lambda: norms_sx[:, y], norms_y), [
+            (norms_start, [run.remote(norms_to(m), norms_c.at[m - 1], partner_seq(m)) for m in range(1, 8)]),
+            (norms_seq, [
                 run.remote(norms_sy.at[lax.bitwise_xor(dp, m)], norms_z.at[n], partner_dp(plan, m))
                 for n, m in enumerate(plan.masks)]),
             (norms_end, []),
@@ -751,15 +757,14 @@
         each = 2 * (len(plan.masks) + plan.hops)
         self.scratch = [
             pltpu.VMEM(shard.shape, shard.dtype),
-            pltpu.SemaphoreType.DMA((2 * lag, each)),
-            pltpu.SemaphoreType.DMA((2 * lag, each)),
+            pltpu.SemaphoreType.DMA((self.pieces, each)),
+            pltpu.SemaphoreType.DMA((self.pieces, each)),
             pltpu.SemaphoreType.DMA((2,)),
         ]
 
     def copies(self, kind, stage, u, full, held, send, recv):
         plan = self.plan
         dp, _ = place()
-        slot = lax.rem(u, 2 * self.lag)
         rows = pl.ds(pl.multiple_of(lax.div(u, self.across) * self.rows, 16), self.rows)
         out = []
         for h in range(2):
@@ -775,7 +780,7 @@
             others = [partner_dp(plan, m) for m in plan.masks] if entry == "dp" else [partner_seq(entry)]
             for n, other in enumerate(others):
                 out.append(pltpu.make_async_remote_copy(
-                    src, part, send.at[slot, at + n], recv.at[slot, at + n], device_id=other, device_id_type=MESH))
+                    src, part, send.at[u, at + n], recv.at[u, at + n], device_id=other, device_id_type=MESH))
         return out
 
     def run(self, tick, shard, full, held, send, recv, local):
@@ -921,8 +926,8 @@
     length, block = owners * columns, 2 * columns
     steps, parts = length // block, 2
     gathers = (
-        (0, Gather(plan, lag, out_shard, out_shard.shape[0], 512, "late")),
-        (3, Gather(plan, lag, up_shard, up_shard.shape[0], 512, "late")),
+        (0, Gather(plan, 3, out_shard, out_shard.shape[0], 512, "late")),
+        (6, Gather(plan, 3, up_shard, up_shard.shape[0], 512, "late")),
     )
     low = jnp.bfloat16
     begin = ARRIVED + 1
@@ -1019,7 +1024,7 @@
             return (0, jnp.clip(t - up, 0, blocks - 1) * (1 - later) + jnp.clip(t - back, 0, blocks - 1) * later)
 
         once = pl.BlockSpec((tokens, width), lambda t: (0, 0), pipeline_mode=pl.Buffered(1))
-        row = pl.BlockSpec((1, width), lambda t: (0, 0))
+        row = pl.BlockSpec((width,), lambda t: (0,))
         hbm = pl.BlockSpec(memory_space=pl.ANY)
         self.in_specs = [hbm, hbm, hbm, row, row, pl.BlockSpec((width, self.block), up_block), once, hbm, hbm]
         self.out_specs = [
@@ -1144,7 +1149,7 @@
                 values = out_ref[rows, :]
                 centre = values - jnp.mean(values, axis=-1, keepdims=True)
                 spread = lax.rsqrt(jnp.mean(centre * centre, axis=-1, keepdims=True) + EPSILON)
-                acts_ref[rows, :] = (centre * spread * gain_ref[...] + offset_ref[...]).astype(low)
+                acts_ref[rows, :] = (centre * spread * gain_ref[...][None] + offset_ref[...][None]).astype(low)
                 return carry
 
             lax.fori_loop(0, tokens // self.chunk, norm, 0)
@@ -1242,7 +1247,7 @@
                 spread = lax.rsqrt(jnp.mean(centre * centre, axis=-1, keepdims=True) + EPSILON)
                 normed = centre * spread
                 grad = back_ref[rows, :]
-                grown = grad * gain_ref[...]
+                grown = grad * gain_ref[...][None]
                 mean_one = jnp.mean(grown, axis=-1, keepdims=True)
                 mean_two = jnp.mean(grown * normed, axis=-1, keepdims=True)
                 made = chunks[slot, 1] + (grown - mean_one - normed * mean_two) * spread
@@ -1577,7 +1582,7 @@
     )
     grad_low = lower(flat(cotangent))
     mlp = Mlp(
-        plan, lag, mixed, full_out.reshape(width, width), flat(inputs), norm2_gain[None], norm2_bias[None],
+        plan, lag, mixed, full_out.reshape(width, width), flat(inputs), norm2_gain, norm2_bias,
         full_up.reshape(width, -1), grad_low, flat(cotangent), w_down,
     )
     rows = width // every
@@ -1599,10 +1604,10 @@
     ) = reduce_all([(w_down.shape[0] // rows, grad_low)], "even", 3, mlp, 14)
     work = Finish(
         plan, 0, packed, grad_pairs, mixed_t, lse, seg_col, seg_row, cosine, sine, turned_one,
-        heads_weight.reshape(3, width, -1), inputs, grad_first.reshape(inputs.shape), norm1_gain[None], sums_two,
+        heads_weight.reshape(3, width, -1), inputs, grad_first.reshape(inputs.shape), norm1_gain, sums_two,
     )
     up_grad, out_grad, grad_input, heads_grad, norm_rows = reduce_all(
-        [(acts_turned[None], grad_upper), (mixed_turned[None], grad_first_low)], "even", 4, work
+        [(acts_turned[None], grad_upper), (mixed_turned[None], grad_first_low)], "x late", 4, work
     )
     return (
         output.reshape(inputs.shape),

time: 599 us -> 580 us (0.968)
  Pallas kernels: 576 us -> 557 us
    pallas_call x2, Pallas kernels: 396 us -> 385 us  [reduce_products(): pl.pallas_call(functools.partial(reduce_kernel, plan, jobs, first, count,...]
    pallas_call x1, Pallas kernels: 180 us -> 171 us  [attention(): pl.pallas_call(functools.partial(attention_kernel, plan, lag, gathers, bl...]
where the time goes in v5:
time: 580 us; the launch traced here: 579 us
  Pallas kernels  557 us (96%)
  local copies, waits for them, and re-layouts  16.2 us (3%)
    pallas_call x2, Pallas kernels, reduce_products(): pl.pallas_call(functools.partial(reduce_kernel, plan, jobs, first, count,...  385 us
    pallas_call x1, Pallas kernels, attention(): pl.pallas_call(functools.partial(attention_kernel, plan, lag, gathers, bl...  171 us

profile of v5, /device:TPU:0, one launch (start us, length us, event | category | flops | bytes accessed | tf_op | source)
XLA Modules:
  0.0 579.4 jit_solution(2927704396465784487)
XLA Ops:
  0.6 0.0 copy-start
  0.7 1.4 broadcast_in_dim.6.s_ref
  2.1 2.1 reduce_sum.18
  4.2 0.0 copy-done
  4.2 0.4 multiply_reduce_fusion
  4.7 1.7 add_convert_fusion.h_ref
  6.4 0.7 copy-done.1
  7.1 1.3 bitcast_convert_fusion.refs_0_.refs_7_
  8.4 171.4 %shard_map.238 = (bf16[8,3,3,256,128]{4,3,2,1,0:T(8,128)(2,1)}, bf16[1536,2048]{1,0:T(8,128)(2,1)}, bf16[8,3,256,128]{3,2,1,0:T(8,128)(2,1)}, f32[3,4,128,512]{3...) custom-call(bf16[2,256,1536]{2,1,0:T(8,128)(2,1)} %add_convert_fusio, ...), custom_call_target="tpu_custom_call" | custom-call | tf_op jit(solution)/shard_map/pallas_call | solution.py:955
  179.9 199.6 %shard_map.239 = (f32[12,48,512]{2,1,0:T(8,128)}, f32[512,1536]{1,0:T(8,128)}, f32[512,1536]{1,0:T(8,128)}, f32[512,1536]{1,0:T(8,128)}, bf16[512,1536]{1,0:T(8,...) custom-call(bf16[512,1536]{1,0:T(8,128)(2,1)} %bitcast_convert_fusio, ...), custom_call_target="tpu_custom_call" | custom-call | tf_op jit(solution)/shard_map/pallas_call | solution.py:319
  379.5 185.7 %shard_map.240 = (f32[15,48,512]{2,1,0:T(8,128)}, f32[2,256,1536]{2,1,0:T(8,128)}, f32[3,48,1536]{2,1,0:T(8,128)}, f32[48,128]{1,0:T(8,128)}) custom-call(bf16[1,1536,512]{2,1,0:T(8,128)(2,1)} %bitcast.48, bf16[1,1536,512]{2,1,0:T(8,128)(2,1)} %bitcast.47, bf16[512,6144]{1,0:T(8,128)(2,1)} %get-tuple-element.41.refs_2_, ...), custom_call_target="tpu_custom_call" | custom-call | tf_op jit(solution)/shard_map/pallas_call | solution.py:319
  565.2 1.6 slice_reduce_fusion
  566.9 1.0 slice_bitcast_fusion.1
  567.9 1.4 fusion
  569.3 1.1 copy.32
  570.4 0.2 copy.28
  570.6 0.8 copy.31
  571.4 0.9 slice_bitcast_fusion.2
  572.4 0.8 copy.30
  573.2 1.5 copy.33
  574.7 0.0 copy-done.2
  574.7 1.7 copy.37
  576.3 1.4 copy-done.3
  577.7 1.7 copy.38
  (13 shorter events, 0.0 us)
Async XLA Ops:
  0.6 3.6 copy-start
  2.1 2.6 copy-start.6
  2.1 2.6 copy-start.7
  4.7 2.5 copy-start.1
  567.8 3.6 copy-start.5
  569.3 3.1 copy-start.4
  572.4 2.3 copy-start.2
  574.7 3.0 copy-start.3

commit v6 on v5

--- a/solution.py
+++ b/solution.py
@@ -102,6 +102,7 @@
         straight = [("dp",) + order for order in self.orders]
         self.routes = {
             "even": [straight, straight],
+            "some late": [straight] * 3 + [[order[:1] + ("dp",) + order[1:] for order in self.orders]],
             "late": [straight, [order[:1] + ("dp",) + order[1:] for order in self.orders]],
             "x late": [
                 [("dp",) + self.orders[1]] * 2,
@@ -370,18 +371,22 @@
         return last
 
 
-def arrive(plan, lag, tick, h_ref, s_ref, weights, hs_ref, ss_ref, w_ref, hv, wv, halves, send, recv, local):
+def arrive(plan, lag, tick, h_ref, s_ref, weights, hs_ref, ss_ref, w_ref, hv, both_ref, rows_ref, wv, halves, send, recv, local):
     dp, seq = place()
     y, x, c = own_bit(4), own_bit(2), own_bit(1)
     loads = [pltpu.make_async_copy(h_ref.at[y], hv, local.at[0])]
     loads += [pltpu.make_async_copy(r, wv.at[i], local.at[1 + i]) for i, r in enumerate(weights)]
     own = pltpu.make_async_copy(hv, hs_ref.at[y, x, c], local.at[0])
-    named = pltpu.make_async_copy(s_ref.at[y], ss_ref.at[y, x, c], local.at[4])
+    named = pltpu.make_async_copy(rows_ref.at[y], ss_ref.at[y, x, c], local.at[4])
+    given = pltpu.make_async_copy(s_ref, both_ref, local.at[5])
 
     @pl.when(tick == 0)
     def _():
-        for load in loads:
+        for load in loads + [given]:
             load.start()
+        given.wait()
+        for i in range(2):
+            rows_ref[i] = both_ref[i : i + 1, :]
         named.start()
         for load in loads:
             load.wait()
@@ -390,7 +395,7 @@
     run = Copies(send, recv)
     pieces = []
     pieces.append((0, [
-        (None, [run.remote(s_ref.at[1 - y], ss_ref.at[y, x, c], partner_seq(4))]),
+        (None, [run.remote(rows_ref.at[1 - y], ss_ref.at[y, x, c], partner_seq(4))]),
         (named.wait, [run.remote(ss_ref.at[:, x, c], ss_ref.at[:, x, c], partner_seq(2))]),
         (None, [run.remote(ss_ref.at[:, :, c], ss_ref.at[:, :, c], partner_seq(1))]),
     ]))
@@ -803,10 +808,16 @@
         stages = plan.hops + 1
         for stage in reversed(range(stages + 1)):
             u = tick - lag * stage
-            kinds = 1 if self.routes[0] == self.routes[1] else 2
-            for kind in range(kinds):
-
-                @pl.when((u >= 0) & (u < self.pieces) & (lax.rem(u, 2) == kind if kinds > 1 else True))
+            count = len(self.routes)
+            for kind in range(count):
+                if self.routes[kind] in self.routes[:kind]:
+                    continue
+                mine = False
+                for other in range(count):
+                    if self.routes[other] == self.routes[kind]:
+                        mine = mine | (lax.rem(u, count) == other)
+
+                @pl.when((u >= 0) & (u < self.pieces) & mine)
                 def _(stage=stage, u=u, kind=kind):
                     if stage > 0:
                         for copy in self.copies(kind, stage - 1, u, full, held, send, recv):
@@ -854,7 +865,7 @@
 def attention_kernel(
     plan, lag, gathers, block, steps, h_ref, s_ref, q_ref, k_ref, v_ref, cos_ref, sin_ref, out_shard, up_shard,
     packed, turned_ref, o_ref, ot_ref, lse_ref, col_ref, row_ref, hs_ref, ss_ref, w_ref, full_out, full_up,
-    vt_ref, x_ref, weights_ref, ids_ref, hv, wv, halves, send, recv, local, fetch, *more,
+    vt_ref, x_ref, weights_ref, ids_ref, hv, both_ref, rows_ref, wv, halves, send, recv, local, fetch, *more,
 ):
     tick = pl.program_id(0)
 
@@ -862,7 +873,7 @@
     def _():
         greet(plan)
 
-    arrive(plan, lag, tick, h_ref, s_ref, (q_ref, k_ref, v_ref), hs_ref, ss_ref, w_ref, hv, wv, halves, send, recv, local)
+    arrive(plan, lag, tick, h_ref, s_ref, (q_ref, k_ref, v_ref), hs_ref, ss_ref, w_ref, hv, both_ref, rows_ref, wv, halves, send, recv, local)
     for (first, gather), shard, full, held in zip(
         gathers, (out_shard, up_shard), (full_out, full_up), (more[:4], more[4:])
     ):
@@ -990,16 +1001,18 @@
             pltpu.VMEM(weights_shape, low),
             pltpu.VMEM(ids_shape, jnp.int32),
             pltpu.VMEM((columns, width), low),
+            pltpu.VMEM((2, columns), jnp.int32),
+            pltpu.VMEM((2, 1, columns), jnp.int32),
             pltpu.VMEM((3, rows, width), low),
             pltpu.VMEM((3, 2, rows, width // 2), low),
             pltpu.SemaphoreType.DMA((copies,)),
             pltpu.SemaphoreType.DMA((copies,)),
-            pltpu.SemaphoreType.DMA((5,)),
+            pltpu.SemaphoreType.DMA((6,)),
             pltpu.SemaphoreType.DMA((4,)),
         ] + gathers[0][1].scratch + gathers[1][1].scratch,
         compiler_params=pltpu.CompilerParams(
             collective_id=collective_id, has_side_effects=True, vmem_limit_bytes=56 << 20),
-    )(acts, segments[:, None, :], *weights, cosine, sine, out_shard, up_shard)
+    )(acts, segments, *weights, cosine, sine, out_shard, up_shard)
 
 
 class Mlp:
@@ -1010,8 +1023,8 @@
         self.blocks = 2 * plan.n_dp
         self.block = hidden // self.blocks
         self.rows = width // (plan.n_dp * plan.n_seq)
-        self.gather = Gather(plan, lag, shard, self.rows, 512, "even")
-        self.meet = 4
+        self.gather = Gather(plan, lag, shard, self.rows, 512, "some late")
+        self.meet = 5
         self.up = self.meet + 1
         self.back = max(self.gather.ticks, self.up + self.blocks)
         self.norm = self.back + self.blocks
@@ -1286,6 +1299,74 @@
         def _():
             for copy in again + [home, done, first_out, low_out]:
                 copy.wait()
+
+
+def settle_kernel(piece, *refs):
+    (out_any, dx_any, heads_any, down_any, rest_any, norms_ref), refs = refs[:6], refs[6:]
+    (output, dx, d_query, d_key, d_value, d_out, d_up, d_down), refs = refs[:8], refs[8:]
+    sums, (out_ref, dx_ref, heads_ref, down_ref, rest_ref, load_sem, store_sem) = refs[:4], refs[4:]
+    rows = heads_ref.shape[1]
+    parts = out_ref.shape[0]
+    across = heads_ref.shape[2] // piece
+    loads, stores = [], []
+
+    def move(src, held, targets):
+        load = pltpu.make_async_copy(src, held, load_sem.at[len(loads)])
+        load.start()
+        loads.append((load, [
+            pltpu.make_async_copy(part, target, store_sem.at[len(stores) + n]) for n, (part, target) in enumerate(targets)
+        ]))
+        stores.extend(loads[-1][1])
+
+    for i in range(parts):
+        move(out_any.at[i], out_ref.at[i], [(out_ref.at[i], output.at[i])])
+        move(dx_any.at[i], dx_ref.at[i], [(dx_ref.at[i], dx.at[i])])
+    wide_count = rest_any.shape[0] - across
+    move(rest_any, rest_ref, [
+        (rest_ref.at[n], d_up.at[:, pl.ds(n * piece, piece)] if n < wide_count
+         else d_out.at[:, pl.ds((n - wide_count) * piece, piece)])
+        for n in range(rest_any.shape[0])
+    ])
+    move(down_any, down_ref, [
+        (down_ref.at[n], d_down.at[pl.ds(n // across * rows, rows), pl.ds(n % across * piece, piece)])
+        for n in range(down_any.shape[0])
+    ])
+    for i, target in enumerate((d_query, d_key, d_value)):
+        move(heads_any.at[i], heads_ref.at[i], [(heads_ref.at[i], target)])
+    turned = norms_ref[...].T
+    for i, target in enumerate(sums):
+        target[...] = turned[i : i + 1, :].reshape(target.shape)
+    for load, after in loads:
+        load.wait()
+        for store in after:
+            store.start()
+    for store in stores:
+        store.wait()
+
+
+def settle(output, dx, heads, down, rest, norms, piece):
+    rows, width = heads.shape[1:]
+    across = width // piece
+    up_width = (rest.shape[0] - across) * piece
+    blocks = down.shape[0] // across
+    hbm = pl.BlockSpec(memory_space=pl.ANY)
+    vmem = pl.BlockSpec(memory_space=pltpu.VMEM)
+    f32 = jnp.float32
+    arrays = (output, dx, heads, down, rest)
+    return pl.pallas_call(
+        functools.partial(settle_kernel, piece),
+        in_specs=[hbm] * 5 + [vmem],
+        out_specs=[hbm] * 8 + [vmem] * 4,
+        out_shape=[jax.ShapeDtypeStruct(output.shape, f32), jax.ShapeDtypeStruct(dx.shape, f32)]
+        + [jax.ShapeDtypeStruct((rows, width), f32)] * 4
+        + [jax.ShapeDtypeStruct((rows, up_width), f32), jax.ShapeDtypeStruct((blocks * rows, width), f32)]
+        + [jax.ShapeDtypeStruct((rows,), f32)] * 4,
+        scratch_shapes=[pltpu.VMEM(a.shape, f32) for a in arrays] + [
+            pltpu.SemaphoreType.DMA((2 * output.shape[0] + 5,)),
+            pltpu.SemaphoreType.DMA((2 * output.shape[0] + 3 + down.shape[0] + rest.shape[0],)),
+        ],
+        compiler_params=pltpu.CompilerParams(vmem_limit_bytes=63 << 20),
+    )(output, dx, heads, down, rest, norms)
 
 
 def layer_norm(values, gain, offset):
@@ -1587,39 +1668,33 @@
     )
     rows = width // every
 
-    def reduce_all(pairs, routes, collective_id, beside, first=0):
-        out, *more = reduce_products(plan, pairs, rows, piece, lag, routes, collective_id, beside, first)
-        results, at = [], 0
-        for left, right in pairs:
-            blocks = left if isinstance(left, int) else left.shape[0]
-            cols = right.shape[1] // piece
-            part = out[at : at + blocks * cols].reshape(blocks, cols, -1, piece)
-            results.append(jnp.transpose(part, (0, 2, 1, 3)).reshape(-1, right.shape[1]))
-            at += blocks * cols
-        return results + more
-
     (
         down_grad, output, _, grad_first, grad_first_low, mixed_turned, acts_turned, grad_upper, grad_pairs,
         sums_two, _,
-    ) = reduce_all([(w_down.shape[0] // rows, grad_low)], "even", 3, mlp, 14)
+    ) = reduce_products(
+        plan, [(w_down.shape[0] // rows, grad_low)], rows, piece, lag, "late", 3, mlp, 14
+    )
     work = Finish(
         plan, 0, packed, grad_pairs, mixed_t, lse, seg_col, seg_row, cosine, sine, turned_one,
         heads_weight.reshape(3, width, -1), inputs, grad_first.reshape(inputs.shape), norm1_gain, sums_two,
     )
-    up_grad, out_grad, grad_input, heads_grad, norm_rows = reduce_all(
-        [(acts_turned[None], grad_upper), (mixed_turned[None], grad_first_low)], "x late", 4, work
-    )
+    rest_grads, grad_input, heads_grad, norm_rows = reduce_products(
+        plan, [(acts_turned[None], grad_upper), (mixed_turned[None], grad_first_low)], rows, piece, lag, "x late", 4, work
+    )
+    (
+        output, grad_input, query_grad, key_grad, value_grad, out_grad, up_grad, down_grad, *norm_sums
+    ) = settle(output.reshape(inputs.shape), grad_input, heads_grad, down_grad, rest_grads, norm_rows, piece)
     return (
-        output.reshape(inputs.shape),
+        output,
         grad_input,
-        norm_rows[:, 0],
-        norm_rows[:, 1],
-        heads_grad[0],
-        heads_grad[1],
-        heads_grad[2],
+        norm_sums[0],
+        norm_sums[1],
+        query_grad,
+        key_grad,
+        value_grad,
         out_grad,
-        norm_rows[:, 2],
-        norm_rows[:, 3],
+        norm_sums[2],
+        norm_sums[3],
         up_grad,
         down_grad,
     )

time: 580 us -> 566 us (0.976)
  local copies, waits for them, and re-layouts: 16.2 us -> 1.24 us
    unnamed x22 -> x8, local copies, waits for them, and re-layouts: 10.2 us -> 1.24 us
    pallas_call x0 -> x1, Pallas kernels: none -> 8.76 us  [settle(): pl.pallas_call(functools.partial(settle_kernel, piece), in_specs=[hbm] *...]
    pallas_call x2, Pallas kernels: 385 us -> 377 us  [reduce_products(): pl.pallas_call(functools.partial(reduce_kernel, plan, jobs, first, count,...]
where the time goes in v6:
time: 566 us; the launch traced here: 565 us
  Pallas kernels  558 us (99%)
  other arithmetic  5.75 us (1%)
    pallas_call x2, Pallas kernels, reduce_products(): pl.pallas_call(functools.partial(reduce_kernel, plan, jobs, first, count,...  377 us
    pallas_call x1, Pallas kernels, attention(): pl.pallas_call(functools.partial(attention_kernel, plan, lag, gathers, bl...  172 us

profile of v6, /device:TPU:0, one launch (start us, length us, event | category | flops | bytes accessed | tf_op | source)
XLA Modules:
  0.0 565.4 jit_solution(11467922104149973043)
XLA Ops:
  0.6 0.0 copy-start
  0.7 0.0 copy-start.2
  0.7 0.0 copy-start.3
  0.7 2.3 reduce_sum.18
  2.9 0.5 copy-done
  3.5 0.4 multiply_reduce_fusion
  3.9 0.0 copy-start.1
  4.0 0.0 copy-done.2
  4.0 0.0 copy-done.3
  4.0 1.7 add_convert_fusion.h_ref
  5.7 0.7 copy-done.1
  6.4 1.3 bitcast_convert_fusion.refs_0_.refs_7_
  7.7 171.7 %shard_map.238 = (bf16[8,3,3,256,128]{4,3,2,1,0:T(8,128)(2,1)}, bf16[1536,2048]{1,0:T(8,128)(2,1)}, bf16[8,3,256,128]{3,2,1,0:T(8,128)(2,1)}, f32[3,4,128,512]{3...) custom-call(bf16[2,256,1536]{2,1,0:T(8,128)(2,1)} %add_convert_fusio, ...), custom_call_target="tpu_custom_call" | custom-call | tf_op jit(solution)/shard_map/pallas_call | solution.py:966
  179.4 193.9 %shard_map.239 = (f32[12,48,512]{2,1,0:T(8,128)}, f32[512,1536]{1,0:T(8,128)}, f32[512,1536]{1,0:T(8,128)}, f32[512,1536]{1,0:T(8,128)}, bf16[512,1536]{1,0:T(8,...) custom-call(bf16[512,1536]{1,0:T(8,128)(2,1)} %bitcast_convert_fusio, ...), custom_call_target="tpu_custom_call" | custom-call | tf_op jit(solution)/shard_map/pallas_call | solution.py:320
  373.4 183.1 %shard_map.240 = (f32[15,48,512]{2,1,0:T(8,128)}, f32[2,256,1536]{2,1,0:T(8,128)}, f32[3,48,1536]{2,1,0:T(8,128)}, f32[48,128]{1,0:T(8,128)}) custom-call(bf16[1,1536,512]{2,1,0:T(8,128)(2,1)} %bitcast.18, bf16[1,1536,512]{2,1,0:T(8,128)(2,1)} %bitcast.17, bf16[512,6144]{1,0:T(8,128)(2,1)} %get-tuple-element.53.refs_2_, ...), custom_call_target="tpu_custom_call" | custom-call | tf_op jit(solution)/shard_map/pallas_call | solution.py:320
  556.5 8.8 %shard_map.241 = (f32[2,256,1536]{2,1,0:T(8,128)}, f32[2,256,1536]{2,1,0:T(8,128)}, f32[48,1536]{1,0:T(8,128)}, f32[48,1536]{1,0:T(8,128)}, f32[48,1536]{1,0:T(8...) custom-call(f32[2,256,1536]{2,1,0:T(8,128)} %bitcast.16, ...), custom_call_target="tpu_custom_call" | custom-call | tf_op jit(solution)/shard_map/pallas_call | solution.py:1356
  (2 shorter events, 0.0 us)
Async XLA Ops:
  0.6 2.8 copy-start
  0.7 3.3 copy-start.2
  0.7 3.3 copy-start.3
  3.9 2.5 copy-start.1

commit v7 on v6

--- a/solution.py
+++ b/solution.py
@@ -427,7 +427,7 @@
 
 
 ARRIVE_LAG = 2
-ACTS_AT, WEIGHTS_AT = 2, (0, 2, 3)
+ACTS_AT, WEIGHTS_AT = 2, (0, 2, 4)
 ARRIVED = max(ACTS_AT + 3 + 3 * ARRIVE_LAG, WEIGHTS_AT[-1] + 4 * ARRIVE_LAG)
 
 
@@ -772,9 +772,11 @@
         dp, _ = place()
         rows = pl.ds(pl.multiple_of(lax.div(u, self.across) * self.rows, 16), self.rows)
         out = []
-        for h in range(2):
+        routes = self.routes[kind]
+        one = routes[0][stage] == routes[1][stage] and set(routes[0][:stage]) == set(routes[1][:stage])
+        for h in range(1 if one else 2):
             start = lax.rem(u, self.across) * self.cols + h * (self.cols // 2)
-            cols = pl.ds(pl.multiple_of(start, 128), self.cols // 2)
+            cols = pl.ds(pl.multiple_of(start, 128), self.cols if one else self.cols // 2)
             route = self.routes[kind][h]
             entry, done = route[stage], route[:stage]
             where = (slice(None) if "dp" in done else dp,)
@@ -885,14 +887,18 @@
     def acts_load(i):
         return pltpu.make_async_copy(hs_ref.at[lax.div(i, 2), lax.rem(i, 2)], x_ref.at[lax.rem(i, 2)], fetch.at[lax.rem(i, 2)])
 
-    weights_load = pltpu.make_async_copy(w_ref, weights_ref, fetch.at[2])
-    ids_load = pltpu.make_async_copy(ss_ref, ids_ref, fetch.at[3])
-
-    @pl.when(tick == ARRIVED)
+    def weights_load(kind):
+        return pltpu.make_async_copy(w_ref.at[kind], weights_ref.at[kind], fetch.at[2 + kind])
+
+    ids_load = pltpu.make_async_copy(ss_ref, ids_ref, fetch.at[5])
+    named = 3 * ARRIVE_LAG
+
+    @pl.when(tick == named)
     def _():
         ids_load.start()
-        weights_load.start()
-        acts_load(0).start()
+
+    @pl.when(tick == named + 1)
+    def _():
         ids_load.wait()
         ids = ids_ref[...].reshape(2 * steps, columns)
         for i in range(2 * steps):
@@ -901,7 +907,18 @@
         for i in range(2 * steps):
             mine = turned[:, i : i + 1]
             col_ref[i * columns : (i + 1) * columns, :] = jnp.where(mine < 0, -2, mine)
-        weights_load.wait()
+
+    for kind in range(3):
+
+        @pl.when(tick == WEIGHTS_AT[kind] + 4 * ARRIVE_LAG)
+        def _(kind=kind):
+            weights_load(kind).start()
+
+    @pl.when(tick == ARRIVED)
+    def _():
+        acts_load(0).start()
+        for kind in range(3):
+            weights_load(kind).wait()
 
     at = tick - first
 
@@ -938,7 +955,7 @@
     steps, parts = length // block, 2
     gathers = (
         (0, Gather(plan, 3, out_shard, out_shard.shape[0], 512, "late")),
-        (6, Gather(plan, 3, up_shard, up_shard.shape[0], 512, "late")),
+        (7, Gather(plan, 3, up_shard, up_shard.shape[0], 512, "late")),
     )
     low = jnp.bfloat16
     begin = ARRIVED + 1
@@ -1008,7 +1025,7 @@
             pltpu.SemaphoreType.DMA((copies,)),
             pltpu.SemaphoreType.DMA((copies,)),
             pltpu.SemaphoreType.DMA((6,)),
-            pltpu.SemaphoreType.DMA((4,)),
+            pltpu.SemaphoreType.DMA((6,)),
         ] + gathers[0][1].scratch + gathers[1][1].scratch,
         compiler_params=pltpu.CompilerParams(
             collective_id=collective_id, has_side_effects=True, vmem_limit_bytes=56 << 20),

time: 566 us -> 562 us (level)
  no operation moved by 1% of the time
where the time goes in v7:
time: 562 us; the launch traced here: 561 us
  Pallas kernels  553 us (98%)
  other arithmetic  5.75 us (1%)
    pallas_call x2, Pallas kernels, reduce_products(): pl.pallas_call(functools.partial(reduce_kernel, plan, jobs, first, count,...  377 us
    pallas_call x1, Pallas kernels, attention(): pl.pallas_call(functools.partial(attention_kernel, plan, lag, gathers, bl...  167 us

profile of v7, /device:TPU:0, one launch (start us, length us, event | category | flops | bytes accessed | tf_op | source)
XLA Modules:
  0.0 561.3 jit_solution(216865164570844609)
XLA Ops:
  0.6 0.0 copy-start
  0.7 0.0 copy-start.2
  0.7 0.0 copy-start.3
  0.7 2.3 reduce_sum.18
  2.9 0.5 copy-done
  3.5 0.4 multiply_reduce_fusion
  3.9 0.0 copy-start.1
  4.0 0.0 copy-done.2
  4.0 0.0 copy-done.3
  4.0 1.7 add_convert_fusion.h_ref
  5.7 0.7 copy-done.1
  6.4 1.3 bitcast_convert_fusion.refs_0_.refs_7_
  7.7 167.3 %shard_map.238 = (bf16[8,3,3,256,128]{4,3,2,1,0:T(8,128)(2,1)}, bf16[1536,2048]{1,0:T(8,128)(2,1)}, bf16[8,3,256,128]{3,2,1,0:T(8,128)(2,1)}, f32[3,4,128,512]{3...) custom-call(bf16[2,256,1536]{2,1,0:T(8,128)(2,1)} %add_convert_fusio, ...), custom_call_target="tpu_custom_call" | custom-call | tf_op jit(solution)/shard_map/pallas_call | solution.py:983
  175.0 194.8 %shard_map.239 = (f32[12,48,512]{2,1,0:T(8,128)}, f32[512,1536]{1,0:T(8,128)}, f32[512,1536]{1,0:T(8,128)}, f32[512,1536]{1,0:T(8,128)}, bf16[512,1536]{1,0:T(8,...) custom-call(bf16[512,1536]{1,0:T(8,128)(2,1)} %bitcast_convert_fusio, ...), custom_call_target="tpu_custom_call" | custom-call | tf_op jit(solution)/shard_map/pallas_call | solution.py:320
  369.8 182.6 %shard_map.240 = (f32[15,48,512]{2,1,0:T(8,128)}, f32[2,256,1536]{2,1,0:T(8,128)}, f32[3,48,1536]{2,1,0:T(8,128)}, f32[48,128]{1,0:T(8,128)}) custom-call(bf16[1,1536,512]{2,1,0:T(8,128)(2,1)} %bitcast.18, bf16[1,1536,512]{2,1,0:T(8,128)(2,1)} %bitcast.17, bf16[512,6144]{1,0:T(8,128)(2,1)} %get-tuple-element.53.refs_2_, ...), custom_call_target="tpu_custom_call" | custom-call | tf_op jit(solution)/shard_map/pallas_call | solution.py:320
  552.4 8.8 %shard_map.241 = (f32[2,256,1536]{2,1,0:T(8,128)}, f32[2,256,1536]{2,1,0:T(8,128)}, f32[48,1536]{1,0:T(8,128)}, f32[48,1536]{1,0:T(8,128)}, f32[48,1536]{1,0:T(8...) custom-call(f32[2,256,1536]{2,1,0:T(8,128)} %bitcast.16, ...), custom_call_target="tpu_custom_call" | custom-call | tf_op jit(solution)/shard_map/pallas_call | solution.py:1373
  (2 shorter events, 0.0 us)
Async XLA Ops:
  0.6 2.8 copy-start
  0.7 3.3 copy-start.2
  0.7 3.3 copy-start.3
  3.9 2.5 copy-start.1

commit v8 on v7

--- a/solution.py
+++ b/solution.py
@@ -255,8 +255,9 @@
             u = tick - first
             kept = lax.rem(u, lag)
             which = lax.div(u - start, cols)
+            given = right[...].astype(jnp.bfloat16)
             for z in range(plan.n_dp):
-                part = dot(left_rows(which, z), right[...]).astype(jnp.bfloat16)
+                part = dot(left_rows(which, z), given).astype(jnp.bfloat16)
                 for h in range(2):
                     piece = part[:, h * half : (h + 1) * half]
                     sums[h][0][kept, z] = piece.reshape(plan.lead()[1:] + (rows, half))
@@ -1056,7 +1057,7 @@
         once = pl.BlockSpec((tokens, width), lambda t: (0, 0), pipeline_mode=pl.Buffered(1))
         row = pl.BlockSpec((width,), lambda t: (0,))
         hbm = pl.BlockSpec(memory_space=pl.ANY)
-        self.in_specs = [hbm, hbm, hbm, row, row, pl.BlockSpec((width, self.block), up_block), once, hbm, hbm]
+        self.in_specs = [hbm, hbm, hbm, row, row, pl.BlockSpec((width, self.block), up_block), hbm, hbm, hbm]
         self.out_specs = [
             hbm,
             hbm,
@@ -1098,7 +1099,7 @@
             pltpu.SemaphoreType.DMA((16,)),
             pltpu.SemaphoreType.DMA((2, 2)),
             pltpu.SemaphoreType.DMA((2,)),
-        ] + self.gather.scratch
+        ] + self.gather.scratch + [pltpu.VMEM((tokens, width), low)]
 
     everyone = True
 
@@ -1114,7 +1115,8 @@
         )
 
     def run(self, tick, refs):
-        mixed_hbm, w_out, inputs, gain_ref, offset_ref, up_ref, grad_ref, cotangent, shard = refs[:9]
+        mixed_hbm, w_out, inputs, gain_ref, offset_ref, up_ref, _, cotangent, shard = refs[:9]
+        grad_ref = refs[36]
         output, first_sum, grad_first, grad_low, mixed_turned, acts_turned, gu_ref, back_pairs, sums_ref, full = refs[9:19]
         hidden_ref, turned_ref, slope_ref, down_ref, out_ref, back_ref, acts_ref, pairs, chunks = refs[19:28]
         swaps, local, loads, fetch = refs[28:32]
@@ -1125,7 +1127,7 @@
         low = jnp.bfloat16
         third = 512
         thirds = width // third
-        self.gather.run(tick, shard, full, *refs[32:])
+        self.gather.run(tick, shard, full, *refs[32:36])
 
         def exchange(which, src, dst):
             return [
@@ -1156,6 +1158,30 @@
         def _():
             for copy in there + [here, based] + outs:
                 copy.start()
+
+        @pl.when(tick == 1)
+        def _():
+            size = self.chunk
+            total = tokens // size
+
+            def load(j):
+                slot = lax.rem(j, 2)
+                rows = pl.ds(pl.multiple_of(j * size, size), size)
+                return pltpu.make_async_copy(cotangent.at[rows, :], chunks.at[slot, 0], loads.at[slot, 0])
+
+            load(0).start()
+
+            def rounded(j, carry):
+                @pl.when(j + 1 < total)
+                def _():
+                    load(j + 1).start()
+
+                load(j).wait()
+                rows = pl.ds(pl.multiple_of(j * size, size), size)
+                grad_ref[rows, :] = chunks[lax.rem(j, 2), 0].astype(low)
+                return carry
+
+            lax.fori_loop(0, total, rounded, 0)
 
         @pl.when(tick == self.meet)
         def _():
@@ -1678,10 +1704,10 @@
     packed, turned_one, mixed, mixed_t, lse, seg_col, seg_row, _, _, heads_weight, full_out, full_up = attention(
         plan, act_one, segments, (w_query, w_key, w_value), cosine, sine, w_out, w_up, lag, 1
     )
-    grad_low = lower(flat(cotangent))
+    grad_out = flat(cotangent)
     mlp = Mlp(
         plan, lag, mixed, full_out.reshape(width, width), flat(inputs), norm2_gain, norm2_bias,
-        full_up.reshape(width, -1), grad_low, flat(cotangent), w_down,
+        full_up.reshape(width, -1), grad_out, grad_out, w_down,
     )
     rows = width // every
 
@@ -1689,7 +1715,7 @@
         down_grad, output, _, grad_first, grad_first_low, mixed_turned, acts_turned, grad_upper, grad_pairs,
         sums_two, _,
     ) = reduce_products(
-        plan, [(w_down.shape[0] // rows, grad_low)], rows, piece, lag, "late", 3, mlp, 14
+        plan, [(w_down.shape[0] // rows, grad_out)], rows, piece, lag, "late", 3, mlp, 14
     )
     work = Finish(
         plan, 0, packed, grad_pairs, mixed_t, lse, seg_col, seg_row, cosine, sine, turned_one,

time: 562 us -> 559 us (level)
  no operation moved by 1% of the time
where the time goes in v8:
time: 559 us; the launch traced here: 558 us
  Pallas kernels  552 us (99%)
    pallas_call x2, Pallas kernels, reduce_products(): pl.pallas_call(functools.partial(reduce_kernel, plan, jobs, first, count,...  376 us
    pallas_call x1, Pallas kernels, attention(): pl.pallas_call(functools.partial(attention_kernel, plan, lag, gathers, bl...  167 us

profile of v8, /device:TPU:0, one launch (start us, length us, event | category | flops | bytes accessed | tf_op | source)
XLA Modules:
  0.0 558.4 jit_solution(14676072901621396101)
XLA Ops:
  0.6 0.0 copy-start
  0.7 0.0 copy-start.1
  0.7 0.0 copy-start.2
  0.7 2.3 reduce_sum.18
  2.9 0.5 copy-done
  3.5 0.4 multiply_reduce_fusion
  3.9 0.0 copy-done.1
  3.9 0.0 copy-done.2
  4.0 1.7 add_convert_fusion.h_ref
  5.7 167.3 %shard_map.238 = (bf16[8,3,3,256,128]{4,3,2,1,0:T(8,128)(2,1)}, bf16[1536,2048]{1,0:T(8,128)(2,1)}, bf16[8,3,256,128]{3,2,1,0:T(8,128)(2,1)}, f32[3,4,128,512]{3...) custom-call(bf16[2,256,1536]{2,1,0:T(8,128)(2,1)} %add_convert_fusio, ...), custom_call_target="tpu_custom_call" | custom-call | tf_op jit(solution)/shard_map/pallas_call | solution.py:984
  173.0 194.7 %shard_map.239 = (f32[12,48,512]{2,1,0:T(8,128)}, f32[512,1536]{1,0:T(8,128)}, f32[512,1536]{1,0:T(8,128)}, f32[512,1536]{1,0:T(8,128)}, bf16[512,1536]{1,0:T(8,...) custom-call(f32[512,1536]{1,0:T(8,128)} %bitcast.10, ...), custom_call_target="tpu_custom_call" | custom-call | tf_op jit(solution)/shard_map/pallas_call | solution.py:321
  367.7 181.7 %shard_map.240 = (f32[15,48,512]{2,1,0:T(8,128)}, f32[2,256,1536]{2,1,0:T(8,128)}, f32[3,48,1536]{2,1,0:T(8,128)}, f32[48,128]{1,0:T(8,128)}) custom-call(bf16[1,1536,512]{2,1,0:T(8,128)(2,1)} %bitcast.19, bf16[1,1536,512]{2,1,0:T(8,128)(2,1)} %bitcast.18, bf16[512,6144]{1,0:T(8,128)(2,1)} %get-tuple-element.53.refs_2_, ...), custom_call_target="tpu_custom_call" | custom-call | tf_op jit(solution)/shard_map/pallas_call | solution.py:321
  549.4 8.8 %shard_map.241 = (f32[2,256,1536]{2,1,0:T(8,128)}, f32[2,256,1536]{2,1,0:T(8,128)}, f32[48,1536]{1,0:T(8,128)}, f32[48,1536]{1,0:T(8,128)}, f32[48,1536]{1,0:T(8...) custom-call(f32[2,256,1536]{2,1,0:T(8,128)} %bitcast.17, ...), custom_call_target="tpu_custom_call" | custom-call | tf_op jit(solution)/shard_map/pallas_call | solution.py:1399
  (2 shorter events, 0.0 us)
Async XLA Ops:
  0.6 2.8 copy-start
  0.7 3.3 copy-start.1
  0.7 3.3 copy-start.2
